TPU v7x, 32 devices: a whole 2x2x4 slice. The times are simulated.
32 devices in a mesh: expert: 16 (over z, y, x), tensor: 2 (over core).
Axes of the slice: x: 2, y: 2, z: 4, core: 2. Of those that a mesh axis runs over, the one named last changes fastest.
Arguments:
- tokens_in: float32 [25216, 768], P('expert'), may hold values from -10 to 10
- valid: int32 [128, 197], P('expert'), may hold values from 0 to 1, as said below
- routes: int32 [25216, 2], P('expert'), may hold values from 0 to 15, all different within a row; in each aligned block of 1576 rows (0 to 1575, 1576 to 3151, ...) at most 248 rows name the same one
- ln1_gain: float32 [768], replicated, may hold values from 0.5 to 1.5
- ln1_bias: float32 [768], replicated, may hold values from -0.875 to 0.875
- w_query: bfloat16 [768, 768], P(None, 'tensor'), may hold values from -0.21875 to 0.21875
- w_key: bfloat16 [768, 768], P(None, 'tensor'), may hold values from -0.21875 to 0.21875
- w_value: bfloat16 [768, 768], P(None, 'tensor'), may hold values from -0.21875 to 0.21875
- b_query: float32 [768], P('tensor'), may hold values from -3 to 3
- b_value: float32 [768], P('tensor'), may hold values from -0.625 to 0.625
- w_proj: bfloat16 [768, 768], P('tensor'), may hold values from -1.5 to 1.5
- b_proj: float32 [768], replicated, may hold values from -1.75 to 1.75
- ln2_gain: float32 [768], replicated, may hold values from 0.5 to 1.5
- ln2_bias: float32 [768], replicated, may hold values from -0.875 to 0.875
- w_router: bfloat16 [768, 16], replicated, may hold values from -0.15625 to 0.15625
- w_in: bfloat16 [16, 768, 3072], P('expert', None, 'tensor'), may hold values from -0.21875 to 0.21875
- b_in: float32 [16, 3072], P('expert', 'tensor'), may hold values from -3 to 3
- w_out: bfloat16 [16, 3072, 768], P('expert', 'tensor'), may hold values from -1.75 to 1.75
- b_out: float32 [16, 768], P('expert'), may hold values from -6 to 6
- cotangent: float32 [25216, 768], P('expert'), may hold values from -6 to 6
Outputs:
- output: float32 [25216, 768], P('expert')
- grad_input: float32 [25216, 768], P('expert')
- grad_ln1_gain: float32 [768], replicated
- grad_ln1_bias: float32 [768], replicated
- grad_w_query: float32 [768, 768], P(None, 'tensor')
- grad_w_key: float32 [768, 768], P(None, 'tensor')
- grad_w_value: float32 [768, 768], P(None, 'tensor')
- grad_b_query: float32 [768], P('tensor')
- grad_b_value: float32 [768], P('tensor')
- grad_w_proj: float32 [768, 768], P('tensor')
- grad_b_proj: float32 [768], replicated
- grad_ln2_gain: float32 [768], replicated
- grad_ln2_bias: float32 [768], replicated
- grad_w_router: float32 [768, 16], replicated
- grad_w_in: float32 [16, 768, 3072], P('expert', None, 'tensor')
- grad_b_in: float32 [16, 3072], P('expert', 'tensor')
- grad_w_out: float32 [16, 3072, 768], P('expert', 'tensor')
- grad_b_out: float32 [16, 768], P('expert')
- rms_values: float32 [5], replicated
Inputs may be any that keep to these rules, and one draw needn't show every extreme that they name: `routes`: among the tokens of one index of the expert axis, no expert is named more than 248 times, a bound that some block reaches. In every image the valid tokens are a prefix of 98 or more positions.
All inputs are finite; a program needn't handle non-finite values.
Results may differ from a plain program's by a relative error of at most 0.017.
Values may be sent and summed in bfloat16 or wider, within the bound.
A program may use at most 320 MiB of HBM per device.

v0:
```python
import jax
import jax.numpy as jnp
from jax import lax
from jax.sharding import PartitionSpec as P

HEAD_DIM = 64


masked_fill = -1e30


def norm_rows(values, gain, bias):
    center = values - jnp.mean(values, -1, keepdims=True)
    inv_std = lax.rsqrt(jnp.mean(center * center, -1, keepdims=True) + 1e-06)
    normed = center * inv_std
    return (normed * gain + bias, normed, inv_std)


def norm_back(grad_out, normed, inv_std, gain):
    scaled = grad_out * gain
    return inv_std * (
        scaled
        - jnp.mean(scaled, -1, keepdims=True)
        - normed * jnp.mean(scaled * normed, -1, keepdims=True)
    )


def slot_positions(expert_ids, experts):
    flat_ids = expert_ids.reshape(-1)
    onehot = (flat_ids[:, None] == jnp.arange(experts, dtype=jnp.int32)[None, :]).astype(jnp.int32)
    before = jnp.cumsum(onehot, 0) - onehot
    return (flat_ids, jnp.sum(before * onehot, 1))


def exact_gelu(values):
    return jax.nn.gelu(values, approximate=False)


def on_device(
    tokens_in,
    valid,
    routes,
    ln1_gain,
    ln1_bias,
    w_query,
    w_key,
    w_value,
    b_query,
    b_value,
    w_proj,
    b_proj,
    ln2_gain,
    ln2_bias,
    w_router,
    w_in,
    b_in,
    w_out,
    b_out,
    cotangent,
):
    tok_rows, width = tokens_in.shape
    images_local, seq_len = valid.shape
    experts = lax.axis_size("expert")
    capacity = (10 * tok_rows // (4 * experts) // 8 + 1) * 8
    heads_local = w_query.shape[1] // HEAD_DIM
    scale = HEAD_DIM ** (-0.5)
    shape4 = (images_local, seq_len, heads_local, HEAD_DIM)
    f32 = jnp.float32
    bf16 = jnp.bfloat16

    def send_out(rows):
        arrived = lax.all_to_all(rows, "expert", split_axis=0, concat_axis=0, tiled=True)
        return arrived.reshape(experts * capacity, width)

    def send_back(partial_value, addend):
        total = lax.psum(partial_value, "tensor")
        if addend is not None:
            total = total + addend
        return lax.all_to_all(
            total.astype(bf16).reshape(experts, capacity, width),
            "expert",
            split_axis=0,
            concat_axis=0,
            tiled=True,
        )

    h1_val, normed_one, inv_one = norm_rows(tokens_in, ln1_gain, ln1_bias)
    h1_low = h1_val.astype(bf16)
    query = (jnp.dot(h1_low, w_query, preferred_element_type=f32) + b_query).astype(bf16)
    keys = jnp.dot(h1_low, w_key, preferred_element_type=f32).astype(bf16)
    values = (jnp.dot(h1_low, w_value, preferred_element_type=f32) + b_value).astype(bf16)
    query4 = query.reshape(shape4)
    keys4 = keys.reshape(shape4)
    values4 = values.reshape(shape4)
    key_ok = valid[:, None, None, :] > 0

    def scores_of():
        raw = jnp.einsum("gqhd,gkhd->ghqk", query4, keys4, preferred_element_type=f32)
        return jnp.where(key_ok, raw * scale, masked_fill)

    scores = scores_of()
    top = jnp.max(scores, -1, keepdims=True)
    expo = jnp.exp(scores - top)
    total = jnp.sum(expo, -1, keepdims=True)
    log_total = top + jnp.log(total)
    probs_low = (expo / total).astype(bf16)
    heads_out = (
        jnp.einsum("ghqk,gkhd->gqhd", probs_low, values4, preferred_element_type=f32)
        .reshape(tok_rows, -1)
        .astype(bf16)
    )
    attn_part = jnp.dot(heads_out, w_proj, preferred_element_type=f32)
    attn_out = lax.psum(attn_part, "tensor") + b_proj
    middle = tokens_in + attn_out
    h2_val, normed_two, inv_two = norm_rows(middle, ln2_gain, ln2_bias)
    h2_low = h2_val.astype(bf16)
    logits = jnp.dot(h2_low, w_router, preferred_element_type=f32)
    logit_top = jnp.max(logits, -1, keepdims=True)
    logit_exp = jnp.exp(logits - logit_top)
    route_probs = logit_exp / jnp.sum(logit_exp, -1, keepdims=True)
    gates = jnp.take_along_axis(route_probs, routes, axis=1)
    flat_ids, slot_pos = slot_positions(routes, experts)
    both_rows = jnp.repeat(h2_low, 2, axis=0)
    send_rows = jnp.zeros((experts, capacity, width), bf16).at[flat_ids, slot_pos].set(both_rows)
    expert_rows = send_out(send_rows)
    pre_act = jnp.dot(expert_rows, w_in[0], preferred_element_type=f32) + b_in[0]
    hidden_low = exact_gelu(pre_act).astype(bf16)
    expert_part = jnp.dot(hidden_low, w_out[0], preferred_element_type=f32)
    back_rows = send_back(expert_part, b_out[0])
    token_res = back_rows[flat_ids, slot_pos].reshape(tok_rows, 2, width).astype(f32)
    moe_out = jnp.sum(gates[:, :, None] * token_res, 1)
    output = middle + moe_out
    valid_rows = valid.reshape(tok_rows).astype(f32)[:, None]
    stat_sums = jnp.stack(
        [
            jnp.sum(valid_rows * field * field)
            for field in (tokens_in, middle, output, attn_out, moe_out)
        ]
    )
    stat_count = jnp.sum(valid_rows) * width
    grad_res = (gates[:, :, None] * cotangent[:, None, :]).astype(bf16)
    grad_gate = jnp.sum(cotangent[:, None, :] * token_res, -1)
    expert_onehot = (
        routes[:, :, None] == jnp.arange(experts, dtype=jnp.int32)[None, None, :]
    ).astype(f32)
    grad_probs = jnp.sum(grad_gate[:, :, None] * expert_onehot, 1)
    grad_logits = (
        route_probs * (grad_probs - jnp.sum(grad_probs * route_probs, -1, keepdims=True))
    ).astype(bf16)
    grad_router = jnp.einsum("td,te->de", h2_low, grad_logits, preferred_element_type=f32)
    grad_h2 = jnp.einsum("te,de->td", grad_logits, w_router, preferred_element_type=f32)
    send_grads = (
        jnp.zeros((experts, capacity, width), bf16)
        .at[flat_ids, slot_pos]
        .set(grad_res.reshape(tok_rows * 2, width))
    )
    grad_rows = send_out(send_grads)
    grad_b_out = jnp.sum(grad_rows.astype(f32), 0)[None]
    grad_w_out = jnp.einsum("rf,rd->fd", hidden_low, grad_rows, preferred_element_type=f32)[None]
    grad_hidden = jnp.einsum("rd,fd->rf", grad_rows, w_out[0], preferred_element_type=f32)
    unused, gelu_back = jax.vjp(exact_gelu, pre_act)
    grad_pre = gelu_back(grad_hidden)[0].astype(bf16)
    grad_b_in = jnp.sum(grad_pre.astype(f32), 0)[None]
    grad_w_in = jnp.einsum("rd,rf->df", expert_rows, grad_pre, preferred_element_type=f32)[None]
    grad_in_part = jnp.einsum("rf,df->rd", grad_pre, w_in[0], preferred_element_type=f32)
    grad_back = send_back(grad_in_part, None)
    grad_h2 = grad_h2 + jnp.sum(
        grad_back[flat_ids, slot_pos].reshape(tok_rows, 2, width).astype(f32), 1
    )
    grad_ln2_gain = jnp.sum(grad_h2 * normed_two, 0)
    grad_ln2_bias = jnp.sum(grad_h2, 0)
    grad_middle = cotangent + norm_back(grad_h2, normed_two, inv_two, ln2_gain)
    grad_attn = grad_middle.astype(bf16)
    grad_b_proj = jnp.sum(grad_attn.astype(f32), 0)
    grad_w_proj = jnp.einsum("tc,td->cd", heads_out, grad_attn, preferred_element_type=f32)
    grad_heads = (
        jnp.einsum("td,cd->tc", grad_attn, w_proj, preferred_element_type=f32)
        .astype(bf16)
        .reshape(shape4)
    )
    probs_again = jnp.exp(scores_of() - log_total)
    probs_again_low = probs_again.astype(bf16)
    grad_values = jnp.einsum(
        "ghqk,gqhd->gkhd", probs_again_low, grad_heads, preferred_element_type=f32
    ).astype(bf16)
    grad_weights = jnp.einsum("gqhd,gkhd->ghqk", grad_heads, values4, preferred_element_type=f32)
    grad_scores = (
        probs_again
        * (grad_weights - jnp.sum(grad_weights * probs_again, -1, keepdims=True))
        * scale
    ).astype(bf16)
    grad_query = (
        jnp.einsum("ghqk,gkhd->gqhd", grad_scores, keys4, preferred_element_type=f32)
        .astype(bf16)
        .reshape(tok_rows, -1)
    )
    grad_keys = (
        jnp.einsum("ghqk,gqhd->gkhd", grad_scores, query4, preferred_element_type=f32)
        .astype(bf16)
        .reshape(tok_rows, -1)
    )
    grad_values = grad_values.reshape(tok_rows, -1)
    grad_b_query = jnp.sum(grad_query.astype(f32), 0)
    grad_b_value = jnp.sum(grad_values.astype(f32), 0)
    grad_w_query = jnp.einsum("tc,tk->ck", h1_low, grad_query, preferred_element_type=f32)
    grad_w_key = jnp.einsum("tc,tk->ck", h1_low, grad_keys, preferred_element_type=f32)
    grad_w_value = jnp.einsum("tc,tk->ck", h1_low, grad_values, preferred_element_type=f32)
    grad_h1_part = jnp.einsum("tk,ck->tc", grad_query, w_query, preferred_element_type=f32)
    grad_h1_part = grad_h1_part + jnp.einsum(
        "tk,ck->tc", grad_keys, w_key, preferred_element_type=f32
    )
    grad_h1_part = grad_h1_part + jnp.einsum(
        "tk,ck->tc", grad_values, w_value, preferred_element_type=f32
    )
    grad_h1 = lax.psum(grad_h1_part, "tensor")
    grad_ln1_gain = jnp.sum(grad_h1 * normed_one, 0)
    grad_ln1_bias = jnp.sum(grad_h1, 0)
    grad_input = grad_middle + norm_back(grad_h1, normed_one, inv_one, ln1_gain)
    summed = lax.psum(
        (
            grad_w_query,
            grad_w_key,
            grad_w_value,
            grad_b_query,
            grad_b_value,
            grad_w_proj,
            grad_b_proj,
            grad_ln1_gain,
            grad_ln1_bias,
            grad_ln2_gain,
            grad_ln2_bias,
            grad_router,
            stat_sums,
            stat_count,
        ),
        "expert",
    )
    rms_values = jnp.sqrt(summed[12] / summed[13])
    return (
        output,
        grad_input,
        summed[7],
        summed[8],
        summed[0],
        summed[1],
        summed[2],
        summed[3],
        summed[4],
        summed[5],
        summed[6],
        summed[9],
        summed[10],
        summed[11],
        grad_w_in,
        grad_b_in,
        grad_w_out,
        grad_b_out,
        rms_values,
    )


def solution(mesh):
    in_specs = (
        P("expert", None),
        P("expert", None),
        P("expert", None),
        P(),
        P(),
        P(None, "tensor"),
        P(None, "tensor"),
        P(None, "tensor"),
        P("tensor"),
        P("tensor"),
        P("tensor", None),
        P(),
        P(),
        P(),
        P(),
        P("expert", None, "tensor"),
        P("expert", "tensor"),
        P("expert", "tensor", None),
        P("expert", None),
        P("expert", None),
    )
    out_specs = (
        P("expert", None),
        P("expert", None),
        P(),
        P(),
        P(None, "tensor"),
        P(None, "tensor"),
        P(None, "tensor"),
        P("tensor"),
        P("tensor"),
        P("tensor", None),
        P(),
        P(),
        P(),
        P(),
        P("expert", None, "tensor"),
        P("expert", "tensor"),
        P("expert", "tensor", None),
        P("expert", None),
        P(),
    )
    return jax.shard_map(
        on_device, mesh=mesh, in_specs=in_specs, out_specs=out_specs, check_vma=False
    )
```

profile of v0, /device:TPU:0, one launch (start us, length us, event | category | flops | bytes accessed | tf_op | source)
XLA Modules:
  0.0 1276.0 jit_solution(16914647547270931748)
XLA Ops:
  20.8 4.8 reshape.302
  25.6 4.6 copy.141
  30.2 4.1 fusion.53
  34.3 4.8 reshape.303
  39.1 4.6 copy.139
  43.7 4.8 reshape.304
  48.5 4.6 copy.140
  53.0 4.4 fusion.9
  61.4 3.4 fusion.80
  66.8 4.0 convert_element_type.133
  70.8 5.0 fusion.107
  77.1 4.6 reduce-window.6
  83.7 24.3 %all-reduce.10.cloned.1.call-done = f32[1576,768]{1,0:T(8,128)} async-done(((f32[1576,768]{1,0:T(8,128)}), f32[1576,768]{1,0:T(8,128)}) %all-reduce.10.cloned.1.call-update) | async-done | bytes 4841488 | tf_op jit(solution)/shard_map/psum | solution.py:113
  108.0 4.5 fusion.103
  116.4 22.3 %broadcast_in_dim.33 = bf16[1576,2,768]{2,1,0:T(2,128)(2,1)} broadcast(bf16[1576,768]{1,0:T(8,128)(2,1)S(1)} %add_convert_fusion.2), dimensions={0,2} | broadcast | bytes 7262208 | tf_op jit(solution)/shard_map/broadcast_in_dim | solution.py:123
  138.7 11.3 reshape.287
  150.0 22.0 %scatter_custom_fusion = bf16[3968,768]{1,0:T(8,128)(2,1)} fusion(s32[3152]{0:T(1024)S(1)} %broadcast_select_fusion, bf16[3152,768]{1,0:T(8,128)(2,1)} %reshape.287, bf16[]{:T(256)} %constant.23.clone.1), kind=kCustom, calls=%fused_computation.92 | custom fusion | bytes 6095360
  172.0 7.0 all-to-all-start
  179.8 13.9 %mul.255 = f32[1576,2,768]{2,1,0:T(2,128)} broadcast(f32[1576,768]{1,0:T(8,128)} %param.39), dimensions={0,2} | broadcast | bytes 14524416 | tf_op jit(solution)/shard_map/mul | solution.py:142
  193.7 12.6 mul.263
  210.7 39.5 %gather_fusion.2 = f32[3152]{0:T(1024)S(1)} fusion(f32[1576,16]{0,1:T(8,128)S(1)} %fusion.83, s32[3152]{0:T(1024)S(1)} %reshape.279), kind=kCustom, calls=%fused_computation.2 | custom fusion | bytes 50432 | tf_op jit(solution)/shard_map/jit(take_along_axis)/gather | solution.py:121
  251.9 33.1 %scatter_custom_fusion.1 = bf16[3968,768]{1,0:T(8,128)(2,1)} fusion(s32[3152]{0:T(1024)} %copy-done.60, f32[3152,768]{1,0:T(8,128)} %mul.263, f32[3152]{0:T(1024)S(1)} %mul.261, bf16[]{:T(256)} %constant.23.clone.1), kind=kCustom, calls=%fused_computation.65 | custom fusion | flops 4841472 | bytes 15790912
  285.0 10.4 all-to-all-done
  295.4 28.6 %all-to-all-start.2 = ((bf16[16,248,768]{2,1,0:T(8,128)(2,1)}), bf16[16,248,768]{2,1,0:T(8,128)(2,1)}, u32[]{:S(2)}, u32[]{:S(2)}) async-start(bf16[16,248,768]{2,1,0:T(8,128)(2,1)} %bitcast.116), calls=%async_computation.2 | async-start | bytes 12189696 | tf_op jit(solution)/shard_map/all_to_all | solution.py:72
  324.1 63.6 %multiply_convert_fusion = (bf16[3968,1536]{1,0:T(8,128)(2,1)S(1)}, f32[3968,1536]{1,0:T(8,128)}, f32[3968,1536]{1,0:T(8,128)}) fusion(f32[1536]{0:T(1024)S(1)} %copy-done.61, bf16[3968,768]{1,0:T(8,128)(2,1)} %bitcast.4, bf16[1,768,1536]{2,1,0:T(8,128)(2,1)S(1)} %copy-done), kind=kOutput, calls=%fused_computation.10 | convolution fusion | flops 9763946496 | bytes 69408768 | tf_op jit(solution)/shard_map/dot_general | solution.py:126
  387.8 4.5 copy-done.71
  392.2 12.1 fusion.55
  404.3 32.7 %all-to-all-done.2 = bf16[16,248,768]{2,1,0:T(8,128)(2,1)} async-done(((bf16[16,248,768]{2,1,0:T(8,128)(2,1)}), bf16[16,248,768]{2,1,0:T(8,128)(2,1)}, u32[]{:S(2)}, u32[]{:S(2)}) %all-to-all-start.2) | async-done | bytes 6094880 | tf_op jit(solution)/shard_map/all_to_all | solution.py:72
  437.0 36.5 %convert_reduce_fusion = (f32[1536]{0:T(1024)S(1)}, bf16[3968,1536]{1,0:T(8,128)(2,1)}) fusion(f32[3968,1536]{1,0:T(8,128)} %get-tuple-element.54, bf16[3968,768]{1,0:T(8,128)(2,1)} %bitcast.9, bf16[1,1536,768]{2,1,0:T(8,128)(2,1)} %param.37, f32[3968,1536]{1,0:T(8,128)} %get-tuple-element.64, f32[1536]{0:T(1024)S(1)} %copy-done.61), kind=kOutput, calls=%fused_computation.8 | convolution fusion | flops 9465296896 | bytes 69414912 | tf_op jit(solution)/shard_map/rd,fd->rf/dot_general | solution.py:160
  473.5 15.2 %fusion.57 = f32[3968,768]{1,0:T(8,128)} fusion(bf16[3968,1536]{1,0:T(8,128)(2,1)} %get-tuple-element.73, bf16[1,768,1536]{2,1,0:T(8,128)(2,1)S(1)} %copy-done), kind=kOutput, calls=%fused_computation.101 | convolution fusion | flops 9361686528 | bytes 26738688 | tf_op jit(solution)/shard_map/rf,df->rd/dot_general | solution.py:165
  488.7 34.8 %all-reduce.17 = bf16[3968,768]{1,0:T(8,128)(2,1)} all-reduce(f32[3968,768]{1,0:T(8,128)} %fusion.57), channel_id=1, replica_groups=mesh['expert'=16,'tensor'=2] {'tensor'}, use_global_device_ids=true, to_apply=%region_19.20 | all-reduce | flops 3047424 | bytes 18284544 | tf_op jit(solution)/shard_map/psum | solution.py:76
  523.6 24.2 %all-to-all-start.3 = ((bf16[16,248,768]{2,1,0:T(8,128)(2,1)}), bf16[16,248,768]{2,1,0:T(8,128)(2,1)}, u32[]{:S(2)}, u32[]{:S(2)}) async-start(bf16[16,248,768]{2,1,0:T(8,128)(2,1)} %bitcast.118), calls=%async_computation.3 | async-start | bytes 12189696 | tf_op jit(solution)/shard_map/all_to_all | solution.py:79
  547.8 8.0 add_convert_fusion.1
  555.8 108.4 %all-to-all-done.3 = bf16[16,248,768]{2,1,0:T(8,128)(2,1)} async-done(((bf16[16,248,768]{2,1,0:T(8,128)(2,1)}), bf16[16,248,768]{2,1,0:T(8,128)(2,1)}, u32[]{:S(2)}, u32[]{:S(2)}) %all-to-all-start.3) | async-done | bytes 6094880 | tf_op jit(solution)/shard_map/all_to_all | solution.py:79
  664.3 28.7 %all-to-all-start.1 = ((bf16[16,248,768]{2,1,0:T(8,128)(2,1)}), bf16[16,248,768]{2,1,0:T(8,128)(2,1)}, u32[]{:S(2)}, u32[]{:S(2)}) async-start(bf16[16,248,768]{2,1,0:T(8,128)(2,1)} %bitcast.117), calls=%async_computation.1 | async-start | bytes 12189696 | tf_op jit(solution)/shard_map/all_to_all | solution.py:79
  693.2 58.2 %gather_fusion.1 = bf16[3152,768]{1,0:T(8,128)(2,1)} fusion(bf16[16,248,768]{2,1,0:T(8,128)(2,1)} %all-to-all-done.3, s32[3152]{0:T(1024)S(1)} %copy-done.1), kind=kCustom, calls=%fused_computation.1 | custom fusion | bytes 9708160 | tf_op jit(solution)/shard_map/gather | solution.py:168
  751.4 11.5 reshape.266
  762.8 44.9 %reduce_sum.306 = f32[1576,768]{1,0:T(8,128)} reduce(f32[1576,2,768]{2,1,0:T(2,128)} %reshape.266, f32[]{:T(128)} %constant.44.clone.1), dimensions={1}, to_apply=%region_20.21 | reduce | flops 1210368 | bytes 14524420 | tf_op jit(solution)/shard_map/reduce_sum | solution.py:167
  807.7 58.3 %gather_fusion = bf16[3152,768]{1,0:T(8,128)(2,1)} fusion(bf16[16,248,768]{2,1,0:T(8,128)(2,1)} %all-to-all-done.1, s32[3152]{0:T(1024)S(1)} %copy-done.1), kind=kCustom, calls=%fused_computation | custom fusion | bytes 9708160 | tf_op jit(solution)/shard_map/gather | solution.py:130
  866.0 11.7 reshape.265
  877.7 25.2 %multiply_reduce_fusion.1 = (f32[1576,2]{1,0:T(8,128)}, f32[1576,768]{1,0:T(8,128)}) fusion(f32[1576,2,768]{2,1,0:T(2,128)} %reshape.265, f32[1576,768]{1,0:T(8,128)} %param.39, f32[1576,2]{1,0:T(8,128)} %copy-done.11), kind=kLoop, calls=%fused_computation.34 | loop fusion | flops 8469424 | bytes 19391104 | tf_op jit(solution)/shard_map/reduce_sum | solution.py:142
  904.6 12.7 multiply_reduce_fusion.3
  917.3 4.2 convert_reduce_fusion.2
  926.3 4.8 reshape.305
  931.1 4.9 copy.152
  936.0 7.3 fusion.108
  943.3 7.5 convert_reduce_fusion.3
  950.8 19.2 %fusion.71 = bf16[8,197,6,64]{1,3,2,0:T(8,128)(2,1)} fusion(bf16[8,197,6,64]{1,3,2,0:T(8,128)(2,1)} %copy.139, f32[8,6,197,197]{2,3,1,0:T(8,128)} %fusion.108, f32[8,6,197,197]{2,3,1,0:T(8,128)} %copy-done.6, f32[8,6,197]{2,1,0:T(8,128)S(1)} %log_add_fusion, pred[8,197]{1,0:T(8,128)(4,1)S(1)} %copy-done.57), kind=kOutput, calls=%fused_computation.109 | convolution fusion | flops 259548480 | bytes 17362792 | tf_op jit(solution)/shard_map/ghqk,gqhd->gkhd/dot_general | solution.py:198
  970.1 19.8 %convert_reduce_fusion.4 = (f32[6,64]{1,0:T(8,128)S(1)}, bf16[8,197,6,64]{1,3,2,0:T(8,128)(2,1)}) fusion(bf16[8,197,6,64]{1,3,2,0:T(8,128)(2,1)} %copy.140, f32[8,6,197,197]{2,3,1,0:T(8,128)} %fusion.108, f32[8,6,197,197]{2,3,1,0:T(8,128)} %copy-done.6, f32[8,6,197]{2,1,0:T(8,128)S(1)} %log_add_fusion, pred[8,197]{1,0:T(8,128)(4,1)S(1)} %copy-done.57), kind=kOutput, calls=%fused_computation.88 | convolution fusion | flops 260758464 | bytes 17364328 | tf_op jit(solution)/shard_map/ghqk,gkhd->gqhd/dot_general | solution.py:193
  989.9 3.5 copy.162
  993.3 4.1 reshape.255
  997.5 3.5 copy.159
  1000.9 4.0 reshape.254
  1005.0 3.5 copy.156
  1008.4 4.0 reshape.253
  1016.9 4.0 add_add_fusion
  1022.2 3.6 convert_reduce_fusion.1
  1027.0 16.5 %convolution_bitcast_fusion.1 = f32[1,768,1536]{2,1,0:T(8,128)} fusion(bf16[3968,768]{1,0:T(8,128)(2,1)} %bitcast.4, bf16[3968,1536]{1,0:T(8,128)(2,1)} %get-tuple-element.73), kind=kOutput, calls=%fused_computation.86 | convolution fusion | flops 9361686528 | bytes 23003136 | tf_op jit(solution)/shard_map/rd,rf->df/dot_general | solution.py:164
  1053.8 16.5 %convolution_bitcast_fusion = f32[1,1536,768]{2,1,0:T(8,128)} fusion(bf16[3968,1536]{1,0:T(8,128)(2,1)} %copy-done.71, bf16[3968,768]{1,0:T(8,128)(2,1)} %bitcast.9), kind=kOutput, calls=%fused_computation.85 | convolution fusion | flops 9361686528 | bytes 23003136 | tf_op jit(solution)/shard_map/rf,rd->fd/dot_general | solution.py:159
  1072.6 7.5 multiply_reduce_fusion.4
  1080.1 3.3 stack.23
  1083.4 98.4 %all-reduce.18 = (f32[768]{0:T(1024)}, f32[768]{0:T(1024)}, f32[384]{0:T(512)}, f32[384]{0:T(512)}, f32[768]{0:T(1024)}, /*index=5*/f32[768]{0:T(1024)}, f32[768...) all-reduce(f32[768]{0:T(1024)S(1)} %get-tuple-element.21, ...), channel_id=1, replica_groups=mesh['expert'=16,'tensor'=2] {'expert'}, use_global_device_ids=true, to_apply=%region_28.29 | all-reduce | flops 16902 | bytes 135216 | tf_op jit(solution)/shard_map/psum | solution.py:219
  1183.0 8.2 multiply_add_fusion
  1191.2 70.9 %all-reduce.16.cloned.1.call-done = (f32[768,384]{1,0:T(8,128)}, f32[768,384]{1,0:T(8,128)}, f32[768,384]{1,0:T(8,128)}, f32[384,768]{1,0:T(8,128)}) async-done(((f32[768,384]{1,0:T(8,128)}, f32[768,384]{1,0:T(8,128)}, f32[768,384]{1,0:T(8,128)}, f32[384,768]{1,0:T(8,128)}), (f32[768,384]{1,0:T(8,128)}, f32[768,384]{1,0:T(8,128)}, f32[768,384]{1,0:T(8,128)}, ...) | async-done | bytes 4718608 | tf_op jit(solution)/shard_map/psum | solution.py:219
  (234 shorter events, 66.6 us)
Async XLA Ops:
  7.2 316.9 %copy-start = (bf16[1,768,1536]{2,1,0:T(8,128)(2,1)S(1)}, bf16[1,768,1536]{2,1,0:T(8,128)(2,1)}, u32[]{:S(2)}) copy-start(bf16[1,768,1536]{2,1,0:T(8,128)(2,1)} %param.35) | copy-start | bytes 7077892
  7.2 100.8 %all-reduce.10.cloned.1.call-start = ((), (), s32[]{:S(2)}) async-start(), calls=%async_computation.4 | async-start | bytes 9682944 | tf_op jit(solution)/shard_map/psum | solution.py:113
  8.1 52.2 %copy-start.56 = (pred[8,197]{1,0:T(8,128)(4,1)}, pred[8,197]{1,0:T(8,128)(4,1)S(1)}, u32[]{:S(2)}) copy-start(pred[8,197]{1,0:T(8,128)(4,1)S(1)} %broadcast_compare_fusion) | copy-start | bytes 4732
  8.1 6.0 copy-start.54
  8.1 6.0 copy-start.63
  10.8 3.8 copy-start.2
  10.8 4.9 copy-start.39
  14.7 3.6 copy-start.45
  20.8 9.4 copy-start.26
  20.8 9.4 copy-start.70
  57.5 3.8 copy-start.6
  57.5 3.9 copy-start.24
  57.5 3.8 copy-start.12
  61.4 3.4 copy-start.32
  64.7 6.1 copy-start.20
  70.8 5.0 copy-start.34
  75.8 7.6 copy-start.67
  75.8 7.7 copy-start.66
  75.8 32.2 %copy-start.58 = (f32[768]{0:T(1024)S(1)}, f32[768]{0:T(1024)}, u32[]{:S(2)}) copy-start(f32[768]{0:T(1024)} %param.31) | copy-start | bytes 9220
  83.7 66.3 %copy-start.60 = (s32[3152]{0:T(1024)}, s32[3152]{0:T(1024)S(1)}, u32[]{:S(2)}) copy-start(s32[3152]{0:T(1024)S(1)} %broadcast_select_fusion) | copy-start | bytes 37828
  172.0 123.4 %all-to-all-start = ((bf16[16,248,768]{2,1,0:T(8,128)(2,1)}), bf16[16,248,768]{2,1,0:T(8,128)(2,1)}, u32[]{:S(2)}, u32[]{:S(2)}) async-start(bf16[16,248,768]{2,1,0:T(8,128)(2,1)} %bitcast.115), calls=%async_computation | async-start | bytes 12189696 | tf_op jit(solution)/shard_map/all_to_all | solution.py:72
  193.7 12.7 copy-start.62
  193.7 13.3 %copy-start.49 = (bf16[768,16]{0,1:T(8,128)(2,1)S(1)}, bf16[768,16]{0,1:T(8,128)(2,1)}, u32[]{:S(2)}) copy-start(bf16[768,16]{0,1:T(8,128)(2,1)} %param.34) | copy-start | bytes 73732
  210.7 40.5 %copy-start.35 = (s32[1576,2]{0,1:T(2,128)S(1)}, s32[1576,2]{0,1:T(2,128)}, u32[]{:S(2)}) copy-start(s32[1576,2]{0,1:T(2,128)} %param.22) | copy-start | bytes 37828
  251.5 33.5 %copy-start.11 = (f32[1576,2]{1,0:T(8,128)}, f32[1576,2]{1,0:T(8,128)S(1)}, u32[]{:S(2)}) copy-start(f32[1576,2]{1,0:T(8,128)S(1)} %copy.146) | copy-start | bytes 37828
  295.4 28.7 %copy-start.61 = (f32[1536]{0:T(1024)S(1)}, f32[1536]{0:T(1024)}, u32[]{:S(2)}) copy-start(f32[1536]{0:T(1024)} %reduce.13) | copy-start | bytes 18436
  295.4 141.6 %all-to-all-start.2 = ((bf16[16,248,768]{2,1,0:T(8,128)(2,1)}), bf16[16,248,768]{2,1,0:T(8,128)(2,1)}, u32[]{:S(2)}, u32[]{:S(2)}) async-start(bf16[16,248,768]{2,1,0:T(8,128)(2,1)} %bitcast.116), calls=%async_computation.2 | async-start | bytes 12189696 | tf_op jit(solution)/shard_map/all_to_all | solution.py:72
  324.0 223.7 %all-reduce.12.cloned.1.call-start = ((), (), s32[]{:S(2)}) async-start(), calls=%async_computation.5 | async-start | bytes 24379392 | tf_op jit(solution)/shard_map/psum | solution.py:76
  324.1 68.1 %copy-start.68 = (bf16[1,1536,768]{2,1,0:T(8,128)(2,1)S(1)}, bf16[1,1536,768]{2,1,0:T(8,128)(2,1)}, u32[]{:S(2)}) copy-start(bf16[1,1536,768]{2,1,0:T(8,128)(2,1)} %param.37) | copy-start | bytes 7077892
  387.8 4.5 copy-start.71
  523.6 24.2 %copy-start.65 = (f32[1,768]{1,0:T(1,128)S(1)}, f32[1,768]{1,0:T(1,128)}, u32[]{:S(2)}) copy-start(f32[1,768]{1,0:T(1,128)} %param.38) | copy-start | bytes 9220
  523.6 140.7 %all-to-all-start.3 = ((bf16[16,248,768]{2,1,0:T(8,128)(2,1)}), bf16[16,248,768]{2,1,0:T(8,128)(2,1)}, u32[]{:S(2)}, u32[]{:S(2)}) async-start(bf16[16,248,768]{2,1,0:T(8,128)(2,1)} %bitcast.118), calls=%async_computation.3 | async-start | bytes 12189696 | tf_op jit(solution)/shard_map/all_to_all | solution.py:79
  664.2 28.8 %copy-start.51 = (s32[8,197]{1,0:T(8,128)S(1)}, s32[8,197]{1,0:T(8,128)}, u32[]{:S(2)}) copy-start(s32[8,197]{1,0:T(8,128)} %param.21) | copy-start | bytes 18916
  664.2 28.9 %copy-start.25 = (f32[8,6,197]{2,1,0:T(8,128)S(1)}, f32[8,6,197]{2,1,0:T(8,128)}, u32[]{:S(2)}) copy-start(f32[8,6,197]{2,1,0:T(8,128)} %copy-done.24) | copy-start | bytes 113476
  664.2 28.9 %copy-start.33 = (f32[8,6,197]{2,1,0:T(8,128)S(1)}, f32[8,6,197]{2,1,0:T(8,128)}, u32[]{:S(2)}) copy-start(f32[8,6,197]{2,1,0:T(8,128)} %copy-done.32) | copy-start | bytes 113476
  664.2 28.9 %copy-start.1 = (s32[3152]{0:T(1024)S(1)}, s32[3152]{0:T(1024)}, u32[]{:S(2)}) copy-start(s32[3152]{0:T(1024)} %get-tuple-element.51) | copy-start | bytes 37828
  664.3 143.5 %all-to-all-start.1 = ((bf16[16,248,768]{2,1,0:T(8,128)(2,1)}), bf16[16,248,768]{2,1,0:T(8,128)(2,1)}, u32[]{:S(2)}, u32[]{:S(2)}) async-start(bf16[16,248,768]{2,1,0:T(8,128)(2,1)} %bitcast.117), calls=%async_computation.1 | async-start | bytes 12189696 | tf_op jit(solution)/shard_map/all_to_all | solution.py:79
  693.0 379.6 %all-reduce.14.cloned.1.call-start = ((), (), s32[]{:S(2)}) async-start(), calls=%async_computation.6 | async-start | bytes 9682944 | tf_op jit(solution)/shard_map/psum | solution.py:215
  877.7 26.7 %copy-start.36 = (s32[1576,2]{0,1:T(2,128)S(1)}, s32[1576,2]{0,1:T(2,128)}, u32[]{:S(2)}) copy-start(s32[1576,2]{0,1:T(2,128)} %param.22) | copy-start | bytes 37828
  877.7 26.7 %copy-start.17 = (f32[1576,16]{0,1:T(8,128)S(1)}, f32[1576,16]{0,1:T(8,128)}, u32[]{:S(2)}) copy-start(f32[1576,16]{0,1:T(8,128)} %copy-done.16) | copy-start | bytes 302596
  877.7 26.7 %copy-start.38 = (f32[1576]{0:T(1024)S(1)}, f32[1576]{0:T(1024)}, u32[]{:S(2)}) copy-start(f32[1576]{0:T(1024)} %copy-done.37) | copy-start | bytes 18916
  877.7 26.8 %copy-start.44 = (f32[1576]{0:T(1024)S(1)}, f32[1576]{0:T(1024)}, u32[]{:S(2)}) copy-start(f32[1576]{0:T(1024)} %copy-done.43) | copy-start | bytes 18916
  877.7 26.9 %copy-start.42 = (f32[1576]{0:T(1024)S(1)}, f32[1576]{0:T(1024)}, u32[]{:S(2)}) copy-start(f32[1576]{0:T(1024)} %copy-done.41) | copy-start | bytes 18916
  877.7 26.9 %copy-start.48 = (f32[1576]{0:T(1024)S(1)}, f32[1576]{0:T(1024)}, u32[]{:S(2)}) copy-start(f32[1576]{0:T(1024)} %copy-done.47) | copy-start | bytes 18916
  877.7 26.9 %copy-start.50 = (bf16[768,16]{0,1:T(8,128)(2,1)S(1)}, bf16[768,16]{0,1:T(8,128)(2,1)}, u32[]{:S(2)}) copy-start(bf16[768,16]{0,1:T(8,128)(2,1)} %param.34) | copy-start | bytes 73732
  877.7 26.9 %copy-start.53 = (f32[768]{0:T(1024)S(1)}, f32[768]{0:T(1024)}, u32[]{:S(2)}) copy-start(f32[768]{0:T(1024)} %param.32) | copy-start | bytes 9220
  877.7 26.9 %copy-start.59 = (f32[768]{0:T(1024)S(1)}, f32[768]{0:T(1024)}, u32[]{:S(2)}) copy-start(f32[768]{0:T(1024)} %param.31) | copy-start | bytes 9220
  877.7 39.6 %slice-start = ((s8[4841472]{0:T(1024)(128)(4,1)}), s8[647168]{0:T(1024)(128)(4,1)S(1)}, s32[]{:S(2)}) async-start(s8[4841472]{0:T(1024)(128)(4,1)} %bitcast.111), calls=%async_computation.8 | async-start | bytes 1294336
  904.6 12.7 slice-start.1
  917.3 6.4 copy-start.21
  936.0 7.3 copy-start.13
  936.0 7.3 copy-start.57
  1000.9 11.5 copy-start.27
  1012.4 2.9 copy-start.29
  1020.9 241.3 %all-reduce.16.cloned.1.call-start = ((), (), s32[]{:S(2)}) async-start(), calls=%async_computation.7 | async-start | bytes 9437184 | tf_op jit(solution)/shard_map/psum | solution.py:219
  1027.0 16.5 %copy-start.15 = (bf16[1576,384]{0,1:T(8,128)(2,1)S(1)}, bf16[1576,384]{0,1:T(8,128)(2,1)}, u32[]{:S(2)}) copy-start(bf16[1576,384]{0,1:T(8,128)(2,1)} %reshape.255) | copy-start | bytes 3631108
  1027.0 16.5 %copy-start.19 = (bf16[1576,768]{1,0:T(8,128)(2,1)S(1)}, bf16[1576,768]{1,0:T(8,128)(2,1)}, u32[]{:S(2)}) copy-start(bf16[1576,768]{1,0:T(8,128)(2,1)} %copy-done.18) | copy-start | bytes 7262212
  1043.5 7.9 slice-start.2
  1046.2 5.3 slice-start.3
  1053.8 18.8 %copy-start.40 = (f32[1576]{0:T(1024)S(1)}, f32[1576]{0:T(1024)}, u32[]{:S(2)}) copy-start(f32[1576]{0:T(1024)} %copy-done.39) | copy-start | bytes 18916
  1053.8 18.8 %copy-start.46 = (f32[1576]{0:T(1024)S(1)}, f32[1576]{0:T(1024)}, u32[]{:S(2)}) copy-start(f32[1576]{0:T(1024)} %copy-done.45) | copy-start | bytes 18916
  1053.8 18.8 %copy-start.55 = (f32[768]{0:T(1024)S(1)}, f32[768]{0:T(1024)}, u32[]{:S(2)}) copy-start(f32[768]{0:T(1024)} %param.23) | copy-start | bytes 9220
  1262.1 4.9 copy-start.23
  1262.1 5.9 copy-start.22
  (20 other events, 36.8 us)
Sparse Core Ops, SparseCore 0:
  76.0 32.0 all-reduce.9
  404.4 50.0 all-reduce.11
  1021.0 49.8 all-reduce.13
  1078.9 183.1 all-reduce.15
where the time goes:
time: 1290 us; the launch traced here: 1280 us
  local copies, waits for them, and re-layouts  357 us (28%)
  matrix products  275 us (21%)
  waiting for transfers between devices  247 us (19%)
  other arithmetic  160 us (12%)
  blocking collectives  133 us (10%)
  starting transfers between devices  88.6 us (7%)
  between operations  15.9 us (1%)
    all_to_all x2, waiting for transfers between devices, send_back(): lax.all_to_all(total.astype(bf16).reshape(experts, capacity, width), 'exp...  108 us
    psum x1, blocking collectives, on_device(): lax.psum((grad_w_query, grad_w_key, grad_w_value, grad_b_query, grad_b_va...  98.4 us
    psum x1, waiting for transfers between devices, on_device(): lax.psum((grad_w_query, grad_w_key, grad_w_value, grad_b_query, grad_b_va...  70.9 us
    dot_general x1, matrix products, on_device(): jnp.dot(expert_rows, w_in[0], preferred_element_type=f32) + b_in[0]  63.6 us
    gather x1, local copies, waits for them, and re-layouts, on_device(): back_rows[flat_ids, slot_pos].reshape(tok_rows, 2, width).astype(f32)  58.3 us
    gather x1, local copies, waits for them, and re-layouts, on_device(): grad_back[flat_ids, slot_pos].reshape(tok_rows, 2, width).astype(f32)  58.2 us
    all_to_all x2, starting transfers between devices, send_back(): lax.all_to_all(total.astype(bf16).reshape(experts, capacity, width), 'exp...  52.8 us
    reduce_sum x1, other arithmetic, on_device(): jnp.sum(grad_back[flat_ids, slot_pos].reshape(tok_rows, 2, width).astype(...  44.9 us
  transfers between devices with their start and end apart: 8, of which 5 were waited for; matrix products, arithmetic and copies ran while one was open for 34% of the time, Pallas kernels for 0%

commit v1 on v0

v1 whole, which is shorter than its diff:
```python
import functools

import jax
import jax.numpy as jnp
from jax import lax
from jax.experimental import pallas as pl
from jax.experimental.pallas import tpu as pltpu
from jax.sharding import PartitionSpec as P

HEAD_DIM = 64
LANES = 128
LOG2E = 1.4426950408889634
MASKED = -1e30
MESH = pl.DeviceIdType.MESH
VMEM_LIMIT = 60 << 20
f32 = jnp.float32
bf16 = jnp.bfloat16
i32 = jnp.int32


def up(value, step):
    return -(-value // step) * step


def params(**more):
    return pltpu.CompilerParams(vmem_limit_bytes=VMEM_LIMIT, **more)


def whole(shape):
    return pl.BlockSpec(shape, lambda *_: (0,) * len(shape))


def dot(a, b):
    return lax.dot_general(a, b, (((1,), (0,)), ((), ())), preferred_element_type=f32)


def dot_nt(a, b):
    return lax.dot_general(a, b, (((1,), (1,)), ((), ())), preferred_element_type=f32)


def dot_tn(a, b):
    return lax.dot_general(a, b, (((0,), (0,)), ((), ())), preferred_element_type=f32)


def lane_iota(shape):
    return lax.broadcasted_iota(i32, shape, len(shape) - 1)


def norm_parts(values):
    center = values - jnp.mean(values, -1, keepdims=True)
    inv_std = lax.rsqrt(jnp.mean(center * center, -1, keepdims=True) + 1e-06)
    return center * inv_std, inv_std


def norm_back(grad_out, normed, inv_std, gain):
    scaled = grad_out * gain
    return inv_std * (
        scaled
        - jnp.mean(scaled, -1, keepdims=True)
        - normed * jnp.mean(scaled * normed, -1, keepdims=True)
    )


def gelu_parts(x):
    z = jnp.abs(x) * 0.7071067811865476
    t = 1.0 / (1.0 + 0.3275911 * z)
    poly = t * (
        0.254829592 * 0.5
        + t
        * (
            -0.284496736 * 0.5
            + t * (1.421413741 * 0.5 + t * (-1.453152027 * 0.5 + t * (1.061405429 * 0.5)))
        )
    )
    e = jnp.exp2(x * x * (-0.5 * LOG2E))
    half = poly * e
    cdf = jnp.where(x >= 0, 1.0 - half, half)
    return x * cdf, cdf + x * e * 0.3989422804014327


def prep_kernel(dims, routes_ref, cot_ref, grow_ref, post_ref, fidx_ref, g16):
    images, seq, seq_pad, experts, cap_dev = dims
    tok_pad = images * seq_pad
    core = lax.axis_index("tensor")
    expert = lax.axis_index("expert")
    for i in range(images):
        rows = cot_ref[seq * i : seq * (i + 1), :].astype(bf16)
        g16[seq_pad * i : seq_pad * (i + 1), :] = jnp.zeros((seq_pad, rows.shape[1]), bf16)
        g16[seq_pad * i : seq_pad * i + seq, :] = rows
    r0 = routes_ref[:, 0:1]
    r1 = routes_ref[:, 1:2]
    lanes = lane_iota((tok_pad, LANES))
    named0 = r0 == lanes
    named1 = r1 == lanes
    named = jnp.where(named0 | named1, 1.0, 0.0)
    named_low = named.astype(bf16)
    lower = (
        lax.broadcasted_iota(i32, (seq_pad, seq_pad), 1)
        < lax.broadcasted_iota(i32, (seq_pad, seq_pad), 0)
    ).astype(f32).astype(bf16)
    run = jnp.zeros((1, LANES), f32)
    parts = []
    for i in range(images):
        rows = slice(seq_pad * i, seq_pad * (i + 1))
        parts.append(dot(lower, named_low[rows]) + run)
        run = run + jnp.sum(named[rows], 0, keepdims=True)
    before = jnp.concatenate(parts, 0) - (core * cap_dev).astype(f32)
    pos = jnp.where(named > 0, before, -1.0)
    groups, _, _, group = post_ref.shape
    for j in range(groups):
        turned = jnp.transpose(pos[group * j : group * (j + 1)], (1, 0))
        for e in range(experts):
            post_ref[j, e] = turned[e : e + 1]
    for k, named_k, r_k in ((0, named0, r0), (1, named1, r1)):
        slot = jnp.sum(jnp.where(named_k, before, 0.0), 1, keepdims=True)
        fits = (slot >= 0) & (slot < cap_dev) & (r_k >= 0)
        turn = lax.rem(r_k - expert + experts, experts)
        flat = turn.astype(f32) * cap_dev + slot
        fidx_ref[:, k : k + 1] = jnp.where(fits, flat, -1.0).astype(i32)
    slots = lax.broadcasted_iota(i32, (cap_dev, group), 0).astype(f32)
    for e in range(experts):
        total = None
        for j in range(groups):
            named_e = post_ref[j, lax.rem(expert + e, experts)]
            pick = jnp.where(named_e == slots, 1.0, 0.0).astype(bf16)
            term = dot(pick, g16[group * j : group * (j + 1), :])
            total = term if total is None else total + term
        grow_ref[e] = total.astype(bf16)


def combine_kernel(cap_dev, with_dots, rows_ref, gslot_ref, fidx_ref, *rest):
    if with_dots:
        grow_ref, own_ref, out_ref, own_dots_ref, dots_ref, scaled, spread = rest
    else:
        own_ref, out_ref, scaled = rest
    rows_all = rows_ref.shape[0]
    tile = LANES
    lanes = lane_iota((tile, LANES))
    for i in range(rows_all // tile):
        here = slice(tile * i, tile * (i + 1))
        rows = rows_ref[here, :].astype(f32)
        scaled[here, :] = (rows * gslot_ref[here, :]).astype(bf16)
        if with_dots:
            dots = jnp.sum(rows * grow_ref[here, :].astype(f32), 1, keepdims=True)
            owner = (lax.broadcasted_iota(i32, (tile, LANES), 0) + tile * i) // cap_dev
            owner = lax.rem(owner + lax.axis_index("expert"), lax.axis_size("expert"))
            spread[here, :] = jnp.where(lanes == owner, dots, 0.0).astype(bf16)
    group = own_ref.shape[0]
    n = out_ref.shape[0] + 1
    me = lax.axis_index("tensor")
    step = 208 if group % 208 == 0 else group
    lanes = lane_iota((step, rows_all))
    for k in range(n):
        base = lax.rem(me + k, n) * group
        for i in range(group // step):
            tok = pl.ds(pl.multiple_of(base + i * step, 16), step)
            hit = (fidx_ref[tok, 0:1] == lanes) | (fidx_ref[tok, 1:2] == lanes)
            pick = jnp.where(hit, 1.0, 0.0).astype(bf16)
            to = slice(i * step, (i + 1) * step)
            (own_ref if k == 0 else out_ref.at[k - 1])[to, :] = dot(pick, scaled[...]).astype(bf16)
            if with_dots:
                (own_dots_ref if k == 0 else dots_ref.at[k - 1])[to, :] = dot(
                    pick, spread[...]
                ).astype(bf16)


def piece(own_ref, rest_ref, j):
    return own_ref[...] if j == 0 else rest_ref[j - 1]


def read_image(dst, src, image, seq):
    for n in range(src.shape[0] // seq):

        @pl.when(image == n)
        def _(n=n):
            dst[0:seq, :] = src[seq * n : seq * (n + 1), :]


def write_image(dst, value, image, seq):
    for n in range(dst.shape[0] // seq):

        @pl.when(image == n)
        def _(n=n):
            dst[seq * n : seq * (n + 1), :] = value[:seq]


def attn_fwd_kernel(
    dims, tok_ref, valid_ref, mask_ref, g1_ref, b1_ref, wq, wqs, wk, wks, wv, wvs, wp, wps,
    bq_ref, bv_ref, bp_ref, g2_ref, b2_ref, wr_ref,
    h1_ref, q_ref, k_ref, v_ref, probs_ref, heads_ref, mid_ref, h2x_ref, acc_ref, x_s
):
    seq, seq_pad, key_pad, own, experts = dims
    width = tok_ref.shape[1]
    step = pl.program_id(0)
    image = lax.axis_index("tensor") * own + step
    x_s[...] = jnp.zeros_like(x_s)
    read_image(x_s, tok_ref, image, seq)
    x = x_s[...]
    normed, _ = norm_parts(x)
    h1 = (normed * g1_ref[...] + b1_ref[...]).astype(bf16)
    h1_ref[0] = h1
    k_ref[0, seq_pad:, :] = jnp.zeros((key_pad - seq_pad, width), bf16)
    v_ref[0, seq_pad:, :] = jnp.zeros((key_pad - seq_pad, width), bf16)
    shares = [slice(wq.shape[1] * j, wq.shape[1] * (j + 1)) for j in range(wqs.shape[0] + 1)]
    for j, cols in enumerate(shares):
        q_ref[0, :, cols] = (dot(h1, piece(wq, wqs, j)) + bq_ref[:, cols]).astype(bf16)
        k_ref[0, 0:seq_pad, cols] = dot(h1, piece(wk, wks, j)).astype(bf16)
        v_ref[0, 0:seq_pad, cols] = (dot(h1, piece(wv, wvs, j)) + bv_ref[:, cols]).astype(bf16)
    low_half = lane_iota((seq_pad, LANES)) < HEAD_DIM
    mask = mask_ref[0]
    for p in range(width // LANES):
        cols = slice(LANES * p, LANES * (p + 1))
        qp = q_ref[0, :, cols]
        zero = jnp.zeros_like(qp)
        qs = jnp.concatenate([jnp.where(low_half, qp, zero), jnp.where(low_half, zero, qp)], 0)
        s = dot_nt(qs, k_ref[0, :, cols]) * (HEAD_DIM**-0.5 * LOG2E) + mask
        e = jnp.exp2(s - jnp.max(s, -1, keepdims=True))
        prob = (e * (1.0 / jnp.sum(e, -1, keepdims=True))).astype(bf16)
        probs_ref[0, p] = prob
        o = dot(prob, v_ref[0, :, cols])
        heads_ref[0, :, cols] = jnp.where(low_half, o[:seq_pad], o[seq_pad:]).astype(bf16)
    attn = bp_ref[...]
    for j, cols in enumerate(shares):
        attn = attn + dot(heads_ref[0, :, cols], piece(wp, wps, j))
    middle = x + attn
    mid_ref[0] = middle
    ok = valid_ref[0]

    @pl.when(step == 0)
    def _():
        acc_ref[...] = jnp.zeros_like(acc_ref)

    for row, field in enumerate((x, middle, attn)):
        acc_ref[row : row + 1, :] += jnp.sum(ok * field * field, 0, keepdims=True)
    normed2, _ = norm_parts(middle)
    h2 = (normed2 * g2_ref[...] + b2_ref[...]).astype(bf16)
    h2x_ref[0, :, 0:width] = h2
    logits = dot(h2, wr_ref[...])
    logits = jnp.where(lane_iota(logits.shape) < experts, logits, MASKED)
    e = jnp.exp(logits - jnp.max(logits, -1, keepdims=True))
    prob = e / jnp.sum(e, -1, keepdims=True)
    high = prob.astype(bf16).astype(f32)
    h2x_ref[0, :, width:] = (high + pltpu.roll(prob - high, experts, 1)).astype(bf16)


def attn_bwd_kernel(
    dims, tok_ref, cot_ref, valid_ref, accf_ref, mid_ref, h2x_ref, h1_ref, q_ref, k_ref, v_ref, probs_ref,
    heads_ref, moe_own, moe_ref, dots_own, dots_ref, gmoe_own, gmoe_ref, g1_ref, g2_ref,
    wq, wqs, wk, wks, wv, wvs, wp, wps, wr_ref,
    out_ref, gin_ref, grad_own, grad_rest, acc_ref,
    x_s, c_s, gh_s, h1_s, heads_s, ga_s, dq_s, dk_s, dv_s
):
    seq, seq_pad, key_pad, own, experts = dims
    width = tok_ref.shape[1]
    step = pl.program_id(0)
    shares = [slice(wq.shape[1] * j, wq.shape[1] * (j + 1)) for j in range(wqs.shape[0] + 1)]
    small_b = small_base(len(shares))
    image = lax.axis_index("tensor") * own + step
    at = pl.multiple_of(step * seq_pad, 16)
    pad = jnp.zeros((seq_pad - seq + 8, width), f32)
    x_s[seq // 8 * 8 :, :] = pad[: seq_pad - seq // 8 * 8]
    c_s[seq // 8 * 8 :, :] = pad[: seq_pad - seq // 8 * 8]
    read_image(x_s, tok_ref, image, seq)
    read_image(c_s, cot_ref, image, seq)
    ok = valid_ref[0]

    @pl.when(step == 0)
    def _():
        acc_ref[...] = jnp.zeros_like(acc_ref)
        acc_ref[small_b : small_b + 8, :] = accf_ref[...]

    def add(row, value):
        acc_ref[row : row + 1, :] += jnp.sum(value, 0, keepdims=True)

    def total(own_ref, rest_ref):
        value = own_ref[0].astype(f32)
        for j in range(rest_ref.shape[0]):
            value = value + rest_ref[j, 0].astype(f32)
        return value

    middle = mid_ref[0]
    moe = total(moe_own, moe_ref)
    output = middle + moe
    write_image(out_ref, output, step, seq)
    add(0, ok * output * output)
    add(1, ok * moe * moe)
    h2 = h2x_ref[0, :, 0:width]
    pair = h2x_ref[0, :, width:].astype(f32)
    prob = jnp.where(
        lane_iota(pair.shape) < experts, pair + pltpu.roll(pair, LANES - experts, 1), 0.0
    )
    grad_probs = total(dots_own, dots_ref)
    grad_logits = (
        prob * (grad_probs - jnp.sum(grad_probs * prob, -1, keepdims=True))
    ).astype(bf16)
    acc_ref[small_b + 8 : small_b + 8 + experts, :] += dot_tn(grad_logits, h2)[:experts]
    grad_h2 = dot_nt(grad_logits, wr_ref[...]) + total(gmoe_own, gmoe_ref)
    normed2, inv2 = norm_parts(middle)
    add(2, grad_h2 * normed2)
    add(3, grad_h2)
    grad_middle = c_s[...] + norm_back(grad_h2, normed2, inv2, g2_ref[...])
    c_s[...] = grad_middle
    grad_attn = grad_middle.astype(bf16)
    add(4, grad_attn.astype(f32))
    ga_s[pl.ds(at, seq_pad), :] = grad_attn
    heads_s[pl.ds(at, seq_pad), :] = heads_ref[0]
    h1_s[pl.ds(at, seq_pad), :] = h1_ref[0]
    for j, cols in enumerate(shares):
        gh_s[:, cols] = dot_nt(grad_attn, piece(wp, wps, j)).astype(bf16)
    low_half = lane_iota((seq_pad, LANES)) < HEAD_DIM

    def split(value):
        zero = jnp.zeros_like(value)
        return jnp.concatenate(
            [jnp.where(low_half, value, zero), jnp.where(low_half, zero, value)], 0
        )

    for p in range(width // LANES):
        cols = slice(LANES * p, LANES * (p + 1))
        gs = split(gh_s[:, cols])
        qs = split(q_ref[0, :, cols])
        low_prob = probs_ref[0, p]
        weights = low_prob.astype(f32)
        mixed = weights * dot_nt(gs, v_ref[0, :, cols])
        ds = (
            (mixed - weights * jnp.sum(mixed, -1, keepdims=True)) * (HEAD_DIM**-0.5)
        ).astype(bf16)
        dq = dot(ds, k_ref[0, :, cols])
        dq_s[pl.ds(at, seq_pad), cols] = jnp.where(
            low_half, dq[:seq_pad], dq[seq_pad:]
        ).astype(bf16)
        dk_s[pl.ds(at, seq_pad), cols] = dot_tn(ds, qs)[:seq_pad].astype(bf16)
        dv_s[pl.ds(at, seq_pad), cols] = dot_tn(low_prob, gs)[:seq_pad].astype(bf16)
    dq = dq_s[pl.ds(at, seq_pad), :]
    dk = dk_s[pl.ds(at, seq_pad), :]
    dv = dv_s[pl.ds(at, seq_pad), :]
    which = lax.broadcasted_iota(i32, (small_b, shares[0].stop), 0)
    for j, cols in enumerate(shares):
        owner = lax.rem(lax.axis_index("tensor") + j, len(shares))
        for base, value in ((8, dq), (8 + len(shares), dv)):
            total_j = jnp.sum(value[:, cols].astype(f32), 0, keepdims=True)
            acc_ref[0:small_b, shares[0]] += jnp.where(which == base + owner, total_j, 0.0)
    grad_h1 = None
    for j, cols in enumerate(shares):
        for left, own_ref, rest_ref in ((dq, wq, wqs), (dk, wk, wks), (dv, wv, wvs)):
            term = dot_nt(left[:, cols], piece(own_ref, rest_ref, j))
            grad_h1 = term if grad_h1 is None else grad_h1 + term
    normed1, inv1 = norm_parts(x_s[...])
    add(5, grad_h1 * normed1)
    add(6, grad_h1)
    add(7, jnp.broadcast_to(ok, grad_h1.shape))
    grad_in = c_s[...] + norm_back(grad_h1, normed1, inv1, g1_ref[...])
    write_image(gin_ref, grad_in, step, seq)

    @pl.when(step == own - 1)
    def _():
        for n, part in enumerate((dq_s, dk_s, dv_s, heads_s)):
            rows = slice(width * n, width * (n + 1))
            left = ga_s if n == 3 else h1_s
            grad = dot_tn(left[...], part[...])
            grad_own[rows, :] = grad[:, shares[0]]
            for j, cols in enumerate(shares[1:]):
                grad_rest[j, rows, :] = grad[:, cols].astype(bf16)


def small_base(cores):
    return up(8 + 2 * cores, 8)


def view(own_ref, rest_ref, j):
    return own_ref if j == 0 else rest_ref.at[j - 1]


def chunk_of(hidden):
    for size in (512, 384, 256, 128):
        if hidden % size == 0:
            return size
    return hidden


def greet(peers):
    barrier = pltpu.get_barrier_semaphore()
    for peer in peers:
        pl.semaphore_signal(barrier, inc=1, device_id=peer, device_id_type=MESH)
    pl.semaphore_wait(barrier, len(peers))


def around(axis):
    n = lax.axis_size(axis)
    me = lax.axis_index(axis)
    return n, lambda k: {axis: lax.rem(me + n + k, n)}


def moe_kernel(
    h2x_ref, post_ref, grow_hbm, w_in, w_ins, b_in, b_ins, w_out, w_outs, b_out_ref,
    back_ref, gback_ref, gslot_ref, gin_own, gout_own, gin_rest, gout_rest,
    gbin_own, gbin_rest, gbout_ref,
    table, out_s, rows_s, hid, slope, grow_s, res_s, gate_out, gate_in, stage_in, stage_out,
    gbin_send, gbout_send,
    local_sem, tab_send, tab_recv, h_send, h_recv, c_send, c_recv, r_send, r_recv, g_send, g_recv,
    w_send, w_recv, own_sem
):
    experts, chip = around("expert")
    cores, core = around("tensor")
    me_e = lax.axis_index("expert")
    me_t = lax.axis_index("tensor")
    cap_dev, width = rows_s.shape[1:]
    group = table.shape[1]
    share = w_in.shape[1]
    size = chunk_of(share)
    per = share // size
    greet([chip(k) for k in range(1, experts)] + [core(k) for k in range(1, cores)])

    def remote(src, dst, send, recv, there):
        return pltpu.make_async_remote_copy(
            src_ref=src, dst_ref=dst, send_sem=send, recv_sem=recv,
            device_id=there, device_id_type=MESH,
        )

    grow_copy = pltpu.make_async_copy(grow_hbm, grow_s, local_sem.at[0])
    grow_copy.start()
    own_copy = pltpu.make_async_copy(h2x_ref, table.at[me_t], local_sem.at[1])
    own_copy.start()
    fills = [
        remote(h2x_ref, table.at[me_t], tab_send.at[k], tab_recv.at[k], core(k))
        for k in range(1, cores)
    ]
    for copy in fills:
        copy.start()
    own_copy.wait()
    for copy in fills:
        copy.wait()

    slots = lax.broadcasted_iota(i32, (cap_dev, group), 0).astype(f32)
    lanes = lane_iota((cap_dev, LANES))

    def select(k):
        e = lax.rem(me_e + k, experts)
        total = None
        for j in range(cores):
            pick = jnp.where(post_ref[j, e] == slots, 1.0, 0.0).astype(bf16)
            term = dot(pick, table[j])
            total = term if total is None else total + term
        mine = (lanes == e) | (lanes == e + experts)
        gate = jnp.sum(jnp.where(mine, total[:, width:], 0.0), 1, keepdims=True)
        gslot_ref[pl.ds(pl.multiple_of(cap_dev * k, 8), cap_dev), :] = gate
        spread = jnp.transpose(jnp.broadcast_to(gate, (cap_dev, LANES)), (1, 0))
        return total[:, :width].astype(bf16), spread[0:8]

    def h_copy(k):
        return remote(out_s.at[k], rows_s.at[k], h_send.at[k], h_recv.at[k], chip(k))

    def c_copy(k):
        return remote(gate_out.at[k], gate_in.at[k], c_send.at[k], c_recv.at[k], chip(k))

    def r_copy(k):
        return remote(res_s.at[k], back_ref.at[k], r_send.at[k], r_recv.at[k], chip(-k))

    def g_copy(k):
        return remote(out_s.at[k], gback_ref.at[k], g_send.at[k], g_recv.at[k], chip(-k))

    def send_rows(k, _):
        rows, gate = select(k)
        out_s[k] = rows
        gate_out[k] = gate
        h_copy(k).start()
        c_copy(k).start()
        return 0

    lax.fori_loop(1, experts, send_rows, 0)
    rows, gate = select(0)
    rows_s[0] = rows
    gate_in[0] = gate

    def forward(i):
        x = rows_s[pl.ds(2 * i, 2)].reshape(2 * cap_dev, width)
        here = pl.ds(pl.multiple_of(2 * cap_dev * i, 16), 2 * cap_dev)
        total = None
        for j in range(cores):
            for n in range(per):
                cols = slice(size * n, size * (n + 1))
                flat = slice(share * j + size * n, share * j + size * (n + 1))
                pre = dot(x, view(w_in, w_ins, j)[:, cols]) + view(b_in, b_ins, j)[:, cols]
                act, steep = gelu_parts(pre)
                act = act.astype(bf16)
                hid[here, flat] = act
                slope[here, flat] = steep.astype(bf16)
                term = dot(act, view(w_out, w_outs, j)[cols, :])
                total = term if total is None else total + term
        res = (total + b_out_ref[...]).astype(bf16)
        res_s[pl.ds(2 * i, 2)] = res.reshape(2, cap_dev, width)

    h_copy(1).wait_recv()
    forward(0)
    own_res = pltpu.make_async_copy(res_s.at[0], back_ref.at[0], own_sem.at[0])
    own_res.start()
    r_copy(1).start()

    def forward_step(i, _):
        h_copy(2 * i).wait_recv()
        h_copy(2 * i + 1).wait_recv()
        forward(i)
        r_copy(2 * i).start()
        r_copy(2 * i + 1).start()
        return 0

    lax.fori_loop(1, experts // 2, forward_step, 0)

    def sent_rows(k, _):
        h_copy(k).wait_send()
        return 0

    lax.fori_loop(1, experts, sent_rows, 0)
    grow_copy.wait()

    def backward(i):
        g = grow_s[pl.ds(2 * i, 2)].reshape(2 * cap_dev, width)
        here = pl.ds(pl.multiple_of(2 * cap_dev * i, 16), 2 * cap_dev)
        total = None
        for j in range(cores):
            for n in range(per):
                cols = slice(size * n, size * (n + 1))
                flat = slice(share * j + size * n, share * j + size * (n + 1))
                grad = dot_nt(g, view(w_out, w_outs, j)[cols, :])
                gpre = (grad * slope[here, flat].astype(f32)).astype(bf16)
                slope[here, flat] = gpre
                term = dot_nt(gpre, view(w_in, w_ins, j)[:, cols])
                total = term if total is None else total + term
        out_s[pl.ds(2 * i, 2)] = total.astype(bf16).reshape(2, cap_dev, width)

    backward(0)
    own_grad = pltpu.make_async_copy(out_s.at[0], gback_ref.at[0], own_sem.at[1])
    own_grad.start()
    g_copy(1).start()

    def backward_step(i, _):
        backward(i)
        g_copy(2 * i).start()
        g_copy(2 * i + 1).start()
        return 0

    lax.fori_loop(1, experts // 2, backward_step, 0)

    def gates_in(k, _):
        c_copy(k).wait()
        return 0

    lax.fori_loop(1, experts, gates_in, 0)

    def scale_rows(k, total):
        square = jnp.broadcast_to(gate_in[k, 0:1, :], (LANES, cap_dev))
        gate = jnp.transpose(square, (1, 0))[:, 0:1]
        rows_s[k] = (rows_s[k].astype(f32) * gate).astype(bf16)
        scaled = (grow_s[k].astype(f32) * gate).astype(bf16)
        grow_s[k] = scaled
        return total + jnp.sum(scaled.astype(f32), 0, keepdims=True)

    bias = lax.fori_loop(0, experts, scale_rows, jnp.zeros((1, width), f32))
    gbout_send[...] = jnp.broadcast_to(bias, gbout_send.shape)
    gbout_ref[me_t] = jnp.broadcast_to(bias, gbout_send.shape)
    rows_all = experts * cap_dev

    def grads(col):
        cols = pl.ds(pl.multiple_of(col, LANES), size)
        left = rows_s[...].reshape(rows_all, width)
        right = grow_s[...].reshape(rows_all, width)
        return dot_tn(left, slope[:, cols]), dot_tn(hid[:, cols], right)

    def column_sums(col):
        cols = pl.ds(pl.multiple_of(col, LANES), size)
        total = jnp.zeros((1, size), f32)
        for k in range(experts):
            square = jnp.broadcast_to(gate_in[k, 0:1, :], (LANES, cap_dev))
            gate = jnp.transpose(square, (1, 0))[:, 0:1]
            here = slice(cap_dev * k, cap_dev * (k + 1))
            total = total + jnp.sum(slope[here, cols].astype(f32) * gate, 0, keepdims=True)
        return total

    pending = []
    for j in list(range(1, cores)) + [0]:
        for n in range(per):
            cols = slice(size * n, size * (n + 1))
            slot = len(pending) % 2
            if len(pending) >= 2:
                for wait in pending[-2]:
                    wait()
            gw_in, gw_out = grads(share * j + size * n)
            stage_in[slot] = gw_in.astype(bf16)
            stage_out[slot] = gw_out.astype(bf16)
            sums = column_sums(share * j + size * n)
            if j == 0:
                gbin_own[:, cols] = sums
                a = pltpu.make_async_copy(stage_in.at[slot], gin_own.at[:, cols], own_sem.at[2 + slot])
                b = pltpu.make_async_copy(stage_out.at[slot], gout_own.at[cols, :], own_sem.at[4 + slot])
                a.start()
                b.start()
                pending.append((a.wait, b.wait))
            else:
                gbin_send[j - 1, :, cols] = sums
                at = (j - 1) * per + n
                a = remote(
                    stage_in.at[slot], gin_rest.at[j - 1, :, cols],
                    w_send.at[0, at], w_recv.at[0, at], core(j),
                )
                b = remote(
                    stage_out.at[slot], gout_rest.at[j - 1, cols, :],
                    w_send.at[1, at], w_recv.at[1, at], core(j),
                )
                a.start()
                b.start()
                pending.append((a.wait_send, b.wait_send))
        if j != 0:
            tail = [
                remote(
                    gbin_send.at[j - 1], gbin_rest.at[j - 1],
                    w_send.at[2, j - 1], w_recv.at[2, j - 1], core(j),
                ),
                remote(
                    gbout_send, gbout_ref.at[me_t],
                    w_send.at[3, j - 1], w_recv.at[3, j - 1], core(j),
                ),
            ]
            for copy in tail:
                copy.start()
    for waits in pending[-2:]:
        for wait in waits:
            wait()
    for j in range(1, cores):
        for n in range(per):
            cols = slice(size * n, size * (n + 1))
            at = (j - 1) * per + n
            remote(
                stage_in.at[0], gin_rest.at[j - 1, :, cols],
                w_send.at[0, at], w_recv.at[0, at], core(j),
            ).wait_recv()
            remote(
                stage_out.at[0], gout_rest.at[j - 1, cols, :],
                w_send.at[1, at], w_recv.at[1, at], core(j),
            ).wait_recv()
        remote(
            gbin_send.at[j - 1], gbin_rest.at[j - 1],
            w_send.at[2, j - 1], w_recv.at[2, j - 1], core(j),
        ).wait()
        remote(
            gbout_send, gbout_ref.at[me_t], w_send.at[3, j - 1], w_recv.at[3, j - 1], core(j)
        ).wait()

    def finish(k, _):
        r_copy(k).wait()
        g_copy(k).wait()
        return 0

    lax.fori_loop(1, experts, finish, 0)
    own_res.wait()
    own_grad.wait()


def swap_kernel(gather, count, *refs):
    srcs, dsts, (ssem, rsem) = refs[:count], refs[count : 2 * count], refs[2 * count :]
    n = lax.axis_size("tensor")
    me = lax.axis_index("tensor")
    barrier = pltpu.get_barrier_semaphore()
    for k in range(1, n):
        pl.semaphore_signal(
            barrier, inc=1, device_id={"tensor": lax.rem(me + k, n)}, device_id_type=MESH
        )
    pl.semaphore_wait(barrier, n - 1)
    copies = []
    for a, (src, dst) in enumerate(zip(srcs, dsts)):
        for k in range(1, n):
            copies.append(
                pltpu.make_async_remote_copy(
                    src_ref=src if gather else src.at[k - 1],
                    dst_ref=dst.at[k - 1],
                    send_sem=ssem.at[a, k],
                    recv_sem=rsem.at[a, k],
                    device_id={"tensor": lax.rem(me + (n - k if gather else k), n)},
                    device_id_type=MESH,
                )
            )
    for copy in copies:
        copy.start()
    for copy in copies:
        copy.wait()


def swap(ident, gather, *arrays):
    n = lax.axis_size("tensor")
    count = len(arrays)
    outs = [
        jax.ShapeDtypeStruct(((n - 1,) + a.shape) if gather else a.shape, a.dtype) for a in arrays
    ]
    anywhere = pl.BlockSpec(memory_space=pl.ANY)
    return pl.pallas_call(
        functools.partial(swap_kernel, gather, count),
        out_shape=outs,
        in_specs=[anywhere] * count,
        out_specs=[anywhere] * count,
        scratch_shapes=[pltpu.SemaphoreType.DMA((count, n)), pltpu.SemaphoreType.DMA((count, n))],
        compiler_params=pltpu.CompilerParams(collective_id=ident, has_side_effects=True),
        name="swap%d" % ident,
    )(*arrays)


def reduce_kernel(
    chunks, own_ref, rest_ref, small_ref, wqkv_ref, wproj_ref, small_out,
    rest_s, acc, send_s, recv_s, low, small_r, small_m, small_s, small_t,
    t_send, t_recv, x_send, x_recv, st_send, st_recv, sx_send, sx_recv, sg_send, sg_recv
):
    experts, _ = around("expert")
    cores, core = around("tensor")
    me_e = lax.axis_index("expert")
    me_t = lax.axis_index("tensor")
    bits = experts.bit_length() - 1
    rows_all = own_ref.shape[0]
    rows = rows_all // chunks
    piece_rows = small_r.shape[1]

    def my_bit(b):
        return lax.rem(me_e // (1 << b), 2)

    def partner(b):
        return {"expert": me_e + (1 << b) * (1 - 2 * my_bit(b))}

    def remote(src, dst, send, recv, there):
        return pltpu.make_async_remote_copy(
            src_ref=src, dst_ref=dst, send_sem=send, recv_sem=recv,
            device_id=there, device_id_type=MESH,
        )

    greet([partner(b) for b in range(bits)] + [core(k) for k in range(1, cores)])

    first = []
    for c in range(chunks):
        here = slice(rows * c, rows * (c + 1))
        first.append([
            remote(
                rest_ref.at[k - 1, here, :], rest_s.at[k - 1, here, :],
                t_send.at[k - 1, c], t_recv.at[k - 1, c], core(k),
            )
            for k in range(1, cores)
        ])
    smalls = [
        remote(
            small_ref.at[pl.ds(pl.multiple_of(lax.rem(me_t + k, cores) * piece_rows, 8), piece_rows), :],
            small_r.at[k - 1], st_send.at[k - 1], st_recv.at[k - 1], core(k),
        )
        for k in range(1, cores)
    ]
    for copy in smalls:
        copy.start()
    for group in first:
        for copy in group:
            copy.start()

    def gather_chunk(c):
        here = slice(rows * c, rows * (c + 1))
        for copy in first[c]:
            copy.wait()
        total = own_ref[here, :]
        for k in range(cores - 1):
            total = total + rest_s[k, here, :].astype(f32)
        acc[here, :] = total

    orders = []
    for c in range(chunks):
        order = list(range(bits))
        if c % 2 == 1 and bits > 1:
            order[0], order[1] = 1, 0
        orders.append(order)
    base = [0] * chunks
    live = {}

    def start(c, s):
        if s < bits:
            b = orders[c][s]
            half = rows >> (s + 1)
            off = rows - 2 * half
            away = pl.ds(pl.multiple_of(rows * c + base[c] + (1 - my_bit(b)) * half, 8), half)
            box = slice(off, off + half)
            send_s[c, box, :] = acc[away, :].astype(bf16)
            copy = remote(
                send_s.at[c, box, :], recv_s.at[c, box, :],
                x_send.at[c, s], x_recv.at[c, s], partner(b),
            )
        else:
            b = orders[c][2 * bits - 1 - s]
            size = rows >> (2 * bits - s)
            if s == bits:
                mine = pl.ds(pl.multiple_of(rows * c + base[c], 16), size)
                low[mine, :] = acc[mine, :].astype(bf16)
            mine = pl.ds(pl.multiple_of(rows * c + base[c], 16), size)
            copy = remote(
                low.at[mine, :], low.at[mine, :], x_send.at[c, s], x_recv.at[c, s], partner(b)
            )
        copy.start()
        live[c, s] = copy

    def finish(c, s):
        live[c, s].wait()
        if s < bits:
            b = orders[c][s]
            half = rows >> (s + 1)
            off = rows - 2 * half
            base[c] = base[c] + my_bit(b) * half
            keep = pl.ds(pl.multiple_of(rows * c + base[c], 8), half)
            acc[keep, :] += recv_s[c, off : off + half, :].astype(f32)
        else:
            b = orders[c][2 * bits - 1 - s]
            size = rows >> (2 * bits - s)
            base[c] = base[c] - my_bit(b) * size
            if s == 2 * bits - 1:
                width = rows_all // 4
                here = slice(rows * c, rows * (c + 1))
                if rows * (c + 1) <= 3 * width:
                    wqkv_ref[here, :] = low[here, :].astype(f32)
                else:
                    top = min(max(rows * c, 3 * width), rows * (c + 1))
                    if top > rows * c:
                        wqkv_ref[rows * c : top, :] = low[rows * c : top, :].astype(f32)
                    wproj_ref[:, top - 3 * width : rows * (c + 1) - 3 * width] = jnp.transpose(
                        low[top : rows * (c + 1), :].astype(f32), (1, 0)
                    )

    def small_start(s):
        small_s[s] = small_m[...]
        copy = remote(
            small_s.at[s], small_t.at[s], sx_send.at[s], sx_recv.at[s], partner(s)
        )
        copy.start()
        live["small", s] = copy

    def small_finish(s):
        live["small", s].wait()
        small_m[...] += small_t[s]

    pairs = max(chunks // 2, 1)
    members = [[c for c in (2 * p, 2 * p + 1) if c < chunks] for p in range(pairs)]
    stages = 2 * bits
    for t in range(stages + pairs):
        for p in range(pairs):
            s = t - p
            for c in members[p]:
                if s == 0:
                    gather_chunk(c)
                if 1 <= s <= stages:
                    finish(c, s - 1)
                if 0 <= s < stages:
                    start(c, s)
        if t == 0:
            for copy in smalls:
                copy.wait()
            total = small_ref[pl.ds(pl.multiple_of(me_t * piece_rows, 8), piece_rows), :]
            for k in range(cores - 1):
                total = total + small_r[k]
            small_m[...] = total
            small_start(0)
        elif t <= bits:
            small_finish(t - 1)
            if t < bits:
                small_start(t)
            else:
                mine = pl.ds(pl.multiple_of(me_t * piece_rows, 8), piece_rows)
                small_out[mine, :] = small_m[...]
                lasts = [
                    remote(
                        small_m, small_out.at[mine, :], sg_send.at[k - 1], sg_recv.at[k - 1], core(k)
                    )
                    for k in range(1, cores)
                ]
                for copy in lasts:
                    copy.start()
    for copy in lasts:
        copy.wait()


def on_device(
    tokens_in, valid, routes, ln1_gain, ln1_bias, w_query, w_key, w_value, b_query, b_value,
    w_proj, b_proj, ln2_gain, ln2_bias, w_router, w_in, b_in, w_out, b_out, cotangent,
):
    tok_rows, width = tokens_in.shape
    images, seq = valid.shape
    experts = lax.axis_size("expert")
    cores = lax.axis_size("tensor")
    core = lax.axis_index("tensor")
    capacity = (10 * tok_rows // (4 * experts) // 8 + 1) * 8
    cap_dev = up(up(capacity, cores) // cores, 16)
    rows_all = experts * cap_dev
    seq_pad = up(seq, 16)
    key_pad = up(seq_pad, LANES)
    own = images // cores
    tok_own = own * seq
    tok_pad = images * seq_pad
    pad_own = own * seq_pad
    share = w_in.shape[2]
    hidden = share * cores
    wide = width + LANES
    pairs = width // LANES
    S = jax.ShapeDtypeStruct

    def row(v):
        return v.reshape(1, -1)

    def a2a(rows):
        return lax.all_to_all(rows, "expert", split_axis=0, concat_axis=0, tiled=True)

    routes_p = jnp.pad(
        routes.reshape(images, seq, 2), ((0, 0), (0, seq_pad - seq), (0, 0)), constant_values=-1
    ).reshape(tok_pad, 2)
    send_g, post, fidx = pl.pallas_call(
        functools.partial(prep_kernel, (images, seq, seq_pad, experts, cap_dev)),
        out_shape=[
            S((experts, cap_dev, width), bf16),
            S((cores, experts, 1, pad_own), f32),
            S((tok_pad, 2), i32),
        ],
        scratch_shapes=[pltpu.VMEM((tok_pad, width), bf16)],
        compiler_params=params(),
        name="prep",
    )(routes_p, cotangent)
    def turn(x):
        return lax.rem(jnp.arange(experts), experts)

    me_e = lax.axis_index("expert")
    turned = (jnp.arange(experts) + experts - me_e) % experts
    grow = a2a(send_g[turned])
    grow = grow[(me_e + experts - jnp.arange(experts)) % experts]

    own_w = (w_query, w_key, w_value, w_proj)
    *rest_w, bqs, bvs = swap(1, True, *own_w, row(b_query), row(b_value))
    attn_w = [w for pair in zip(own_w, rest_w) for w in pair]
    bq = jnp.concatenate([row(b_query)] + [bqs[j] for j in range(cores - 1)], 1)
    bv = jnp.concatenate([row(b_value)] + [bvs[j] for j in range(cores - 1)], 1)
    w_ins, w_outs, b_ins = swap(7, True, w_in[0], w_out[0], b_in)
    wr = jnp.pad(w_router, ((0, 0), (0, LANES - experts)))
    valid_own = lax.dynamic_slice_in_dim(valid, core * own, own, 0)
    valid_col = jnp.pad(valid_own.astype(f32), ((0, 0), (0, seq_pad - seq)))[:, :, None]
    mask_row = jnp.where(
        jnp.pad(valid_own, ((0, 0), (0, key_pad - seq))) > 0, 0.0, MASKED
    ).astype(f32)[:, None, :]

    dims = (seq, seq_pad, key_pad, own, experts)

    def per_image(*shape):
        return pl.BlockSpec((1,) + shape, lambda i: (i,) + (0,) * len(shape))

    h1, q, k, v, probs, heads, middle, h2x, acc_f = pl.pallas_call(
        functools.partial(attn_fwd_kernel, dims),
        grid=(own,),
        in_specs=[
            whole(tokens_in.shape),
            per_image(seq_pad, 1),
            per_image(1, key_pad),
            whole((1, width)),
            whole((1, width)),
            *[whole(w.shape) for w in attn_w],
            whole((1, width)),
            whole((1, width)),
            whole((1, width)),
            whole((1, width)),
            whole((1, width)),
            whole((width, LANES)),
        ],
        out_specs=[
            per_image(seq_pad, width),
            per_image(seq_pad, width),
            per_image(key_pad, width),
            per_image(key_pad, width),
            per_image(pairs, 2 * seq_pad, key_pad),
            per_image(seq_pad, width),
            per_image(seq_pad, width),
            per_image(seq_pad, wide),
            whole((8, width)),
        ],
        out_shape=[
            S((own, seq_pad, width), bf16),
            S((own, seq_pad, width), bf16),
            S((own, key_pad, width), bf16),
            S((own, key_pad, width), bf16),
            S((own, pairs, 2 * seq_pad, key_pad), bf16),
            S((own, seq_pad, width), bf16),
            S((own, seq_pad, width), f32),
            S((own, seq_pad, wide), bf16),
            S((8, width), f32),
        ],
        scratch_shapes=[pltpu.VMEM((seq_pad, width), f32)],
        compiler_params=params(),
        cost_estimate=pl.CostEstimate(
            flops=2 * pad_own * width * (4 * width + 2 * key_pad),
            bytes_accessed=24 << 20,
            transcendentals=0,
        ),
        name="attn_fwd",
    )(
        tokens_in, valid_col, mask_row, row(ln1_gain), row(ln1_bias), *attn_w, bq, bv,
        row(b_proj), row(ln2_gain), row(ln2_bias), wr,
    )

    size = chunk_of(share)
    per = share // size
    anywhere = pl.BlockSpec(memory_space=pl.ANY)
    inside = pl.BlockSpec(memory_space=pltpu.VMEM)
    block = (experts, cap_dev, width)
    DMA = pltpu.SemaphoreType.DMA
    (
        res_back, grad_back, gslot, gin_w, gout_w, gin_rest, gout_rest, gbin_own, gbin_rest, gb_out,
    ) = pl.pallas_call(
        moe_kernel,
        in_specs=[anywhere, inside, anywhere] + [inside] * 7,
        out_specs=[anywhere, anywhere, inside] + [anywhere] * 4 + [inside] * 3,
        out_shape=[
            S(block, bf16),
            S(block, bf16),
            S((rows_all, 1), f32),
            S((width, share), bf16),
            S((share, width), bf16),
            S((cores - 1, width, share), bf16),
            S((cores - 1, share, width), bf16),
            S((1, share), f32),
            S((cores - 1, 1, share), f32),
            S((cores, 8, width), f32),
        ],
        scratch_shapes=[
            pltpu.VMEM((cores, pad_own, wide), bf16),
            pltpu.VMEM(block, bf16),
            pltpu.VMEM(block, bf16),
            pltpu.VMEM((rows_all, hidden), bf16),
            pltpu.VMEM((rows_all, hidden), bf16),
            pltpu.VMEM(block, bf16),
            pltpu.VMEM(block, bf16),
            pltpu.VMEM((experts, 8, cap_dev), f32),
            pltpu.VMEM((experts, 8, cap_dev), f32),
            pltpu.VMEM((2, width, size), bf16),
            pltpu.VMEM((2, size, width), bf16),
            pltpu.VMEM((cores - 1, 1, share), f32),
            pltpu.VMEM((8, width), f32),
            DMA((2,)),
            DMA((cores,)),
            DMA((cores,)),
            *[DMA((experts,))] * 8,
            DMA((4, (cores - 1) * per)),
            DMA((4, (cores - 1) * per)),
            DMA((6,)),
        ],
        compiler_params=params(collective_id=2, has_side_effects=True),
        name="moe",
    )(
        h2x.reshape(pad_own, wide), post, grow, w_in[0], w_ins, b_in, b_ins, w_out[0], w_outs, b_out
    )
    res_back = res_back.reshape(rows_all, width)
    grad_back = grad_back.reshape(rows_all, width)
    grad_w_in, grad_w_out = [
        (own_part.astype(f32) + jnp.sum(rest_part.astype(f32), 0))[None]
        for own_part, rest_part in ((gin_w, gin_rest), (gout_w, gout_rest))
    ]
    grad_b_in = gbin_own + jnp.sum(gbin_rest, 0)
    grad_b_out = jnp.sum(gb_out[:, 0, :], 0, keepdims=True)

    moe_own, moe_p, dots_own, dots_p = pl.pallas_call(
        functools.partial(combine_kernel, cap_dev, True),
        out_shape=[
            S((pad_own, width), bf16),
            S((cores - 1, pad_own, width), bf16),
            S((pad_own, LANES), bf16),
            S((cores - 1, pad_own, LANES), bf16),
        ],
        scratch_shapes=[pltpu.VMEM((rows_all, width), bf16), pltpu.VMEM((rows_all, LANES), bf16)],
        compiler_params=params(),
        name="combine_res",
    )(res_back, gslot, fidx, send_g.reshape(rows_all, width))
    moe, dots = swap(4, False, moe_p, dots_p)
    gmoe_own, gmoe_p = pl.pallas_call(
        functools.partial(combine_kernel, cap_dev, False),
        out_shape=[S((pad_own, width), bf16), S((cores - 1, pad_own, width), bf16)],
        scratch_shapes=[pltpu.VMEM((rows_all, width), bf16)],
        compiler_params=params(),
        name="combine_grad",
    )(grad_back, gslot, fidx)
    (gmoe,) = swap(5, False, gmoe_p)

    def pieces(n):
        return pl.BlockSpec((cores - 1, 1, seq_pad, n), lambda i: (0, i, 0, 0))

    def by_image(x):
        return x.reshape(x.shape[:-2] + (own, seq_pad, x.shape[-1]))

    head_share = w_query.shape[1]
    small_b = small_base(cores)
    small_rows = up(small_b + 8 + experts, 8 * cores)
    out_own, gin_own, grad_own, grad_rest, small = pl.pallas_call(
        functools.partial(attn_bwd_kernel, dims),
        grid=(own,),
        in_specs=[
            whole(tokens_in.shape),
            whole(cotangent.shape),
            per_image(seq_pad, 1),
            whole((8, width)),
            per_image(seq_pad, width),
            per_image(seq_pad, wide),
            per_image(seq_pad, width),
            per_image(seq_pad, width),
            per_image(key_pad, width),
            per_image(key_pad, width),
            per_image(pairs, 2 * seq_pad, key_pad),
            per_image(seq_pad, width),
            per_image(seq_pad, width),
            pieces(width),
            per_image(seq_pad, LANES),
            pieces(LANES),
            per_image(seq_pad, width),
            pieces(width),
            whole((1, width)),
            whole((1, width)),
            *[whole(w.shape) for w in attn_w],
            whole((width, LANES)),
        ],
        out_specs=[
            whole((tok_own, width)),
            whole((tok_own, width)),
            whole((4 * width, head_share)),
            whole((cores - 1, 4 * width, head_share)),
            whole((small_rows, width)),
        ],
        out_shape=[
            S((tok_own, width), f32),
            S((tok_own, width), f32),
            S((4 * width, head_share), f32),
            S((cores - 1, 4 * width, head_share), bf16),
            S((small_rows, width), f32),
        ],
        scratch_shapes=[pltpu.VMEM((seq_pad, width), f32)] * 2
        + [pltpu.VMEM((seq_pad, width), bf16)]
        + [pltpu.VMEM((pad_own, width), bf16)] * 6,
        compiler_params=params(),
        name="attn_bwd",
    )(
        tokens_in, cotangent, valid_col, acc_f, middle, h2x, h1, q, k, v, probs, heads,
        by_image(moe_own), by_image(moe), by_image(dots_own), by_image(dots),
        by_image(gmoe_own), by_image(gmoe), row(ln1_gain), row(ln2_gain), *attn_w, wr,
    )
    output = lax.all_gather(out_own, "tensor", axis=0, tiled=True)
    grad_input = lax.all_gather(gin_own, "tensor", axis=0, tiled=True)

    chunks = next(c for c in (4, 2, 1) if (4 * width // c // experts) % 16 == 0)
    bits = experts.bit_length() - 1
    piece_rows = small_rows // cores
    chunk_rows = 4 * width // chunks
    wqkv, grad_w_proj, small = pl.pallas_call(
        functools.partial(reduce_kernel, chunks),
        in_specs=[inside, anywhere, inside],
        out_specs=[inside] * 3,
        out_shape=[
            S((3 * width, head_share), f32),
            S((head_share, width), f32),
            S((small_rows, width), f32),
        ],
        scratch_shapes=[
            pltpu.VMEM((cores - 1, 4 * width, head_share), bf16),
            pltpu.VMEM((4 * width, head_share), f32),
            pltpu.VMEM((chunks, chunk_rows, head_share), bf16),
            pltpu.VMEM((chunks, chunk_rows, head_share), bf16),
            pltpu.VMEM((4 * width, head_share), bf16),
            pltpu.VMEM((cores - 1, piece_rows, width), f32),
            pltpu.VMEM((piece_rows, width), f32),
            pltpu.VMEM((bits, piece_rows, width), f32),
            pltpu.VMEM((bits, piece_rows, width), f32),
            DMA((cores - 1, chunks)),
            DMA((cores - 1, chunks)),
            DMA((chunks, 2 * bits)),
            DMA((chunks, 2 * bits)),
            DMA((cores - 1,)),
            DMA((cores - 1,)),
            DMA((bits,)),
            DMA((bits,)),
            DMA((cores - 1,)),
            DMA((cores - 1,)),
        ],
        compiler_params=params(collective_id=6, has_side_effects=True),
        name="reduce",
    )(grad_own, grad_rest, small)
    squares = jnp.sum(
        jnp.stack([small[small_b], small[small_b + 1], small[0], small[small_b + 2], small[1]]), -1
    )
    rms_values = jnp.sqrt(squares / (small[7, 0] * width))

    def mine(first):
        return lax.dynamic_slice(small, (first + core, 0), (1, head_share))[0]

    return (
        output,
        grad_input,
        small[5],
        small[6],
        wqkv[:width],
        wqkv[width : 2 * width],
        wqkv[2 * width :],
        mine(8),
        mine(8 + cores),
        grad_w_proj,
        small[4],
        small[2],
        small[3],
        jnp.transpose(small[small_b + 8 : small_b + 8 + experts]),
        grad_w_in,
        grad_b_in,
        grad_w_out,
        grad_b_out,
        rms_values,
    )


def solution(mesh):
    in_specs = (
        P("expert", None), P("expert", None), P("expert", None), P(), P(),
        P(None, "tensor"), P(None, "tensor"), P(None, "tensor"), P("tensor"), P("tensor"),
        P("tensor", None), P(), P(), P(), P(),
        P("expert", None, "tensor"), P("expert", "tensor"), P("expert", "tensor", None),
        P("expert", None), P("expert", None),
    )
    out_specs = (
        P("expert", None), P("expert", None), P(), P(),
        P(None, "tensor"), P(None, "tensor"), P(None, "tensor"), P("tensor"), P("tensor"),
        P("tensor", None), P(), P(), P(), P(),
        P("expert", None, "tensor"), P("expert", "tensor"), P("expert", "tensor", None),
        P("expert", None), P(),
    )
    return jax.shard_map(
        on_device, mesh=mesh, in_specs=in_specs, out_specs=out_specs, check_vma=False
    )
```

time: 1290 us -> 536 us (0.42)
  Pallas kernels: 0 us -> 439 us
  local copies, waits for them, and re-layouts: 357 us -> 38.6 us
  matrix products: 275 us -> 0 us
  waiting for transfers between devices: 247 us -> 17.3 us
  other arithmetic: 160 us -> 9.19 us
  blocking collectives: 133 us -> 0 us
  starting transfers between devices: 88.6 us -> 9.04 us
    pallas_call x0 -> x11, Pallas kernels: none -> 439 us  [the longest x1 249 us: on_device(): pl.pallas_call(moe_kernel, in_specs=[anywhere, inside, anywhere] + [insid...]
    dot_general x27 -> x0, matrix products: 275 us -> none  [the longest x1 63.6 us: on_device(): jnp.dot(expert_rows, w_in[0], preferred_element_type=f32) + b_in[0]]
    gather x7 -> x2, local copies, waits for them, and re-layouts: 158 us -> 6.71 us  [the longest x1 4.3 us: on_device(): grow = a2a(send_g[turned])]
    all_to_all x4 -> x1, waiting for transfers between devices: 151 us -> 16.8 us  [a2a(): lax.all_to_all(rows, 'expert', split_axis=0, concat_axis=0, tiled=True)]
    psum x2 -> x0, blocking collectives: 133 us -> none  [the longest x1 98.4 us: on_device(): lax.psum((grad_w_query, grad_w_key, grad_w_value, grad_b_query, grad_b_va...]
    reduce_sum x15 -> x2, other arithmetic: 100 us -> 0.94 us  [the longest x1 0.81 us: on_device(): grad_b_out = jnp.sum(gb_out[:, 0, :], 0, keepdims=True)]
    psum x4 -> x0, waiting for transfers between devices: 95.3 us -> none  [the longest x1 70.9 us: on_device(): lax.psum((grad_w_query, grad_w_key, grad_w_value, grad_b_query, grad_b_va...]
    all_to_all x4 -> x1, starting transfers between devices: 88.5 us -> 8.45 us  [a2a(): lax.all_to_all(rows, 'expert', split_axis=0, concat_axis=0, tiled=True)]
  transfers between devices with their start and end apart: 8 -> 3, of which waited for: 5 -> 1; matrix products, arithmetic and copies ran while one was open for 34% -> 6% of each run, Pallas kernels for 0% -> 20%
where the time goes in v1:
time: 536 us; the launch traced here: 528 us
  Pallas kernels  439 us (82%)
  local copies, waits for them, and re-layouts  38.6 us (7%)
  waiting for transfers between devices  17.3 us (3%)
  between operations  15.2 us (3%)
  other arithmetic  9.19 us (2%)
  starting transfers between devices  9.04 us (2%)
    pallas_call x1, Pallas kernels, on_device(): pl.pallas_call(moe_kernel, in_specs=[anywhere, inside, anywhere] + [insid...  249 us
    pallas_call x1, Pallas kernels, on_device(): pl.pallas_call(functools.partial(reduce_kernel, chunks), in_specs=[inside...  69.1 us
    pallas_call x1, Pallas kernels, on_device(): pl.pallas_call(functools.partial(attn_bwd_kernel, dims), grid=(own,), in_...  42.2 us
    pallas_call x1, Pallas kernels, on_device(): pl.pallas_call(functools.partial(attn_fwd_kernel, dims), grid=(own,), in_...  22.4 us
    pallas_call x4, Pallas kernels, swap(): pl.pallas_call(functools.partial(swap_kernel, gather, count), out_shape=o...  20.5 us
    all_to_all x1, waiting for transfers between devices, a2a(): lax.all_to_all(rows, 'expert', split_axis=0, concat_axis=0, tiled=True)  16.8 us
    pallas_call x1, Pallas kernels, on_device(): pl.pallas_call(functools.partial(combine_kernel, cap_dev, True), out_shap...  13.5 us
    pallas_call x1, Pallas kernels, on_device(): pl.pallas_call(functools.partial(prep_kernel, (images, seq, seq_pad, expe...  13.1 us
  transfers between devices with their start and end apart: 3, of which 1 were waited for; matrix products, arithmetic and copies ran while one was open for 6% of the time, Pallas kernels for 20%

profile of v1, /device:TPU:0, one launch (start us, length us, event | category | flops | bytes accessed | tf_op | source)
XLA Modules:
  0.0 528.0 jit_solution(1932443444245158134)
XLA Ops:
  7.2 0.8 reshape.215
  8.0 0.3 copy.48
  8.3 1.0 pad.19
  9.3 13.1 %prep.1 = (bf16[16,128,768]{2,1,0:T(8,128)(2,1)}, f32[2,16,1,832]{3,2,1,0:T(1,128)}, s32[1664,2]{1,0:T(8,128)}) custom-call(s32[1664,2]{1,0:T(8,128)} %bitcast.47, f32[1576,768]{1,0:T(8,128)} %cot_ref.3), custom_call_target="tpu_custom_call" | custom-call | tf_op jit(solution)/shard_map/prep/pallas_call | solution.py:910
  22.4 4.3 gather_fusion
  26.7 0.0 copy-start.17
  26.7 0.0 copy-start.12
  26.7 0.0 copy-start.13
  26.8 0.0 copy-start.14
  26.8 0.0 copy-start.5
  26.8 8.5 %all-to-all-start = ((bf16[16,128,768]{2,1,0:T(8,128)(2,1)}), bf16[16,128,768]{2,1,0:T(8,128)(2,1)S(1)}, u32[]{:S(2)}, u32[]{:S(2)}) async-start(bf16[16,128,768]{2,1,0:T(8,128)(2,1)} %gather_fusion), calls=%async_computation | async-start | bytes 6291456 | tf_op jit(solution)/shard_map/all_to_all | solution.py:905
  35.2 0.3 all-gather.5.cloned.1.call-start
  35.6 0.0 copy-done.15
  35.6 1.0 copy.49.valid_ref
  36.6 0.6 broadcast_in_dim.28.mask_ref
  37.2 0.0 copy-done.10
  37.2 0.6 reshape.207.g1_ref
  37.8 0.0 copy-done.11
  37.8 0.6 reshape.208.b1_ref
  38.4 0.0 copy-done.16
  38.4 0.6 reshape.209.refs_4_
  38.9 0.0 copy-done.17
  38.9 0.6 reshape.210.refs_5_
  39.5 0.0 copy-done.12
  39.5 0.6 reshape.211.bp_ref
  40.1 0.0 copy-done.13
  40.1 0.6 reshape.212.g2_ref
  40.7 0.6 reshape.213.b2_ref
  41.2 0.2 copy.46
  41.4 0.7 pad.18.wr_ref
  42.2 8.4 %swap7.1 = (bf16[1,768,1536]{2,1,0:T(8,128)(2,1)}, bf16[1,1536,768]{2,1,0:T(8,128)(2,1)}, f32[1,1,1536]{2,1,0:T(1,128)}) custom-call(bf16[768,1536]{1,0:T(8,128)(2,1)} %bitcast.41, bf16[1536,768]{1,0:T(8,128)(2,1)} %bitcast.43, f32[1,1536]{1,0:T(1,128)} %b_in.1), custom_call_target="tpu_custom_call" | custom-call | tf_op jit(solution)/shard_map/swap7/pallas_call | solution.py:694
  50.5 5.1 swap1.1
  55.7 1.3 pad_maximum_fusion
  57.0 22.4 %attn_fwd.1 = (bf16[4,208,768]{2,1,0:T(8,128)(2,1)}, bf16[4,208,768]{2,1,0:T(8,128)(2,1)}, bf16[4,256,768]{2,1,0:T(8,128)(2,1)}, bf16[4,256,768]{2,1,0:T(8,128)(...) custom-call(f32[1576,768]{1,0:T(8,128)} %tok_ref.3, ...), custom_call_target="tpu_custom_call" | custom-call | flops 4580179968 | bytes 25165824 | tf_op jit(solution)/shard_map/attn_fwd/pallas_call | solution.py:947
  79.4 16.8 %all-to-all-done = bf16[16,128,768]{2,1,0:T(8,128)(2,1)S(1)} async-done(((bf16[16,128,768]{2,1,0:T(8,128)(2,1)}), bf16[16,128,768]{2,1,0:T(8,128)(2,1)S(1)}, u32[]{:S(2)}, u32[]{:S(2)}) %all-to-all-start) | async-done | bytes 3145760 | tf_op jit(solution)/shard_map/all_to_all | solution.py:905
  96.2 2.4 gather_fusion.1
  98.6 248.6 %moe.1 = (bf16[16,128,768]{2,1,0:T(8,128)(2,1)}, bf16[16,128,768]{2,1,0:T(8,128)(2,1)}, f32[2048,1]{1,0:T(8,128)}, bf16[768,1536]{1,0:T(8,128)(2,1)}, bf16[1536,...) custom-call(bf16[832,896]{1,0:T(8,128)(2,1)} %bitcast.45, ...), custom_call_target="tpu_custom_call" | custom-call | tf_op jit(solution)/shard_map/moe/pallas_call | solution.py:1007
  347.2 9.3 %combine_grad.1 = (bf16[832,768]{1,0:T(8,128)(2,1)}, bf16[1,832,768]{2,1,0:T(8,128)(2,1)}) custom-call(bf16[2048,768]{1,0:T(8,128)(2,1)} %bitcast.48, f32[2048,1]{1,0:T(8,128)} %get-tuple-element.87.gslot_ref, s32[1664,2]{1,0:T(8,128)} %get-tuple-element.88.fidx_ref), custom_call_target="tpu_custom_call" | custom-call | tf_op jit(solution)/shard_map/combine_grad/pallas_call | solution.py:1072
  356.5 3.4 swap5.1
  359.9 13.5 %combine_res.1 = (bf16[832,768]{1,0:T(8,128)(2,1)}, bf16[1,832,768]{2,1,0:T(8,128)(2,1)}, bf16[832,128]{1,0:T(8,128)(2,1)}, bf16[1,832,128]{2,1,0:T(8,128)(2,1)}) custom-call(bf16[2048,768]{1,0:T(8,128)(2,1)} %bitcast.49, f32[2048,1]{1,0:T(8,128)} %get-tuple-element.87.gslot_ref, s32[1664,2]{1,0:T(8,128)} %get-tuple-element.88.fidx_ref, ...), custom_call_target="tpu_custom_call" | custom-call | tf_op jit(solution)/shard_map/combine_res/pallas_call | solution.py:1059
  373.4 3.7 swap4.1
  377.1 42.2 %attn_bwd.1 = (f32[788,768]{1,0:T(8,128)}, f32[788,768]{1,0:T(8,128)}, f32[3072,384]{1,0:T(8,128)}, bf16[1,3072,384]{2,1,0:T(8,128)(2,1)}, f32[48,768]{1,0:T(8,128)}) custom-call(f32[1576,768]{1,0:T(8,128)} %tok_ref.3, f32[1576,768]{1,0:T(8,128)} %cot_ref.3, f32[4,208,1]{2,1,0:T(8,128)} %copy.49.valid_ref, f32[8,768]{1,0:T(8,128)} %get-tuple-element.72.accf_ref, ...), custom_call_target="tpu_custom_call" | custom-call | tf_op jit(solution)/shard_map/attn_bwd/pallas_call | solution.py:1090
  419.3 0.0 all-gather.5.cloned.1.call-update
  419.3 0.3 all-gather.7.cloned.1.call-start
  419.6 0.5 all-gather.7.cloned.1.call-update
  420.0 69.1 %reduce.16 = (f32[2304,384]{1,0:T(8,128)}, f32[384,768]{1,0:T(8,128)}, f32[48,768]{1,0:T(8,128)}) custom-call(f32[3072,384]{1,0:T(8,128)} %get-tuple-element.100.own_ref, bf16[1,3072,384]{2,1,0:T(8,128)(2,1)} %get-tuple-element.101.rest_ref, f32[48,768]{1,0:T(8,128)} %get-tuple-element.102.small_ref), custom_call_target="tpu_custom_call" | custom-call | tf_op jit(solution)/shard_map/reduce/pallas_call | solution.py:1148
  489.2 0.7 slice.57
  489.9 1.2 slice.61
  491.1 0.8 slice_reduce_fusion
  491.9 0.6 broadcast_in_dim.31
  493.2 1.4 dynamic-slice_reduce_fusion
  494.6 1.6 slice_reduce_fusion.1
  496.2 0.1 maximum_reduce_fusion
  496.3 0.5 divide_sqrt_fusion
  496.9 1.4 slice_bitcast_fusion
  498.3 4.0 fusion.8
  502.3 0.6 bitcast_add_fusion
  502.9 0.0 copy-done.3
  502.9 3.1 fusion.1
  506.0 1.0 copy-done.1
  507.0 2.7 fusion
  509.7 5.1 reshape.245
  514.8 5.2 reshape.247
  519.9 1.0 copy.51
  (31 shorter events, 0.1 us)
Async XLA Ops:
  26.7 8.9 %copy-start.15 = (s32[8,197]{1,0:T(8,128)S(1)}, s32[8,197]{1,0:T(8,128)}, u32[]{:S(2)}) copy-start(s32[8,197]{1,0:T(8,128)} %param.21) | copy-start | bytes 18916
  26.7 10.5 %copy-start.10 = (f32[768]{0:T(1024)S(1)}, f32[768]{0:T(1024)}, u32[]{:S(2)}) copy-start(f32[768]{0:T(1024)} %param.23) | copy-start | bytes 9220
  26.7 11.1 %copy-start.11 = (f32[768]{0:T(1024)S(1)}, f32[768]{0:T(1024)}, u32[]{:S(2)}) copy-start(f32[768]{0:T(1024)} %param.24) | copy-start | bytes 9220
  26.7 11.7 %copy-start.16 = (f32[384]{0:T(512)S(1)}, f32[384]{0:T(512)}, u32[]{:S(2)}) copy-start(f32[384]{0:T(512)} %param.28) | copy-start | bytes 4612
  26.7 12.2 %copy-start.17 = (f32[384]{0:T(512)S(1)}, f32[384]{0:T(512)}, u32[]{:S(2)}) copy-start(f32[384]{0:T(512)} %param.29) | copy-start | bytes 4612
  26.7 12.8 %copy-start.12 = (f32[768]{0:T(1024)S(1)}, f32[768]{0:T(1024)}, u32[]{:S(2)}) copy-start(f32[768]{0:T(1024)} %param.31) | copy-start | bytes 9220
  26.7 13.3 %copy-start.13 = (f32[768]{0:T(1024)S(1)}, f32[768]{0:T(1024)}, u32[]{:S(2)}) copy-start(f32[768]{0:T(1024)} %param.32) | copy-start | bytes 9220
  26.8 13.9 %copy-start.14 = (f32[768]{0:T(1024)S(1)}, f32[768]{0:T(1024)}, u32[]{:S(2)}) copy-start(f32[768]{0:T(1024)} %param.33) | copy-start | bytes 9220
  26.8 14.5 %copy-start.5 = (bf16[768,16]{0,1:T(8,128)(2,1)S(1)}, bf16[768,16]{0,1:T(8,128)(2,1)}, u32[]{:S(2)}) copy-start(bf16[768,16]{0,1:T(8,128)(2,1)} %param.34) | copy-start | bytes 73732
  26.8 69.4 %all-to-all-start = ((bf16[16,128,768]{2,1,0:T(8,128)(2,1)}), bf16[16,128,768]{2,1,0:T(8,128)(2,1)S(1)}, u32[]{:S(2)}, u32[]{:S(2)}) async-start(bf16[16,128,768]{2,1,0:T(8,128)(2,1)} %gather_fusion), calls=%async_computation | async-start | bytes 6291456 | tf_op jit(solution)/shard_map/all_to_all | solution.py:905
  35.2 474.5 %all-gather.5.cloned.1.call-start = ((), (), s32[]{:S(2)}) async-start(), calls=%async_computation.1 | async-start | bytes 7299072 | tf_op jit(solution)/shard_map/all_gather | solution.py:1141
  42.2 13.5 %copy-start.6 = (f32[1,384]{1,0:T(1,128)S(1)}, f32[1,384]{1,0:T(1,128)}, u32[]{:S(2)}) copy-start(f32[1,384]{1,0:T(1,128)} %reshape.209.refs_4_) | copy-start | bytes 4612
  42.2 13.5 %copy-start.7 = (f32[1,384]{1,0:T(1,128)S(1)}, f32[1,384]{1,0:T(1,128)}, u32[]{:S(2)}) copy-start(f32[1,384]{1,0:T(1,128)} %reshape.210.refs_5_) | copy-start | bytes 4612
  419.3 95.5 %all-gather.7.cloned.1.call-start = ((), (), s32[]{:S(2)}) async-start(), calls=%async_computation.2 | async-start | bytes 7299072 | tf_op jit(solution)/shard_map/all_gather | solution.py:1142
  498.3 4.0 copy-start.8
  498.3 4.0 copy-start.9
  498.3 4.6 copy-start.2
  498.3 4.6 copy-start.3
  502.9 3.1 copy-start
  502.9 4.1 copy-start.1
  514.8 5.2 copy-start.4
Sparse Core Ops, SparseCore 0:
  419.4 11.8 all-gather.4
  432.8 14.5 all-gather.6

commit v2 on v1

--- a/solution.py
+++ b/solution.py
@@ -27,7 +27,7 @@
 
 
 def whole(shape):
-    return pl.BlockSpec(shape, lambda *_: (0,) * len(shape))
+    return pl.BlockSpec(shape, lambda *_: (0,) * len(shape), pipeline_mode=pl.Buffered(1))
 
 
 def dot(a, b):
@@ -128,42 +128,6 @@
         grow_ref[e] = total.astype(bf16)
 
 
-def combine_kernel(cap_dev, with_dots, rows_ref, gslot_ref, fidx_ref, *rest):
-    if with_dots:
-        grow_ref, own_ref, out_ref, own_dots_ref, dots_ref, scaled, spread = rest
-    else:
-        own_ref, out_ref, scaled = rest
-    rows_all = rows_ref.shape[0]
-    tile = LANES
-    lanes = lane_iota((tile, LANES))
-    for i in range(rows_all // tile):
-        here = slice(tile * i, tile * (i + 1))
-        rows = rows_ref[here, :].astype(f32)
-        scaled[here, :] = (rows * gslot_ref[here, :]).astype(bf16)
-        if with_dots:
-            dots = jnp.sum(rows * grow_ref[here, :].astype(f32), 1, keepdims=True)
-            owner = (lax.broadcasted_iota(i32, (tile, LANES), 0) + tile * i) // cap_dev
-            owner = lax.rem(owner + lax.axis_index("expert"), lax.axis_size("expert"))
-            spread[here, :] = jnp.where(lanes == owner, dots, 0.0).astype(bf16)
-    group = own_ref.shape[0]
-    n = out_ref.shape[0] + 1
-    me = lax.axis_index("tensor")
-    step = 208 if group % 208 == 0 else group
-    lanes = lane_iota((step, rows_all))
-    for k in range(n):
-        base = lax.rem(me + k, n) * group
-        for i in range(group // step):
-            tok = pl.ds(pl.multiple_of(base + i * step, 16), step)
-            hit = (fidx_ref[tok, 0:1] == lanes) | (fidx_ref[tok, 1:2] == lanes)
-            pick = jnp.where(hit, 1.0, 0.0).astype(bf16)
-            to = slice(i * step, (i + 1) * step)
-            (own_ref if k == 0 else out_ref.at[k - 1])[to, :] = dot(pick, scaled[...]).astype(bf16)
-            if with_dots:
-                (own_dots_ref if k == 0 else dots_ref.at[k - 1])[to, :] = dot(
-                    pick, spread[...]
-                ).astype(bf16)
-
-
 def piece(own_ref, rest_ref, j):
     return own_ref[...] if j == 0 else rest_ref[j - 1]
 
@@ -174,14 +138,6 @@
         @pl.when(image == n)
         def _(n=n):
             dst[0:seq, :] = src[seq * n : seq * (n + 1), :]
-
-
-def write_image(dst, value, image, seq):
-    for n in range(dst.shape[0] // seq):
-
-        @pl.when(image == n)
-        def _(n=n):
-            dst[seq * n : seq * (n + 1), :] = value[:seq]
 
 
 def attn_fwd_kernel(
@@ -245,9 +201,9 @@
 
 def attn_bwd_kernel(
     dims, tok_ref, cot_ref, valid_ref, accf_ref, mid_ref, h2x_ref, h1_ref, q_ref, k_ref, v_ref, probs_ref,
-    heads_ref, moe_own, moe_ref, dots_own, dots_ref, gmoe_own, gmoe_ref, g1_ref, g2_ref,
+    heads_ref, moe_own, moe_ref, gmoe_own, gmoe_ref, gin_w, gin_ws, gout_w, gout_ws, g1_ref, g2_ref,
     wq, wqs, wk, wks, wv, wvs, wp, wps, wr_ref,
-    out_ref, gin_ref, grad_own, grad_rest, acc_ref,
+    out_ref, gin_ref, grad_own, grad_rest, acc_ref, gw_in_ref, gw_out_ref,
     x_s, c_s, gh_s, h1_s, heads_s, ga_s, dq_s, dk_s, dv_s
 ):
     seq, seq_pad, key_pad, own, experts = dims
@@ -272,16 +228,24 @@
     def add(row, value):
         acc_ref[row : row + 1, :] += jnp.sum(value, 0, keepdims=True)
 
-    def total(own_ref, rest_ref):
-        value = own_ref[0].astype(f32)
+    def total(own_ref, rest_ref, cols):
+        value = own_ref[0, :, cols].astype(f32)
         for j in range(rest_ref.shape[0]):
-            value = value + rest_ref[j, 0].astype(f32)
+            value = value + rest_ref[j, 0, :, cols].astype(f32)
         return value
 
+    for sum_ref, own_ref, rest_ref in (
+        (gw_in_ref, gin_w, gin_ws), (gw_out_ref, gout_w, gout_ws)
+    ):
+        value = own_ref[...].astype(f32)
+        for j in range(rest_ref.shape[0]):
+            value = value + rest_ref[j].astype(f32)
+        sum_ref[0] = value
+
     middle = mid_ref[0]
-    moe = total(moe_own, moe_ref)
+    moe = total(moe_own, moe_ref, slice(0, width))
     output = middle + moe
-    write_image(out_ref, output, step, seq)
+    out_ref[0] = output
     add(0, ok * output * output)
     add(1, ok * moe * moe)
     h2 = h2x_ref[0, :, 0:width]
@@ -289,12 +253,12 @@
     prob = jnp.where(
         lane_iota(pair.shape) < experts, pair + pltpu.roll(pair, LANES - experts, 1), 0.0
     )
-    grad_probs = total(dots_own, dots_ref)
+    grad_probs = total(moe_own, moe_ref, slice(width, width + LANES))
     grad_logits = (
         prob * (grad_probs - jnp.sum(grad_probs * prob, -1, keepdims=True))
     ).astype(bf16)
     acc_ref[small_b + 8 : small_b + 8 + experts, :] += dot_tn(grad_logits, h2)[:experts]
-    grad_h2 = dot_nt(grad_logits, wr_ref[...]) + total(gmoe_own, gmoe_ref)
+    grad_h2 = dot_nt(grad_logits, wr_ref[...]) + total(gmoe_own, gmoe_ref, slice(0, width))
     normed2, inv2 = norm_parts(middle)
     add(2, grad_h2 * normed2)
     add(3, grad_h2)
@@ -350,7 +314,7 @@
     add(6, grad_h1)
     add(7, jnp.broadcast_to(ok, grad_h1.shape))
     grad_in = c_s[...] + norm_back(grad_h1, normed1, inv1, g1_ref[...])
-    write_image(gin_ref, grad_in, step, seq)
+    gin_ref[0] = grad_in
 
     @pl.when(step == own - 1)
     def _():
@@ -392,12 +356,13 @@
 
 
 def moe_kernel(
-    h2x_ref, post_ref, grow_hbm, w_in, w_ins, b_in, b_ins, w_out, w_outs, b_out_ref,
-    back_ref, gback_ref, gslot_ref, gin_own, gout_own, gin_rest, gout_rest,
-    gbin_own, gbin_rest, gbout_ref,
-    table, out_s, rows_s, hid, slope, grow_s, res_s, gate_out, gate_in, stage_in, stage_out,
+    h2x_ref, post_ref, grow_hbm, sent_hbm, fidx_ref, w_in, w_ins, b_in, b_ins, w_out, w_outs,
+    b_out_ref,
+    back_ref, gback_ref, gin_own, gout_own, gin_rest, gout_rest,
+    gbin_own, gbin_rest, gbout_ref, moe_own, moe_rest, gmoe_own, gmoe_rest,
+    table, out_s, rows_s, grow_s, res_s, gate_out, gate_in, gslot_ref,
     gbin_send, gbout_send,
-    local_sem, tab_send, tab_recv, h_send, h_recv, c_send, c_recv, r_send, r_recv, g_send, g_recv,
+    m_send, m_recv, load_sem, local_sem, tab_send, tab_recv, h_send, h_recv, c_send, c_recv, r_send, r_recv, g_send, g_recv,
     w_send, w_recv, own_sem
 ):
     experts, chip = around("expert")
@@ -459,18 +424,196 @@
     def g_copy(k):
         return remote(out_s.at[k], gback_ref.at[k], g_send.at[k], g_recv.at[k], chip(-k))
 
-    def send_rows(k, _):
+    def far(j):
+        return lax.rem(j + experts // 2, experts)
+
+    def send_rows(j, _):
+        k = far(j)
         rows, gate = select(k)
         out_s[k] = rows
         gate_out[k] = gate
-        h_copy(k).start()
-        c_copy(k).start()
+
+        @pl.when(k > 0)
+        def _():
+            h_copy(k).start()
+            c_copy(k).start()
+
         return 0
 
-    lax.fori_loop(1, experts, send_rows, 0)
-    rows, gate = select(0)
-    rows_s[0] = rows
-    gate_in[0] = gate
+    lax.fori_loop(0, experts, send_rows, 0)
+    rows_s[0] = out_s[0]
+    gate_in[0] = gate_out[0]
+    pl.run_scoped(
+        functools.partial(
+            expert_phase, locals_of(
+                experts=experts, cores=cores, core=core, me_t=me_t, width=width, cap_dev=cap_dev,
+                share=share, size=size, per=per, w_in=w_in, w_ins=w_ins, b_in=b_in, b_ins=b_ins,
+                w_out=w_out, w_outs=w_outs, b_out_ref=b_out_ref, rows_s=rows_s, res_s=res_s,
+                back_ref=back_ref, own_sem=own_sem, h_copy=h_copy, r_copy=r_copy, c_copy=c_copy,
+                g_copy=g_copy, grow_copy=grow_copy, grow_s=grow_s, out_s=out_s,
+                gback_ref=gback_ref, gate_in=gate_in, gbout_send=gbout_send, gbout_ref=gbout_ref,
+                gbin_own=gbin_own, gbin_send=gbin_send, gbin_rest=gbin_rest, gin_own=gin_own,
+                gout_own=gout_own, gin_rest=gin_rest, gout_rest=gout_rest, w_send=w_send,
+                w_recv=w_recv, remote=remote, far=far,
+            ),
+        ),
+        pltpu.VMEM((experts * cap_dev, share * cores), bf16),
+        pltpu.VMEM((experts * cap_dev, share * cores), bf16),
+        pltpu.VMEM((2, width, size), bf16),
+        pltpu.VMEM((2, size, width), bf16),
+    )
+    rows_all = experts * cap_dev
+    wide = width + LANES
+
+    def token_phase(picks, values, total):
+        loads = [
+            pltpu.make_async_copy(sent_hbm, grow_s, load_sem.at[0]),
+            pltpu.make_async_copy(back_ref, rows_s, load_sem.at[1]),
+        ]
+        loads[0].start()
+
+        def arrived(k, _):
+            r_copy(k).wait()
+            return 0
+
+        lax.fori_loop(1, experts, arrived, 0)
+        loads[1].start()
+        step = 208 if group % 208 == 0 else group
+        tiles = group // step
+        slot_lanes = lane_iota((step, rows_all))
+
+        def make_picks(i, _):
+            tok = pl.ds(pl.multiple_of(i * step, 16), step)
+            hit = (fidx_ref[tok, 0:1] == slot_lanes) | (fidx_ref[tok, 1:2] == slot_lanes)
+            picks[tok, :] = jnp.where(hit, 1.0, 0.0).astype(bf16)
+            return 0
+
+        lax.fori_loop(0, cores * tiles, make_picks, 0)
+        for copy in loads:
+            copy.wait()
+
+        def gated(k):
+            return gslot_ref[pl.ds(pl.multiple_of(cap_dev * k, 8), cap_dev), :]
+
+        def weigh(k, _):
+            rows = rows_s[k].astype(f32)
+            dots = jnp.sum(rows * grow_s[k].astype(f32), 1, keepdims=True)
+            here = pl.ds(pl.multiple_of(cap_dev * k, 16), cap_dev)
+            values[here, 0:width] = (rows * gated(k)).astype(bf16)
+            mine = lanes == lax.rem(me_e + k, experts)
+            values[here, width:] = jnp.where(mine, dots, 0.0).astype(bf16)
+            return 0
+
+        lax.fori_loop(0, experts, weigh, 0)
+
+        def m_copy(kind, k):
+            source = table.at[k] if kind == 0 else table.at[k, :, 0:width]
+            return remote(
+                source, (moe_rest, gmoe_rest)[kind].at[k - 1],
+                m_send.at[kind, k - 1], m_recv.at[kind, k - 1], core(k),
+            )
+
+        keep_moe = pltpu.make_async_copy(table.at[0], moe_own, load_sem.at[0])
+        keep_gmoe = pltpu.make_async_copy(table.at[0, :, 0:width], gmoe_own, load_sem.at[0])
+
+        for k in list(range(1, cores)) + [0]:
+
+            def sums(i, _, k=k):
+                tok = pl.ds(
+                    pl.multiple_of(lax.rem(me_t + k, cores) * group + i * step, 16), step
+                )
+                to = pl.ds(pl.multiple_of(i * step, 16), step)
+                table[k, to, :] = dot(picks[tok, :], values[...]).astype(bf16)
+                return 0
+
+            lax.fori_loop(0, tiles, sums, 0)
+            if k > 0:
+                m_copy(0, k).start()
+        keep_moe.start()
+        keep_moe.wait()
+        for k in range(1, cores):
+            m_copy(0, k).wait()
+
+        batch = 4
+        batches = experts // batch
+        for b in range(batches):
+            first = (b * batch + experts // 2) % experts
+            for k in range(first, first + batch):
+                if k > 0:
+                    g_copy(k).wait_recv()
+                else:
+                    own_grad.wait()
+            box = pl.ds(first, batch)
+            load = pltpu.make_async_copy(gback_ref.at[box], rows_s.at[box], load_sem.at[0])
+            load.start()
+            load.wait()
+            cols = slice(cap_dev * first, cap_dev * (first + batch))
+            for k in range(first, first + batch):
+                rows_s[k] = (rows_s[k].astype(f32) * gated(k)).astype(bf16)
+            for k in list(range(1, cores)) + [0]:
+
+                def gsums(i, _, k=k, b=b, cols=cols, box=box):
+                    tok = pl.ds(
+                        pl.multiple_of(lax.rem(me_t + k, cores) * group + i * step, 16), step
+                    )
+                    to = pl.ds(pl.multiple_of(i * step, 16), step)
+                    rows = rows_s[box].reshape(batch * cap_dev, width)
+                    value = dot(picks[tok, cols], rows)
+                    if b > 0:
+                        value = value + total[tok, :]
+                    if b < batches - 1:
+                        total[tok, :] = value
+                    else:
+                        table[k, to, 0:width] = value.astype(bf16)
+                    return 0
+
+                lax.fori_loop(0, tiles, gsums, 0)
+                if b == batches - 1 and k > 0:
+                    m_copy(1, k).start()
+        keep_gmoe.start()
+        keep_gmoe.wait()
+        for k in range(1, cores):
+            m_copy(1, k).wait()
+
+        def finish(k, _):
+            g_copy(k).wait_send()
+            return 0
+
+        lax.fori_loop(1, experts, finish, 0)
+
+    own_grad = pltpu.make_async_copy(out_s.at[0], gback_ref.at[0], own_sem.at[1])
+    pl.run_scoped(
+        token_phase,
+        pltpu.VMEM((cores * group, rows_all), bf16),
+        pltpu.VMEM((rows_all, wide), bf16),
+        pltpu.VMEM((cores * group, width), f32),
+    )
+
+
+class Bag:
+    pass
+
+
+def locals_of(**names):
+    bag = Bag()
+    bag.__dict__.update(names)
+    return bag
+
+
+def expert_phase(at, hid, slope, stage_in, stage_out):
+    experts, cores, core, me_t, width, cap_dev = (
+        at.experts, at.cores, at.core, at.me_t, at.width, at.cap_dev
+    )
+    share, size, per, far, remote = at.share, at.size, at.per, at.far, at.remote
+    w_in, w_ins, b_in, b_ins, w_out, w_outs = at.w_in, at.w_ins, at.b_in, at.b_ins, at.w_out, at.w_outs
+    b_out_ref, rows_s, res_s, back_ref, own_sem = at.b_out_ref, at.rows_s, at.res_s, at.back_ref, at.own_sem
+    h_copy, r_copy, c_copy, g_copy, grow_copy = at.h_copy, at.r_copy, at.c_copy, at.g_copy, at.grow_copy
+    grow_s, out_s, gback_ref, gate_in = at.grow_s, at.out_s, at.gback_ref, at.gate_in
+    gbout_send, gbout_ref, gbin_own, gbin_send, gbin_rest = (
+        at.gbout_send, at.gbout_ref, at.gbin_own, at.gbin_send, at.gbin_rest
+    )
+    gin_own, gout_own, gin_rest, gout_rest = at.gin_own, at.gout_own, at.gin_rest, at.gout_rest
+    w_send, w_recv = at.w_send, at.w_recv
 
     def forward(i):
         x = rows_s[pl.ds(2 * i, 2)].reshape(2 * cap_dev, width)
@@ -490,21 +633,30 @@
         res = (total + b_out_ref[...]).astype(bf16)
         res_s[pl.ds(2 * i, 2)] = res.reshape(2, cap_dev, width)
 
-    h_copy(1).wait_recv()
-    forward(0)
     own_res = pltpu.make_async_copy(res_s.at[0], back_ref.at[0], own_sem.at[0])
-    own_res.start()
-    r_copy(1).start()
-
-    def forward_step(i, _):
-        h_copy(2 * i).wait_recv()
+
+    def forward_step(j, _):
+        i = lax.rem(j + experts // 4, experts // 2)
+
+        @pl.when(i > 0)
+        def _():
+            h_copy(2 * i).wait_recv()
+
         h_copy(2 * i + 1).wait_recv()
         forward(i)
-        r_copy(2 * i).start()
+
+        @pl.when(i > 0)
+        def _():
+            r_copy(2 * i).start()
+
+        @pl.when(i == 0)
+        def _():
+            own_res.start()
+
         r_copy(2 * i + 1).start()
         return 0
 
-    lax.fori_loop(1, experts // 2, forward_step, 0)
+    lax.fori_loop(0, experts // 2, forward_step, 0)
 
     def sent_rows(k, _):
         h_copy(k).wait_send()
@@ -528,18 +680,24 @@
                 total = term if total is None else total + term
         out_s[pl.ds(2 * i, 2)] = total.astype(bf16).reshape(2, cap_dev, width)
 
-    backward(0)
     own_grad = pltpu.make_async_copy(out_s.at[0], gback_ref.at[0], own_sem.at[1])
-    own_grad.start()
-    g_copy(1).start()
-
-    def backward_step(i, _):
+
+    def backward_step(j, _):
+        i = lax.rem(j + experts // 4, experts // 2)
         backward(i)
-        g_copy(2 * i).start()
+
+        @pl.when(i > 0)
+        def _():
+            g_copy(2 * i).start()
+
+        @pl.when(i == 0)
+        def _():
+            own_grad.start()
+
         g_copy(2 * i + 1).start()
         return 0
 
-    lax.fori_loop(1, experts // 2, backward_step, 0)
+    lax.fori_loop(0, experts // 2, backward_step, 0)
 
     def gates_in(k, _):
         c_copy(k).wait()
@@ -645,14 +803,7 @@
             gbout_send, gbout_ref.at[me_t], w_send.at[3, j - 1], w_recv.at[3, j - 1], core(j)
         ).wait()
 
-    def finish(k, _):
-        r_copy(k).wait()
-        g_copy(k).wait()
-        return 0
-
-    lax.fori_loop(1, experts, finish, 0)
     own_res.wait()
-    own_grad.wait()
 
 
 def swap_kernel(gather, count, *refs):
@@ -703,9 +854,10 @@
 
 
 def reduce_kernel(
-    chunks, own_ref, rest_ref, small_ref, wqkv_ref, wproj_ref, small_out,
-    rest_s, acc, send_s, recv_s, low, small_r, small_m, small_s, small_t,
-    t_send, t_recv, x_send, x_recv, st_send, st_recv, sx_send, sx_recv, sg_send, sg_recv
+    chunks, own_ref, rest_ref, small_ref, out_ref, gin_ref, low, small_out, outs_ref, gins_ref,
+    rest_s, acc, send_s, recv_s, small_r, small_m, small_s, small_t,
+    t_send, t_recv, x_send, x_recv, st_send, st_recv, sx_send, sx_recv, sg_send, sg_recv,
+    o_send, o_recv
 ):
     experts, _ = around("expert")
     cores, core = around("tensor")
@@ -752,6 +904,14 @@
     for group in first:
         for copy in group:
             copy.start()
+
+    tokens = [
+        remote(src, dst.at[k - 1], o_send.at[n, k - 1], o_recv.at[n, k - 1], core(k))
+        for k in range(1, cores)
+        for n, (src, dst) in enumerate(((gin_ref, gins_ref), (out_ref, outs_ref)))
+    ]
+    for copy in tokens:
+        copy.start()
 
     def gather_chunk(c):
         here = slice(rows * c, rows * (c + 1))
@@ -809,18 +969,6 @@
             b = orders[c][2 * bits - 1 - s]
             size = rows >> (2 * bits - s)
             base[c] = base[c] - my_bit(b) * size
-            if s == 2 * bits - 1:
-                width = rows_all // 4
-                here = slice(rows * c, rows * (c + 1))
-                if rows * (c + 1) <= 3 * width:
-                    wqkv_ref[here, :] = low[here, :].astype(f32)
-                else:
-                    top = min(max(rows * c, 3 * width), rows * (c + 1))
-                    if top > rows * c:
-                        wqkv_ref[rows * c : top, :] = low[rows * c : top, :].astype(f32)
-                    wproj_ref[:, top - 3 * width : rows * (c + 1) - 3 * width] = jnp.transpose(
-                        low[top : rows * (c + 1), :].astype(f32), (1, 0)
-                    )
 
     def small_start(s):
         small_s[s] = small_m[...]
@@ -870,8 +1018,76 @@
                 ]
                 for copy in lasts:
                     copy.start()
-    for copy in lasts:
+    for copy in lasts + tokens:
         copy.wait()
+
+
+def finish_kernel(
+    seq, low_ref, small_ref, gbin_own, gbin_rest, gbout_ref, out_own, out_rest, gin_own, gin_rest,
+    out_hbm, gin_hbm, gl1, bl1, gq, gk, gv, gbq, gbv, gwp, gbp, gl2, bl2, grout, gbin, gbout, rms,
+    out_s, gin_s, in_sem, to_sem
+):
+    cores, own, seq_pad, width = (out_rest.shape[0] + 1,) + out_rest.shape[1:]
+    me_t = lax.axis_index("tensor")
+    images = cores * own
+    share = gbq.shape[0]
+    experts = grout.shape[1]
+    jobs = []
+    for n, (mine, rest, full, hbm) in enumerate(
+        ((out_own, out_rest, out_s, out_hbm), (gin_own, gin_rest, gin_s, gin_hbm))
+    ):
+        jobs.append((n, mine, rest, full, hbm))
+    rows_all = images * seq
+
+    def place(c):
+        for n, mine, rest, full, hbm in jobs:
+            done = 0
+            for im in range(images):
+                p = (im // own - c) % cores
+                src = mine.at[im % own] if p == 0 else rest.at[p - 1, im % own]
+                full[seq * im : seq * (im + 1), :] = src[0:seq, :]
+                upto = rows_all if im == images - 1 else seq * (im + 1) // 8 * 8
+                pltpu.make_async_copy(
+                    full.at[done:upto, :], hbm.at[done:upto, :], to_sem.at[n, im]
+                ).start()
+                done = upto
+
+    for c in range(cores):
+
+        @pl.when(me_t == c)
+        def _(c=c):
+            place(c)
+
+    for n, grad in enumerate((gq, gk, gv)):
+        grad[...] = low_ref[width * n : width * (n + 1), :].astype(f32)
+    gwp[...] = jnp.transpose(low_ref[3 * width : 4 * width, :].astype(f32), (1, 0))
+    base = small_base(cores)
+    for dst, row in ((gl1, 5), (bl1, 6), (gbp, 4), (gl2, 2), (bl2, 3)):
+        dst[...] = small_ref[row]
+    which = lax.broadcasted_iota(i32, (base, share), 0)
+    for dst, row in ((gbq, 8), (gbv, 8 + cores)):
+        dst[...] = jnp.sum(jnp.where(which == row + me_t, small_ref[0:base, 0:share], 0.0), 0)
+    grout[...] = jnp.transpose(small_ref[base + 8 : base + 8 + up(experts, 8), :], (1, 0))[:, :experts]
+    value = gbin_own[...]
+    for k in range(cores - 1):
+        value = value + gbin_rest[k]
+    gbin[...] = value
+    value = gbout_ref[0, 0:1, :]
+    for k in range(1, cores):
+        value = value + gbout_ref[k, 0:1, :]
+    gbout[...] = value
+    count = small_ref[7:8, :] * width
+    for n, row in enumerate((base, base + 1, 0, base + 2, 1)):
+        square = jnp.sum(small_ref[row : row + 1, :], 1, keepdims=True)
+        rms[n : n + 1, :] = jnp.sqrt(square / count[:, 0:LANES])
+    done = [0] * 2
+    for im in range(images):
+        upto = rows_all if im == images - 1 else seq * (im + 1) // 8 * 8
+        for n, mine, rest, full, hbm in jobs:
+            pltpu.make_async_copy(
+                full.at[done[n] : upto, :], hbm.at[done[n] : upto, :], to_sem.at[n, im]
+            ).wait()
+            done[n] = upto
 
 
 def on_device(
@@ -1003,15 +1219,15 @@
     block = (experts, cap_dev, width)
     DMA = pltpu.SemaphoreType.DMA
     (
-        res_back, grad_back, gslot, gin_w, gout_w, gin_rest, gout_rest, gbin_own, gbin_rest, gb_out,
+        _, _, gin_w, gout_w, gin_rest, gout_rest, gbin_own, gbin_rest, gb_out,
+        moe_own, moe_rest, gmoe_own, gmoe_rest,
     ) = pl.pallas_call(
         moe_kernel,
-        in_specs=[anywhere, inside, anywhere] + [inside] * 7,
-        out_specs=[anywhere, anywhere, inside] + [anywhere] * 4 + [inside] * 3,
+        in_specs=[anywhere, inside, anywhere, anywhere] + [inside] * 8,
+        out_specs=[anywhere] * 6 + [inside] * 3 + [anywhere] * 4,
         out_shape=[
             S(block, bf16),
             S(block, bf16),
-            S((rows_all, 1), f32),
             S((width, share), bf16),
             S((share, width), bf16),
             S((cores - 1, width, share), bf16),
@@ -1019,21 +1235,25 @@
             S((1, share), f32),
             S((cores - 1, 1, share), f32),
             S((cores, 8, width), f32),
+            S((pad_own, wide), bf16),
+            S((cores - 1, pad_own, wide), bf16),
+            S((pad_own, width), bf16),
+            S((cores - 1, pad_own, width), bf16),
         ],
         scratch_shapes=[
             pltpu.VMEM((cores, pad_own, wide), bf16),
             pltpu.VMEM(block, bf16),
             pltpu.VMEM(block, bf16),
-            pltpu.VMEM((rows_all, hidden), bf16),
-            pltpu.VMEM((rows_all, hidden), bf16),
             pltpu.VMEM(block, bf16),
             pltpu.VMEM(block, bf16),
             pltpu.VMEM((experts, 8, cap_dev), f32),
             pltpu.VMEM((experts, 8, cap_dev), f32),
-            pltpu.VMEM((2, width, size), bf16),
-            pltpu.VMEM((2, size, width), bf16),
+            pltpu.VMEM((rows_all, 1), f32),
             pltpu.VMEM((cores - 1, 1, share), f32),
             pltpu.VMEM((8, width), f32),
+            DMA((2, cores - 1)),
+            DMA((2, cores - 1)),
+            DMA((2,)),
             DMA((2,)),
             DMA((cores,)),
             DMA((cores,)),
@@ -1045,39 +1265,8 @@
         compiler_params=params(collective_id=2, has_side_effects=True),
         name="moe",
     )(
-        h2x.reshape(pad_own, wide), post, grow, w_in[0], w_ins, b_in, b_ins, w_out[0], w_outs, b_out
+        h2x.reshape(pad_own, wide), post, grow, send_g, fidx, w_in[0], w_ins, b_in, b_ins, w_out[0], w_outs, b_out
     )
-    res_back = res_back.reshape(rows_all, width)
-    grad_back = grad_back.reshape(rows_all, width)
-    grad_w_in, grad_w_out = [
-        (own_part.astype(f32) + jnp.sum(rest_part.astype(f32), 0))[None]
-        for own_part, rest_part in ((gin_w, gin_rest), (gout_w, gout_rest))
-    ]
-    grad_b_in = gbin_own + jnp.sum(gbin_rest, 0)
-    grad_b_out = jnp.sum(gb_out[:, 0, :], 0, keepdims=True)
-
-    moe_own, moe_p, dots_own, dots_p = pl.pallas_call(
-        functools.partial(combine_kernel, cap_dev, True),
-        out_shape=[
-            S((pad_own, width), bf16),
-            S((cores - 1, pad_own, width), bf16),
-            S((pad_own, LANES), bf16),
-            S((cores - 1, pad_own, LANES), bf16),
-        ],
-        scratch_shapes=[pltpu.VMEM((rows_all, width), bf16), pltpu.VMEM((rows_all, LANES), bf16)],
-        compiler_params=params(),
-        name="combine_res",
-    )(res_back, gslot, fidx, send_g.reshape(rows_all, width))
-    moe, dots = swap(4, False, moe_p, dots_p)
-    gmoe_own, gmoe_p = pl.pallas_call(
-        functools.partial(combine_kernel, cap_dev, False),
-        out_shape=[S((pad_own, width), bf16), S((cores - 1, pad_own, width), bf16)],
-        scratch_shapes=[pltpu.VMEM((rows_all, width), bf16)],
-        compiler_params=params(),
-        name="combine_grad",
-    )(grad_back, gslot, fidx)
-    (gmoe,) = swap(5, False, gmoe_p)
-
     def pieces(n):
         return pl.BlockSpec((cores - 1, 1, seq_pad, n), lambda i: (0, i, 0, 0))
 
@@ -1085,9 +1274,10 @@
         return x.reshape(x.shape[:-2] + (own, seq_pad, x.shape[-1]))
 
     head_share = w_query.shape[1]
+    buffers = {"pipeline_mode": pl.Buffered(1)} if cores > 2 else {}
     small_b = small_base(cores)
     small_rows = up(small_b + 8 + experts, 8 * cores)
-    out_own, gin_own, grad_own, grad_rest, small = pl.pallas_call(
+    out_own, gin_own, grad_own, grad_rest, small, grad_w_in, grad_w_out = pl.pallas_call(
         functools.partial(attn_bwd_kernel, dims),
         grid=(own,),
         in_specs=[
@@ -1103,30 +1293,36 @@
             per_image(key_pad, width),
             per_image(pairs, 2 * seq_pad, key_pad),
             per_image(seq_pad, width),
+            per_image(seq_pad, wide),
+            pieces(wide),
             per_image(seq_pad, width),
             pieces(width),
-            per_image(seq_pad, LANES),
-            pieces(LANES),
-            per_image(seq_pad, width),
-            pieces(width),
+            pl.BlockSpec((width // own, share), lambda i: (i, 0)),
+            pl.BlockSpec((cores - 1, width // own, share), lambda i: (0, i, 0), **buffers),
+            pl.BlockSpec((share // own, width), lambda i: (i, 0)),
+            pl.BlockSpec((cores - 1, share // own, width), lambda i: (0, i, 0), **buffers),
             whole((1, width)),
             whole((1, width)),
             *[whole(w.shape) for w in attn_w],
             whole((width, LANES)),
         ],
         out_specs=[
-            whole((tok_own, width)),
-            whole((tok_own, width)),
+            per_image(seq_pad, width),
+            per_image(seq_pad, width),
             whole((4 * width, head_share)),
             whole((cores - 1, 4 * width, head_share)),
             whole((small_rows, width)),
+            pl.BlockSpec((1, width // own, share), lambda i: (0, i, 0)),
+            pl.BlockSpec((1, share // own, width), lambda i: (0, i, 0)),
         ],
         out_shape=[
-            S((tok_own, width), f32),
-            S((tok_own, width), f32),
+            S((own, seq_pad, width), f32),
+            S((own, seq_pad, width), f32),
             S((4 * width, head_share), f32),
             S((cores - 1, 4 * width, head_share), bf16),
             S((small_rows, width), f32),
+            S((1, width, share), f32),
+            S((1, share, width), f32),
         ],
         scratch_shapes=[pltpu.VMEM((seq_pad, width), f32)] * 2
         + [pltpu.VMEM((seq_pad, width), bf16)]
@@ -1135,31 +1331,28 @@
         name="attn_bwd",
     )(
         tokens_in, cotangent, valid_col, acc_f, middle, h2x, h1, q, k, v, probs, heads,
-        by_image(moe_own), by_image(moe), by_image(dots_own), by_image(dots),
-        by_image(gmoe_own), by_image(gmoe), row(ln1_gain), row(ln2_gain), *attn_w, wr,
+        by_image(moe_own), by_image(moe_rest), by_image(gmoe_own), by_image(gmoe_rest),
+        gin_w, gin_rest, gout_w, gout_rest, row(ln1_gain), row(ln2_gain), *attn_w, wr,
     )
-    output = lax.all_gather(out_own, "tensor", axis=0, tiled=True)
-    grad_input = lax.all_gather(gin_own, "tensor", axis=0, tiled=True)
-
     chunks = next(c for c in (4, 2, 1) if (4 * width // c // experts) % 16 == 0)
     bits = experts.bit_length() - 1
     piece_rows = small_rows // cores
     chunk_rows = 4 * width // chunks
-    wqkv, grad_w_proj, small = pl.pallas_call(
+    low, small, out_rest, gin_tok = pl.pallas_call(
         functools.partial(reduce_kernel, chunks),
-        in_specs=[inside, anywhere, inside],
-        out_specs=[inside] * 3,
+        in_specs=[inside, anywhere, inside, anywhere, anywhere],
+        out_specs=[inside, inside, anywhere, anywhere],
         out_shape=[
-            S((3 * width, head_share), f32),
-            S((head_share, width), f32),
+            S((4 * width, head_share), bf16),
             S((small_rows, width), f32),
+            S((cores - 1, own, seq_pad, width), f32),
+            S((cores - 1, own, seq_pad, width), f32),
         ],
         scratch_shapes=[
             pltpu.VMEM((cores - 1, 4 * width, head_share), bf16),
             pltpu.VMEM((4 * width, head_share), f32),
             pltpu.VMEM((chunks, chunk_rows, head_share), bf16),
             pltpu.VMEM((chunks, chunk_rows, head_share), bf16),
-            pltpu.VMEM((4 * width, head_share), bf16),
             pltpu.VMEM((cores - 1, piece_rows, width), f32),
             pltpu.VMEM((piece_rows, width), f32),
             pltpu.VMEM((bits, piece_rows, width), f32),
@@ -1174,38 +1367,39 @@
             DMA((bits,)),
             DMA((cores - 1,)),
             DMA((cores - 1,)),
+            DMA((2, cores - 1)),
+            DMA((2, cores - 1)),
         ],
         compiler_params=params(collective_id=6, has_side_effects=True),
         name="reduce",
-    )(grad_own, grad_rest, small)
-    squares = jnp.sum(
-        jnp.stack([small[small_b], small[small_b + 1], small[0], small[small_b + 2], small[1]]), -1
-    )
-    rms_values = jnp.sqrt(squares / (small[7, 0] * width))
-
-    def mine(first):
-        return lax.dynamic_slice(small, (first + core, 0), (1, head_share))[0]
-
+    )(grad_own, grad_rest, small, out_own, gin_own)
+    vector = S((width,), f32)
+    part = S((head_share,), f32)
+    square = S((width, head_share), f32)
+    (
+        output, grad_input, gl1, bl1, gq, gk, gv, gbq, gbv, gwp, gbp, gl2, bl2, grout,
+        grad_b_in, grad_b_out, rms,
+    ) = pl.pallas_call(
+        functools.partial(finish_kernel, seq),
+        in_specs=[inside] * 9,
+        out_specs=[anywhere] * 2 + [inside] * 15,
+        out_shape=[
+            S(tokens_in.shape, f32), S(tokens_in.shape, f32), vector, vector, square, square, square,
+            part, part, S((head_share, width), f32), vector, vector, vector,
+            S((width, experts), f32), S((1, share), f32), S((1, width), f32), S((8, LANES), f32),
+        ],
+        scratch_shapes=[
+            pltpu.VMEM(tokens_in.shape, f32),
+            pltpu.VMEM(tokens_in.shape, f32),
+            DMA((2, images)),
+            DMA((2, images)),
+        ],
+        compiler_params=params(),
+        name="finish",
+    )(low, small, gbin_own, gbin_rest, gb_out, out_own, out_rest, gin_own, gin_tok)
     return (
-        output,
-        grad_input,
-        small[5],
-        small[6],
-        wqkv[:width],
-        wqkv[width : 2 * width],
-        wqkv[2 * width :],
-        mine(8),
-        mine(8 + cores),
-        grad_w_proj,
-        small[4],
-        small[2],
-        small[3],
-        jnp.transpose(small[small_b + 8 : small_b + 8 + experts]),
-        grad_w_in,
-        grad_b_in,
-        grad_w_out,
-        grad_b_out,
-        rms_values,
+        output, grad_input, gl1, bl1, gq, gk, gv, gbq, gbv, gwp, gbp, gl2, bl2, grout,
+        grad_w_in, grad_b_in, grad_w_out, grad_b_out, rms[:5, 0],
     )
 
 

time: 536 us -> 492 us (0.918)
  local copies, waits for them, and re-layouts: 38.6 us -> 18.4 us
  between operations: 15.2 us -> 1.05 us
  other arithmetic: 9.19 us -> 1.33 us
    unnamed x40 -> x24, local copies, waits for them, and re-layouts: 12.5 us -> 1.97 us
    pallas_call x1, Pallas kernels: 69.1 us -> 79.1 us  [on_device(): pl.pallas_call(functools.partial(reduce_kernel, chunks), in_specs=[inside...]
    pallas_call x4 -> x2, Pallas kernels: 20.5 us -> 13.5 us  [swap(): pl.pallas_call(functools.partial(swap_kernel, gather, count), out_shape=o...]
    slice x4 -> x1, local copies, waits for them, and re-layouts: 7.58 us -> 1.31 us  [on_device(): rms[:5, 0]]
    broadcast_in_dim x2 -> x0, other arithmetic: 5.79 us -> none  [on_device(): (own_part.astype(f32) + jnp.sum(rest_part.astype(f32), 0))[None]]
    pallas_call x3 -> x2, Pallas kernels: 271 us -> 267 us  [the longest x1 256 us: on_device(): pl.pallas_call(moe_kernel, in_specs=[anywhere, inside, anywhere, anywhere...]
  transfers between devices with their start and end apart: 3 -> 1, of which waited for: 1 -> 1; matrix products, arithmetic and copies ran while one was open for 6% -> 2% of each run, Pallas kernels for 20% -> 7%
where the time goes in v2:
time: 492 us; the launch traced here: 485 us
  Pallas kernels  438 us (89%)
  local copies, waits for them, and re-layouts  18.4 us (4%)
  waiting for transfers between devices  17.1 us (3%)
  starting transfers between devices  8.63 us (2%)
    pallas_call x1, Pallas kernels, on_device(): pl.pallas_call(moe_kernel, in_specs=[anywhere, inside, anywhere, anywhere...  256 us
    pallas_call x1, Pallas kernels, on_device(): pl.pallas_call(functools.partial(reduce_kernel, chunks), in_specs=[inside...  79.1 us
    pallas_call x1, Pallas kernels, on_device(): pl.pallas_call(functools.partial(attn_bwd_kernel, dims), grid=(own,), in_...  43 us
    pallas_call x1, Pallas kernels, on_device(): pl.pallas_call(functools.partial(attn_fwd_kernel, dims), grid=(own,), in_...  22.4 us
    all_to_all x1, waiting for transfers between devices, a2a(): lax.all_to_all(rows, 'expert', split_axis=0, concat_axis=0, tiled=True)  17.1 us
    pallas_call x2, Pallas kernels, swap(): pl.pallas_call(functools.partial(swap_kernel, gather, count), out_shape=o...  13.5 us
    pallas_call x1, Pallas kernels, on_device(): pl.pallas_call(functools.partial(prep_kernel, (images, seq, seq_pad, expe...  13.1 us
    pallas_call x1, Pallas kernels, on_device(): pl.pallas_call(functools.partial(finish_kernel, seq), in_specs=[inside] *...  11.1 us
  transfers between devices with their start and end apart: 1, of which 1 were waited for; matrix products, arithmetic and copies ran while one was open for 2% of the time, Pallas kernels for 7%

profile of v2, /device:TPU:0, one launch (start us, length us, event | category | flops | bytes accessed | tf_op | source)
XLA Modules:
  0.0 484.9 jit_solution(10157725772768159519)
XLA Ops:
  0.7 0.8 reshape.193
  1.5 0.3 copy.45
  1.8 1.0 pad.19
  2.8 13.1 %prep.1 = (bf16[16,128,768]{2,1,0:T(8,128)(2,1)}, f32[2,16,1,832]{3,2,1,0:T(1,128)}, s32[1664,2]{1,0:T(8,128)}) custom-call(s32[1664,2]{1,0:T(8,128)} %bitcast.23, f32[1576,768]{1,0:T(8,128)} %cot_ref.3), custom_call_target="tpu_custom_call" | custom-call | tf_op jit(solution)/shard_map/prep/pallas_call | solution.py:1126
  15.9 4.3 gather_fusion
  20.2 0.0 copy-start.9
  20.2 0.0 copy-start.10
  20.2 0.0 copy-start.3
  20.2 0.0 copy-start.4
  20.2 0.0 copy-start.5
  20.2 0.0 copy-start.6
  20.2 0.0 copy-start.7
  20.2 0.0 copy-start.8
  20.2 0.0 copy-start
  20.2 8.6 %all-to-all-start = ((bf16[16,128,768]{2,1,0:T(8,128)(2,1)}), bf16[16,128,768]{2,1,0:T(8,128)(2,1)S(1)}, u32[]{:S(2)}, u32[]{:S(2)}) async-start(bf16[16,128,768]{2,1,0:T(8,128)(2,1)} %gather_fusion), calls=%async_computation | async-start | bytes 6291456 | tf_op jit(solution)/shard_map/all_to_all | solution.py:1121
  28.9 0.0 copy-done.9
  28.9 0.6 reshape.187.refs_4_
  29.5 0.0 copy-done.10
  29.5 0.6 reshape.188.refs_5_
  30.0 0.0 copy-done.3
  30.0 0.6 reshape.185.g1_ref
  30.6 0.0 copy-done.4
  30.6 0.6 reshape.190.g2_ref
  31.2 0.0 copy-done.5
  31.2 0.6 reshape.186.b1_ref
  31.8 0.0 copy-done.6
  31.8 0.6 reshape.189.bp_ref
  32.4 0.0 copy-done.7
  32.4 0.6 reshape.191.b2_ref
  33.0 0.0 copy-done.8
  33.0 0.6 broadcast_in_dim.19.mask_ref
  33.6 0.0 copy-done
  33.6 0.2 copy.43
  33.8 1.0 copy.46.valid_ref
  34.7 0.7 pad.18.wr_ref
  35.4 0.0 copy-start.1
  35.4 0.0 copy-start.2
  35.4 8.4 %swap7.1 = (bf16[1,768,1536]{2,1,0:T(8,128)(2,1)}, bf16[1,1536,768]{2,1,0:T(8,128)(2,1)}, f32[1,1,1536]{2,1,0:T(1,128)}) custom-call(bf16[768,1536]{1,0:T(8,128)(2,1)} %bitcast.18, bf16[1536,768]{1,0:T(8,128)(2,1)} %bitcast.20, f32[1,1536]{1,0:T(1,128)} %b_in.1), custom_call_target="tpu_custom_call" | custom-call | tf_op jit(solution)/shard_map/swap7/pallas_call | solution.py:845
  43.8 5.1 %swap1.1 = (bf16[1,768,384]{2,1,0:T(8,128)(2,1)}, bf16[1,768,384]{2,1,0:T(8,128)(2,1)}, bf16[1,768,384]{2,1,0:T(8,128)(2,1)}, bf16[1,384,768]{2,1,0:T(8,128)(2,1...) custom-call(bf16[768,384]{1,0:T(8,128)(2,1)} %wq.3, bf16[768,384]{1,0:T(8,128)(2,1)} %wk.3, bf16[768,384]{1,0:T(8,128)(2,1)} %wv.3, ...), custom_call_target="tpu_custom_call" | custom-call | tf_op jit(solution)/shard_map/swap1/pallas_call | solution.py:845
  49.0 0.0 copy-done.1
  49.0 0.0 copy-done.2
  49.0 1.3 pad_maximum_fusion
  50.3 22.4 %attn_fwd.1 = (bf16[4,208,768]{2,1,0:T(8,128)(2,1)}, bf16[4,208,768]{2,1,0:T(8,128)(2,1)}, bf16[4,256,768]{2,1,0:T(8,128)(2,1)}, bf16[4,256,768]{2,1,0:T(8,128)(...) custom-call(f32[1576,768]{1,0:T(8,128)} %tok_ref.3, ...), custom_call_target="tpu_custom_call" | custom-call | flops 4580179968 | bytes 25165824 | tf_op jit(solution)/shard_map/attn_fwd/pallas_call | solution.py:1163
  72.6 17.1 %all-to-all-done = bf16[16,128,768]{2,1,0:T(8,128)(2,1)S(1)} async-done(((bf16[16,128,768]{2,1,0:T(8,128)(2,1)}), bf16[16,128,768]{2,1,0:T(8,128)(2,1)S(1)}, u32[]{:S(2)}, u32[]{:S(2)}) %all-to-all-start) | async-done | bytes 3145760 | tf_op jit(solution)/shard_map/all_to_all | solution.py:1121
  89.8 2.4 gather_fusion.1
  92.2 256.1 %moe.1 = (bf16[16,128,768]{2,1,0:T(8,128)(2,1)}, bf16[16,128,768]{2,1,0:T(8,128)(2,1)}, bf16[768,1536]{1,0:T(8,128)(2,1)}, bf16[1536,768]{1,0:T(8,128)(2,1)}, bf...) custom-call(bf16[832,896]{1,0:T(8,128)(2,1)} %bitcast.22, ...), custom_call_target="tpu_custom_call" | custom-call | tf_op jit(solution)/shard_map/moe/pallas_call | solution.py:1224
  348.3 43.0 %attn_bwd.1 = (f32[4,208,768]{2,1,0:T(8,128)}, f32[4,208,768]{2,1,0:T(8,128)}, f32[3072,384]{1,0:T(8,128)}, bf16[1,3072,384]{2,1,0:T(8,128)(2,1)}, f32[48,768]{1...) custom-call(f32[1576,768]{1,0:T(8,128)} %tok_ref.3, f32[1576,768]{1,0:T(8,128)} %cot_ref.3, ...), custom_call_target="tpu_custom_call" | custom-call | tf_op jit(solution)/shard_map/attn_bwd/pallas_call | solution.py:1280
  391.4 79.1 %reduce.3 = (bf16[3072,384]{1,0:T(8,128)(2,1)}, f32[48,768]{1,0:T(8,128)}, f32[1,4,208,768]{3,2,1,0:T(8,128)}, f32[1,4,208,768]{3,2,1,0:T(8,128)}) custom-call(f32[3072,384]{1,0:T(8,128)} %get-tuple-element.108.own_ref, bf16[1,3072,384]{2,1,0:T(8,128)(2,1)} %get-tuple-element.109.rest_ref, f32[48,768]{1,0:T(8,128)} %get-tuple-element.110.small_ref, ...), custom_call_target="tpu_custom_call" | custom-call | tf_op jit(solution)/shard_map/reduce/pallas_call | solution.py:1341
  470.5 11.1 %finish.1 = (f32[1576,768]{1,0:T(8,128)}, f32[1576,768]{1,0:T(8,128)}, f32[768]{0:T(1024)}, f32[768]{0:T(1024)}, f32[768,384]{1,0:T(8,128)}, /*index=5*/f32[768,...) custom-call(bf16[3072,384]{1,0:T(8,128)(2,1)} %get-tuple-element.113, ...), custom_call_target="tpu_custom_call" | custom-call | tf_op jit(solution)/shard_map/finish/pallas_call | solution.py:1382
  481.7 1.3 slice_reduce_fusion
  483.0 1.8 copy.47
  (7 shorter events, 0.1 us)
Async XLA Ops:
  20.2 8.7 %copy-start.9 = (f32[384]{0:T(512)S(1)}, f32[384]{0:T(512)}, u32[]{:S(2)}) copy-start(f32[384]{0:T(512)} %param.28) | copy-start | bytes 4612
  20.2 9.3 %copy-start.10 = (f32[384]{0:T(512)S(1)}, f32[384]{0:T(512)}, u32[]{:S(2)}) copy-start(f32[384]{0:T(512)} %param.29) | copy-start | bytes 4612
  20.2 9.9 %copy-start.3 = (f32[768]{0:T(1024)S(1)}, f32[768]{0:T(1024)}, u32[]{:S(2)}) copy-start(f32[768]{0:T(1024)} %param.23) | copy-start | bytes 9220
  20.2 10.4 %copy-start.4 = (f32[768]{0:T(1024)S(1)}, f32[768]{0:T(1024)}, u32[]{:S(2)}) copy-start(f32[768]{0:T(1024)} %param.32) | copy-start | bytes 9220
  20.2 11.0 %copy-start.5 = (f32[768]{0:T(1024)S(1)}, f32[768]{0:T(1024)}, u32[]{:S(2)}) copy-start(f32[768]{0:T(1024)} %param.24) | copy-start | bytes 9220
  20.2 11.6 %copy-start.6 = (f32[768]{0:T(1024)S(1)}, f32[768]{0:T(1024)}, u32[]{:S(2)}) copy-start(f32[768]{0:T(1024)} %param.31) | copy-start | bytes 9220
  20.2 12.2 %copy-start.7 = (f32[768]{0:T(1024)S(1)}, f32[768]{0:T(1024)}, u32[]{:S(2)}) copy-start(f32[768]{0:T(1024)} %param.33) | copy-start | bytes 9220
  20.2 12.7 %copy-start.8 = (s32[8,197]{1,0:T(8,128)S(1)}, s32[8,197]{1,0:T(8,128)}, u32[]{:S(2)}) copy-start(s32[8,197]{1,0:T(8,128)} %param.21) | copy-start | bytes 18916
  20.2 13.3 %copy-start = (bf16[768,16]{0,1:T(8,128)(2,1)S(1)}, bf16[768,16]{0,1:T(8,128)(2,1)}, u32[]{:S(2)}) copy-start(bf16[768,16]{0,1:T(8,128)(2,1)} %param.34) | copy-start | bytes 73732
  20.2 69.5 %all-to-all-start = ((bf16[16,128,768]{2,1,0:T(8,128)(2,1)}), bf16[16,128,768]{2,1,0:T(8,128)(2,1)S(1)}, u32[]{:S(2)}, u32[]{:S(2)}) async-start(bf16[16,128,768]{2,1,0:T(8,128)(2,1)} %gather_fusion), calls=%async_computation | async-start | bytes 6291456 | tf_op jit(solution)/shard_map/all_to_all | solution.py:1121
  35.4 13.5 %copy-start.1 = (f32[1,384]{1,0:T(1,128)S(1)}, f32[1,384]{1,0:T(1,128)}, u32[]{:S(2)}) copy-start(f32[1,384]{1,0:T(1,128)} %reshape.187.refs_4_) | copy-start | bytes 4612
  35.4 13.5 %copy-start.2 = (f32[1,384]{1,0:T(1,128)S(1)}, f32[1,384]{1,0:T(1,128)}, u32[]{:S(2)}) copy-start(f32[1,384]{1,0:T(1,128)} %reshape.188.refs_5_) | copy-start | bytes 4612

commit v3 on v2

v3 whole, which is shorter than its diff:
```python
import functools

import jax
import jax.numpy as jnp
from jax import lax
from jax.experimental import pallas as pl
from jax.experimental.pallas import tpu as pltpu
from jax.sharding import PartitionSpec as P

HEAD_DIM = 64
LANES = 128
LOG2E = 1.4426950408889634
MASKED = -1e30
MESH = pl.DeviceIdType.MESH
VMEM_LIMIT = 60 << 20
f32 = jnp.float32
bf16 = jnp.bfloat16
i32 = jnp.int32


def up(value, step):
    return -(-value // step) * step


def params(**more):
    return pltpu.CompilerParams(vmem_limit_bytes=VMEM_LIMIT, **more)


def whole(shape):
    return pl.BlockSpec(shape, lambda *_: (0,) * len(shape), pipeline_mode=pl.Buffered(1))


def dot(a, b):
    return lax.dot_general(a, b, (((1,), (0,)), ((), ())), preferred_element_type=f32)


def dot_nt(a, b):
    return lax.dot_general(a, b, (((1,), (1,)), ((), ())), preferred_element_type=f32)


def dot_tn(a, b):
    return lax.dot_general(a, b, (((0,), (0,)), ((), ())), preferred_element_type=f32)


def lane_iota(shape):
    return lax.broadcasted_iota(i32, shape, len(shape) - 1)


def norm_parts(values):
    center = values - jnp.mean(values, -1, keepdims=True)
    inv_std = lax.rsqrt(jnp.mean(center * center, -1, keepdims=True) + 1e-06)
    return center * inv_std, inv_std


def norm_back(grad_out, normed, inv_std, gain):
    scaled = grad_out * gain
    return inv_std * (
        scaled
        - jnp.mean(scaled, -1, keepdims=True)
        - normed * jnp.mean(scaled * normed, -1, keepdims=True)
    )


def gelu_parts(x):
    z = jnp.abs(x) * 0.7071067811865476
    t = 1.0 / (1.0 + 0.3275911 * z)
    poly = t * (
        0.254829592 * 0.5
        + t
        * (
            -0.284496736 * 0.5
            + t * (1.421413741 * 0.5 + t * (-1.453152027 * 0.5 + t * (1.061405429 * 0.5)))
        )
    )
    e = jnp.exp2(x * x * (-0.5 * LOG2E))
    half = poly * e
    cdf = jnp.where(x >= 0, 1.0 - half, half)
    return x * cdf, cdf + x * e * 0.3989422804014327


def piece(own_ref, rest_ref, j):
    return own_ref[...] if j == 0 else rest_ref[j - 1]


def read_image(dst, src, image, seq):
    for n in range(src.shape[0] // seq):

        @pl.when(image == n)
        def _(n=n):
            dst[0:seq, :] = src[seq * n : seq * (n + 1), :]


def route_rows(dims, expert, core, routes_ref, cot_ref, routes_s, post_ref, fidx_ref, g16):
    images, seq, seq_pad, experts, cap_dev = dims
    tok_pad = images * seq_pad
    wide_s, routes_s = routes_s
    routes_s[...] = jnp.full(routes_s.shape, -1.0, f32)
    wide_s[...] = jnp.zeros_like(wide_s)
    wide_s[0:2, 0 : images * seq] = routes_ref[...].astype(f32)
    turned = jnp.transpose(wide_s[...], (1, 0))
    for i in range(images):
        rows = slice(seq_pad * i, seq_pad * i + seq)
        routes_s[rows, :] = turned[seq * i : seq * (i + 1), :]
        g16[seq_pad * i : seq_pad * (i + 1), :] = jnp.zeros((seq_pad, g16.shape[1]), bf16)
        g16[rows, :] = cot_ref[seq * i : seq * (i + 1), :].astype(bf16)
    r0 = routes_s[:, 0:1].astype(i32)
    r1 = routes_s[:, 1:2].astype(i32)
    lanes = lane_iota((tok_pad, LANES))
    named0 = r0 == lanes
    named1 = r1 == lanes
    named = jnp.where(named0 | named1, 1.0, 0.0)
    named_low = named.astype(bf16)
    lower = (
        lax.broadcasted_iota(i32, (seq_pad, seq_pad), 1)
        < lax.broadcasted_iota(i32, (seq_pad, seq_pad), 0)
    ).astype(f32).astype(bf16)
    run = jnp.zeros((1, LANES), f32)
    parts = []
    for i in range(images):
        rows = slice(seq_pad * i, seq_pad * (i + 1))
        parts.append(dot(lower, named_low[rows]) + run)
        run = run + jnp.sum(named[rows], 0, keepdims=True)
    before = jnp.concatenate(parts, 0) - (core * cap_dev).astype(f32)
    pos = jnp.where(named > 0, before, -1.0)
    groups, _, _, group = post_ref.shape
    for j in range(groups):
        turned = jnp.transpose(pos[group * j : group * (j + 1)], (1, 0))
        for e in range(experts):
            post_ref[j, e] = turned[e : e + 1]
    for k, named_k, r_k in ((0, named0, r0), (1, named1, r1)):
        slot = jnp.sum(jnp.where(named_k, before, 0.0), 1, keepdims=True)
        fits = (slot >= 0) & (slot < cap_dev) & (r_k >= 0)
        turn = lax.rem(r_k - expert + experts, experts)
        half = experts // 2
        far = jnp.where(turn >= half, 1, 0)
        flat = ((turn - far * half) * 2 + far).astype(f32) * cap_dev + slot
        fidx_ref[:, k : k + 1] = jnp.where(fits, flat, -1.0).astype(i32)


def vec(ref):
    return ref[...].reshape(1, -1)


def attn_fwd_kernel(
    dims, tok_ref, cot_ref, valid_ref, routes_ref, g1_ref, b1_ref, wq, wk, wv, wp, bq, bv,
    bp_ref, g2_ref, b2_ref, wr_ref, w_in_hbm, w_out_hbm, b_in_hbm,
    h1_ref, q_ref, k_ref, v_ref, probs_ref, heads_ref, mid_ref, ok_ref, x_ref,
    h2x_ref, acc_ref, sent_ref, post_ref, fidx_ref, wr_pad,
    wqs_hbm, wks_hbm, wvs_hbm, wps_hbm, grow_ref, h2x_rest, w_ins, w_outs, b_ins,
    wqs, wks, wvs, wps, g16, wide_s, routes_s, valid_s, bias_s, bias_in,
    w_send, w_recv, b_send, b_recv, h_send, h_recv, g_send, g_recv, own_sem, keep_sem
):
    images, seq, seq_pad, key_pad, own, cap_dev = dims
    width = tok_ref.shape[1]
    step = pl.program_id(0)
    experts, chip = around("expert")
    cores, core = around("tensor")
    me_e = lax.axis_index("expert")
    me_t = lax.axis_index("tensor")
    image = me_t * own + step
    group = own * seq_pad
    shares = shares_of(wq, wqs)
    share = wq.shape[1]

    def remote(src, dst, send, recv, there):
        return pltpu.make_async_remote_copy(
            src_ref=src, dst_ref=dst, send_sem=send, recv_sem=recv,
            device_id=there, device_id_type=MESH,
        )

    def weight_copy(n, k):
        src, dst = (
            (wq, wqs), (wk, wks), (wv, wvs), (wp, wps),
            (w_in_hbm, w_ins), (w_out_hbm, w_outs), (b_in_hbm, b_ins),
        )[n]
        return remote(src, dst.at[k - 1], w_send.at[n, k - 1], w_recv.at[n, k - 1], core(-k))

    def bias_copy(k):
        return remote(
            bias_s, bias_in.at[k - 1], b_send.at[k - 1], b_recv.at[k - 1], core(-k)
        )

    def h_copy(i, k):
        return remote(
            h2x_ref.at[i], h2x_rest.at[k - 1, i], h_send.at[i, k - 1], h_recv.at[i, k - 1], core(-k)
        )

    def g_copy(k):
        there = chip(offset_at(k, experts))
        return remote(sent_ref.at[k], grow_ref.at[k], g_send.at[k], g_recv.at[k], there)

    own_rows = pltpu.make_async_copy(sent_ref.at[0], grow_ref.at[0], own_sem)
    keeps = [
        pltpu.make_async_copy(src, dst, keep_sem.at[n])
        for n, (src, dst) in enumerate(
            ((wqs, wqs_hbm), (wks, wks_hbm), (wvs, wvs_hbm), (wps, wps_hbm))
        )
    ]

    @pl.when(step == 0)
    def _():
        peers = [core(k) for k in range(1, cores)] + [chip(k) for k in range(1, experts)]
        greet_start(peers)
        route_rows(
            (images, seq, seq_pad, experts, cap_dev), me_e, me_t,
            routes_ref, cot_ref, (wide_s, routes_s), post_ref, fidx_ref, g16,
        )
        greet_end(peers)
        bias_s[0:1, :] = vec(bq)
        bias_s[1:2, :] = vec(bv)
        for k in range(1, cores):
            bias_copy(k).start()
            for n in range(4):
                weight_copy(n, k).start()
        slots = lax.broadcasted_iota(i32, (cap_dev, group), 0).astype(f32)

        def send_rows(n, _):
            k = lax.rem(n + 1, experts)
            total = None
            for j in range(cores):
                named_e = post_ref[j, lax.rem(me_e + offset_at(k, experts), experts)]
                pick = jnp.where(named_e == slots, 1.0, 0.0).astype(bf16)
                term = dot(pick, g16[group * j : group * (j + 1), :])
                total = term if total is None else total + term
            sent_ref[k] = total.astype(bf16)

            @pl.when(k > 0)
            def _():
                g_copy(k).start()

            return 0

        lax.fori_loop(0, experts, send_rows, 0)
        own_rows.start()
        valid_s[...] = jnp.zeros_like(valid_s)
        valid_s[:, 0:seq] = valid_ref[...].astype(f32)
        wr_pad[...] = jnp.zeros_like(wr_pad)
        wr_pad[0:experts, :] = wr_ref[...]
        acc_ref[...] = jnp.zeros_like(acc_ref)
        for k in range(1, cores):
            bias_copy(k).wait()
            for n in range(4):
                weight_copy(n, k).wait()
            for n in range(4, 7):
                weight_copy(n, k).start()
        for copy in keeps:
            copy.start()

    x_ref[...] = jnp.zeros_like(x_ref)
    read_image(x_ref.at[0], tok_ref, image, seq)
    x = x_ref[0]
    normed, _ = norm_parts(x)
    h1 = (normed * vec(g1_ref) + vec(b1_ref)).astype(bf16)
    h1_ref[0] = h1
    k_ref[0, seq_pad:, :] = jnp.zeros((key_pad - seq_pad, width), bf16)
    v_ref[0, seq_pad:, :] = jnp.zeros((key_pad - seq_pad, width), bf16)
    for j, cols in enumerate(shares):
        bias = bias_s if j == 0 else bias_in.at[j - 1]
        q_ref[0, :, cols] = (dot(h1, piece(wq, wqs, j)) + bias[0:1, :]).astype(bf16)
        k_ref[0, 0:seq_pad, cols] = dot(h1, piece(wk, wks, j)).astype(bf16)
        v_ref[0, 0:seq_pad, cols] = (dot(h1, piece(wv, wvs, j)) + bias[1:2, :]).astype(bf16)
    low_half = lane_iota((seq_pad, LANES)) < HEAD_DIM
    which = lax.broadcasted_iota(i32, valid_s.shape, 0)
    ok_row = jnp.sum(jnp.where(which == image, valid_s[...], 0.0), 0, keepdims=True)
    ok_col = jnp.transpose(jnp.broadcast_to(ok_row, (LANES, key_pad)), (1, 0))[:seq_pad, 0:1]
    ok_ref[0] = ok_col
    mask = jnp.where(ok_row > 0, 0.0, MASKED)
    for p in range(width // LANES):
        cols = slice(LANES * p, LANES * (p + 1))
        qs = split_heads(q_ref[0, :, cols])
        s = dot_nt(qs, k_ref[0, :, cols]) * (HEAD_DIM**-0.5 * LOG2E) + mask
        e = jnp.exp2(s - jnp.max(s, -1, keepdims=True))
        prob = (e * (1.0 / jnp.sum(e, -1, keepdims=True))).astype(bf16)
        probs_ref[0, p] = prob
        o = dot(prob, v_ref[0, :, cols])
        heads_ref[0, :, cols] = jnp.where(low_half, o[:seq_pad], o[seq_pad:]).astype(bf16)
    attn = vec(bp_ref)
    for j, cols in enumerate(shares):
        attn = attn + dot(heads_ref[0, :, cols], piece(wp, wps, j))
    middle = x + attn
    mid_ref[0] = middle
    for row, field in enumerate((x, middle, attn)):
        acc_ref[row : row + 1, :] += jnp.sum(ok_col * field * field, 0, keepdims=True)
    normed2, _ = norm_parts(middle)
    h2 = (normed2 * vec(g2_ref) + vec(b2_ref)).astype(bf16)
    h2x_ref[step, :, 0:width] = h2
    logits = dot_nt(h2, wr_pad[...])
    logits = jnp.where(lane_iota(logits.shape) < experts, logits, MASKED)
    e = jnp.exp(logits - jnp.max(logits, -1, keepdims=True))
    prob = e / jnp.sum(e, -1, keepdims=True)
    high = prob.astype(bf16).astype(f32)
    h2x_ref[step, :, width:] = (high + pltpu.roll(prob - high, experts, 1)).astype(bf16)
    for k in range(1, cores):
        h_copy(step, k).start()

    @pl.when(step == own - 1)
    def _():
        for k in range(1, cores):
            for n in range(4, 7):
                weight_copy(n, k).wait()
            for i in range(own):
                h_copy(i, k).wait()

        def arrived(k, _):
            g_copy(k).wait()
            return 0

        lax.fori_loop(1, experts, arrived, 0)
        own_rows.wait()
        for copy in keeps:
            copy.wait()


def split_heads(value):
    low_half = lane_iota(value.shape) < HEAD_DIM
    zero = jnp.zeros_like(value)
    return jnp.concatenate([jnp.where(low_half, value, zero), jnp.where(low_half, zero, value)], 0)


def shares_of(own_ref, rest_ref):
    share = own_ref.shape[1]
    return [slice(share * j, share * (j + 1)) for j in range(rest_ref.shape[0] + 1)]


def add_parts(acc_ref, base, shares, value):
    rows = small_base(len(shares))
    which = lax.broadcasted_iota(i32, (rows, shares[0].stop), 0)
    for j, cols in enumerate(shares):
        owner = lax.rem(lax.axis_index("tensor") + j, len(shares))
        total = jnp.sum(value[:, cols].astype(f32), 0, keepdims=True)
        acc_ref[0:rows, shares[0]] += jnp.where(which == base + owner, total, 0.0)


def attn_bwd_a_kernel(
    dims, cot_ref, valid_ref, accf_ref, mid_ref, h2x_ref, h1_ref, probs_ref, heads_ref,
    moe_own, moe_ref, gmoe_own, gmoe_ref, gin_w, gin_ws, gout_w, gout_ws, g2_ref, wq, wp, wps, wr_ref,
    out_ref, gm_ref, gh_ref, dv_ref, grad_own, grad_rest, acc_ref, gw_in_ref, gw_out_ref,
    c_s, h1_s, heads_s, ga_s, dv_s
):
    seq, seq_pad, key_pad, own, experts = dims
    width = cot_ref.shape[1]
    step = pl.program_id(0)
    shares = shares_of(wq, wps)
    small_b = small_base(len(shares))
    image = lax.axis_index("tensor") * own + step
    at = pl.multiple_of(step * seq_pad, 16)
    c_s[seq // 8 * 8 :, :] = jnp.zeros((seq_pad - seq // 8 * 8, width), f32)
    read_image(c_s, cot_ref, image, seq)
    ok = valid_ref[0]

    @pl.when(step == 0)
    def _():
        acc_ref[...] = jnp.zeros_like(acc_ref)
        acc_ref[small_b : small_b + 8, :] = accf_ref[...]

    def add(row, value):
        acc_ref[row : row + 1, :] += jnp.sum(value, 0, keepdims=True)

    def total(own_ref, rest_ref, cols):
        value = own_ref[0, :, cols].astype(f32)
        for j in range(rest_ref.shape[0]):
            value = value + rest_ref[j, 0, :, cols].astype(f32)
        return value

    for sum_ref, own_ref, rest_ref in (
        (gw_in_ref, gin_w, gin_ws), (gw_out_ref, gout_w, gout_ws)
    ):
        value = own_ref[...].astype(f32)
        for j in range(rest_ref.shape[0]):
            value = value + rest_ref[j].astype(f32)
        sum_ref[0] = value
    middle = mid_ref[0]
    moe = total(moe_own, moe_ref, slice(0, width))
    output = middle + moe
    out_ref[0] = output
    add(0, ok * output * output)
    add(1, ok * moe * moe)
    h2 = h2x_ref[0, :, 0:width]
    pair = h2x_ref[0, :, width:].astype(f32)
    prob = jnp.where(
        lane_iota(pair.shape) < experts, pair + pltpu.roll(pair, LANES - experts, 1), 0.0
    )
    grad_probs = total(moe_own, moe_ref, slice(width, width + LANES))
    grad_logits = (
        prob * (grad_probs - jnp.sum(grad_probs * prob, -1, keepdims=True))
    ).astype(bf16)
    acc_ref[small_b + 8 : small_b + 8 + experts, :] += dot_tn(grad_logits, h2)[:experts]
    grad_h2 = dot(grad_logits, wr_ref[...]) + total(gmoe_own, gmoe_ref, slice(0, width))
    normed2, inv2 = norm_parts(middle)
    add(2, grad_h2 * normed2)
    add(3, grad_h2)
    add(7, jnp.broadcast_to(ok, grad_h2.shape))
    grad_middle = c_s[...] + norm_back(grad_h2, normed2, inv2, vec(g2_ref))
    gm_ref[0] = grad_middle
    grad_attn = grad_middle.astype(bf16)
    add(4, grad_attn.astype(f32))
    here = pl.ds(at, seq_pad)
    ga_s[here, :] = grad_attn
    heads_s[here, :] = heads_ref[0]
    h1_s[here, :] = h1_ref[0]
    for j, cols in enumerate(shares):
        gh_ref[0, :, cols] = dot_nt(grad_attn, piece(wp, wps, j)).astype(bf16)
    for p in range(width // LANES):
        cols = slice(LANES * p, LANES * (p + 1))
        gs = split_heads(gh_ref[0, :, cols])
        dv_s[here, cols] = dot_tn(probs_ref[0, p], gs)[:seq_pad].astype(bf16)
    dv = dv_s[here, :]
    dv_ref[0] = dv
    add_parts(acc_ref, 8 + len(shares), shares, dv)

    @pl.when(step == own - 1)
    def _():
        for n, (left, right) in enumerate(((ga_s, heads_s), (h1_s, dv_s))):
            rows = slice(width * n, width * (n + 1))
            grad = dot_tn(left[...], right[...])
            put_chunks(grad_own, grad_rest, rows, shares, grad)


def put_chunks(own_ref, rest_ref, rows, shares, grad):
    lanes = own_ref.shape[2]
    for j, cols in enumerate(shares):
        for c in range(own_ref.shape[0]):
            value = grad[:, cols.start + lanes * c : cols.start + lanes * (c + 1)]
            if j == 0:
                own_ref[c, rows, :] = value
            else:
                rest_ref[j - 1, c, rows, :] = value.astype(bf16)


def attn_bwd_b_kernel(
    dims, q_ref, k_ref, v_ref, probs_ref, gh_ref, first_own, first_rest, small_ref, g1_ref,
    wq, wqs, wk, wks, wv, wvs, x_hbm, gm_hbm, dv_hbm, h1_hbm, out_hbm,
    low_hbm, small_hbm, gin_ref, outs_ref, gins_ref,
    low, small_out, dq_s, dk_s, x_s, gm_s, dv_s, h1_s, rest_out, rest_s, acc, send_s, recv_s,
    small_a, small_r, small_m, small_s, small_t,
    load_sem, t_send, t_recv, x_send, x_recv, st_send, st_recv, sx_send, sx_recv, sg_send, sg_recv,
    o_send, o_recv, i_send, i_recv
):
    seq, seq_pad, key_pad, own, _ = dims
    width = q_ref.shape[2]
    step = pl.program_id(0)
    shares = shares_of(wq, wqs)
    at = pl.multiple_of(step * seq_pad, 16)
    here = pl.ds(at, seq_pad)
    experts, _ = around("expert")
    cores, core = around("tensor")
    me_e = lax.axis_index("expert")
    me_t = lax.axis_index("tensor")
    bits = experts.bit_length() - 1
    chunks, rows, _ = acc.shape[1:]
    piece_rows = small_r.shape[1]
    low_half = lane_iota((seq_pad, LANES)) < HEAD_DIM

    def my_bit(b):
        return lax.rem(me_e // (1 << b), 2)

    def partner(b):
        return {"expert": me_e + (1 << b) * (1 - 2 * my_bit(b))}

    def remote(src, dst, send, recv, there):
        return pltpu.make_async_remote_copy(
            src_ref=src, dst_ref=dst, send_sem=send, recv_sem=recv,
            device_id=there, device_id_type=MESH,
        )

    orders = []
    for c in range(chunks):
        order = list(range(bits))
        if c == 1:
            order = [1, 0] + order[2:]
        elif c == 2:
            order = order[2:] + order[:2]
        orders.append(order)

    def base_at(c, s):
        value = 0
        for n in range(s):
            value = value + my_bit(orders[c][n]) * (rows >> (n + 1))
        return value

    def inner(phase, c, k):
        source = first_rest if phase == 0 else rest_out
        return remote(
            source.at[k - 1, c], rest_s.at[phase, k - 1, c],
            t_send.at[phase, k - 1, c], t_recv.at[phase, k - 1, c], core(k),
        )

    def across(phase, c, s):
        sems = (x_send.at[phase, c, s], x_recv.at[phase, c, s])
        if s < bits:
            half = rows >> (s + 1)
            box = slice(rows - 2 * half, rows - half)
            return remote(
                send_s.at[phase, c, box, :], recv_s.at[phase, c, box, :], *sems,
                partner(orders[c][s]),
            )
        size = rows >> (2 * bits - s)
        mine = pl.ds(pl.multiple_of(base_at(c, 2 * bits - s), 16), size)
        return remote(
            low.at[phase, c, mine, :], low.at[phase, c, mine, :], *sems,
            partner(orders[c][2 * bits - 1 - s]),
        )

    def send_stage(phase, c, s):
        if s < bits:
            half = rows >> (s + 1)
            away = pl.ds(
                pl.multiple_of(base_at(c, s) + (1 - my_bit(orders[c][s])) * half, 16), half
            )
            send_s[phase, c, rows - 2 * half : rows - half, :] = acc[phase, c, away, :].astype(bf16)
        elif s == bits:
            mine = pl.ds(pl.multiple_of(base_at(c, bits), 16), rows >> bits)
            low[phase, c, mine, :] = acc[phase, c, mine, :].astype(bf16)
        across(phase, c, s).start()

    def end_stage(phase, c, s):
        across(phase, c, s).wait()
        if s < bits:
            half = rows >> (s + 1)
            keep = pl.ds(pl.multiple_of(base_at(c, s + 1), 16), half)
            acc[phase, c, keep, :] += recv_s[phase, c, rows - 2 * half : rows - half, :].astype(f32)

    def point(phase, s):
        for c in range(chunks):
            if s == 0:
                for k in range(1, cores):
                    inner(phase, c, k).wait()
                value = first_own[c] if phase == 0 else acc[phase, c]
                for k in range(cores - 1):
                    value = value + rest_s[phase, k, c].astype(f32)
                acc[phase, c] = value
            else:
                end_stage(phase, c, s - 1)
            if s < 2 * bits:
                send_stage(phase, c, s)

    def out_copy(k):
        return remote(out_hbm, outs_ref.at[k - 1], o_send.at[k - 1], o_recv.at[k - 1], core(k))

    def gin_copy(i, k):
        return remote(
            gin_ref.at[i], gins_ref.at[k - 1, i], i_send.at[i, k - 1], i_recv.at[i, k - 1], core(k)
        )

    loads = [
        pltpu.make_async_copy(src, dst, load_sem.at[n])
        for n, (src, dst) in enumerate(
            ((x_hbm, x_s), (gm_hbm, gm_s), (dv_hbm, dv_s), (h1_hbm, h1_s))
        )
    ]

    @pl.when(step == 0)
    def _():
        peers = [partner(b) for b in range(bits)] + [core(k) for k in range(1, cores)]
        greet_start(peers)
        for copy in loads:
            copy.start()
        greet_end(peers)
        for c in range(chunks):
            for k in range(1, cores):
                inner(0, c, k).start()

    pairs = width // LANES
    points = {}
    hidden_points = min(7, 2 * bits + 1)
    for n in range(hidden_points):
        turn = 4 + (n * (own * pairs - 5)) // max(hidden_points - 1, 1)
        points.setdefault((turn // pairs, turn % pairs), []).append(n)

    for p in range(pairs):
        cols = slice(LANES * p, LANES * (p + 1))
        gs = split_heads(gh_ref[0, :, cols])
        qs = split_heads(q_ref[0, :, cols])
        weights = probs_ref[0, p].astype(f32)
        mixed = weights * dot_nt(gs, v_ref[0, :, cols])
        ds = (
            (mixed - weights * jnp.sum(mixed, -1, keepdims=True)) * (HEAD_DIM**-0.5)
        ).astype(bf16)
        dq = dot(ds, k_ref[0, :, cols])
        dq_s[here, cols] = jnp.where(low_half, dq[:seq_pad], dq[seq_pad:]).astype(bf16)
        dk_s[here, cols] = dot_tn(ds, qs)[:seq_pad].astype(bf16)
        for i in range(own):
            if (i, p) in points:

                @pl.when(step == i)
                def _(i=i, p=p):
                    for n in points[i, p]:
                        point(0, n)
                        if n == 0:
                            for k in range(1, cores):
                                out_copy(k).start()

    @pl.when(step == own - 1)
    def _():
        for copy in loads:
            copy.wait()
        for n, part in enumerate((dq_s, dk_s)):
            box = slice(width * n, width * (n + 1))
            grad = dot_tn(h1_s[...].reshape(own * seq_pad, width), part[...])
            put_chunks(acc.at[1], rest_out, box, shares, grad)
        for c in range(chunks):
            for k in range(1, cores):
                inner(1, c, k).start()
        small_a[...] = small_ref[...]
        add_parts(small_a, 8, shares, dq_s[...])

        def first_norm(i):
            box = slice(seq_pad * i, seq_pad * (i + 1))
            grad_h1 = None
            for j, cols in enumerate(shares):
                for left, own_ref, rest_ref in (
                    (dq_s[box, cols], wq, wqs), (dk_s[box, cols], wk, wks), (dv_s[i, :, cols], wv, wvs)
                ):
                    term = dot_nt(left, piece(own_ref, rest_ref, j))
                    grad_h1 = term if grad_h1 is None else grad_h1 + term
            normed1, inv1 = norm_parts(x_s[i])
            for row, value in ((5, grad_h1 * normed1), (6, grad_h1)):
                small_a[row : row + 1, :] += jnp.sum(value, 0, keepdims=True)
            gin_ref[i] = gm_s[i] + norm_back(grad_h1, normed1, inv1, vec(g1_ref))
            for k in range(1, cores):
                gin_copy(i, k).start()

        def small_piece(k):
            mine = pl.ds(
                pl.multiple_of(lax.rem(me_t + k, cores) * piece_rows, 8), piece_rows
            )
            return remote(
                small_a.at[mine, :], small_r.at[k - 1], st_send.at[k - 1], st_recv.at[k - 1], core(k)
            )

        def small_across(n):
            return remote(small_s.at[n], small_t.at[n], sx_send.at[n], sx_recv.at[n], partner(n))

        mine = pl.ds(pl.multiple_of(me_t * piece_rows, 8), piece_rows)

        def small_back(k):
            return remote(
                small_m, small_out.at[mine, :], sg_send.at[k - 1], sg_recv.at[k - 1], core(k)
            )

        def small_point(n):
            if n == 0:
                for k in range(1, cores):
                    small_piece(k).wait()
                total = small_a[mine, :]
                for k in range(cores - 1):
                    total = total + small_r[k]
                small_m[...] = total
            else:
                small_across(n - 1).wait()
                small_m[...] += small_t[n - 1]
            if n < bits:
                small_s[n] = small_m[...]
                small_across(n).start()
            else:
                small_out[mine, :] = small_m[...]
                for k in range(1, cores):
                    small_back(k).start()

        older = list(range(hidden_points, 2 * bits + 1))
        newer = list(range(2 * bits + 1))
        norms = list(range(own))
        smalls = []
        while older or newer or norms or smalls:
            if norms:
                first_norm(norms.pop(0))
                if not norms:
                    for k in range(1, cores):
                        small_piece(k).start()
                    smalls = list(range(bits + 1))
            elif smalls:
                small_point(smalls.pop(0))
            if older:
                point(0, older.pop(0))
            if newer:
                point(1, newer.pop(0))
        keeps = [pltpu.make_async_copy(low, low_hbm, load_sem.at[0])]
        keeps[0].start()
        for k in range(1, cores):
            small_back(k).wait()
        keeps.append(pltpu.make_async_copy(small_out, small_hbm, load_sem.at[1]))
        keeps[1].start()
        for k in range(1, cores):
            out_copy(k).wait()
            for i in range(own):
                gin_copy(i, k).wait()
        for copy in keeps:
            copy.wait()


def small_base(cores):
    return up(8 + 2 * cores, 8)


def view(own_ref, rest_ref, j):
    return own_ref if j == 0 else rest_ref.at[j - 1]


def chunk_of(hidden):
    for size in (512, 384, 256, 128):
        if hidden % size == 0:
            return size
    return hidden


def greet_start(peers):
    barrier = pltpu.get_barrier_semaphore()
    for peer in peers:
        pl.semaphore_signal(barrier, inc=1, device_id=peer, device_id_type=MESH)


def greet_end(peers):
    pl.semaphore_wait(pltpu.get_barrier_semaphore(), len(peers))


def offset_at(place, experts):
    return place // 2 + lax.rem(place, 2) * (experts // 2)


def around(axis):
    n = lax.axis_size(axis)
    me = lax.axis_index(axis)
    return n, lambda k: {axis: lax.rem(me + n + k, n)}


def moe_kernel(
    h2x_ref, h2x_rest, post_ref, grow_hbm, sent_hbm, fidx_ref, w_in, w_ins, b_in, b_ins, w_out, w_outs,
    b_out_ref,
    back_ref, gback_ref, gin_own, gout_own, gin_rest, gout_rest,
    gbin_own, gbin_rest, gbout_ref, moe_own, moe_rest, gmoe_own, gmoe_rest,
    table, out_s, rows_s, grow_s, res_s, gate_out, gate_in, gslot_ref,
    gbin_send, gbout_send,
    m_send, m_recv, load_sem, local_sem, h_send, h_recv, c_send, c_recv, r_send, r_recv, g_send, g_recv,
    w_send, w_recv, own_sem
):
    experts, chip = around("expert")
    cores, core = around("tensor")
    me_e = lax.axis_index("expert")
    me_t = lax.axis_index("tensor")
    cap_dev, width = rows_s.shape[1:]
    group = table.shape[1]
    share = w_in.shape[1]
    size = chunk_of(share)
    per = share // size
    peers = [chip(k) for k in range(1, experts)] + [core(k) for k in range(1, cores)]
    greet_start(peers)

    def remote(src, dst, send, recv, there):
        return pltpu.make_async_remote_copy(
            src_ref=src, dst_ref=dst, send_sem=send, recv_sem=recv,
            device_id=there, device_id_type=MESH,
        )

    grow_copy = pltpu.make_async_copy(grow_hbm, grow_s, local_sem.at[0])
    grow_copy.start()
    fills = [
        pltpu.make_async_copy(
            h2x_ref if k == 0 else h2x_rest.at[k - 1],
            table.at[lax.rem(me_t + k, cores)], local_sem.at[1 + k],
        )
        for k in range(cores)
    ]
    for copy in fills:
        copy.start()
    for copy in fills:
        copy.wait()
    greet_end(peers)

    slots = lax.broadcasted_iota(i32, (cap_dev, group), 0).astype(f32)
    lanes = lane_iota((cap_dev, LANES))

    def select(k):
        e = lax.rem(me_e + offset_at(k, experts), experts)
        total = None
        for j in range(cores):
            pick = jnp.where(post_ref[j, e] == slots, 1.0, 0.0).astype(bf16)
            term = dot(pick, table[j])
            total = term if total is None else total + term
        mine = (lanes == e) | (lanes == e + experts)
        gate = jnp.sum(jnp.where(mine, total[:, width:], 0.0), 1, keepdims=True)
        gslot_ref[pl.ds(pl.multiple_of(cap_dev * k, 8), cap_dev), :] = gate
        spread = jnp.transpose(jnp.broadcast_to(gate, (cap_dev, LANES)), (1, 0))
        return total[:, :width].astype(bf16), spread[0:8]

    def h_copy(k):
        there = chip(offset_at(k, experts))
        return remote(out_s.at[k], rows_s.at[k], h_send.at[k], h_recv.at[k], there)

    def c_copy(k):
        there = chip(offset_at(k, experts))
        return remote(gate_out.at[k], gate_in.at[k], c_send.at[k], c_recv.at[k], there)

    def r_copy(k):
        there = chip(-offset_at(k, experts))
        return remote(res_s.at[k], back_ref.at[k], r_send.at[k], r_recv.at[k], there)

    def g_copy(k):
        there = chip(-offset_at(k, experts))
        return remote(out_s.at[k], gback_ref.at[k], g_send.at[k], g_recv.at[k], there)

    def send_rows(j, _):
        k = lax.rem(j + 1, experts)
        rows, gate = select(k)
        out_s[k] = rows
        gate_out[k] = gate

        @pl.when(k > 0)
        def _():
            h_copy(k).start()
            c_copy(k).start()

        return 0

    lax.fori_loop(0, experts, send_rows, 0)
    rows_s[0] = out_s[0]
    gate_in[0] = gate_out[0]
    pl.run_scoped(
        functools.partial(
            expert_phase, locals_of(
                experts=experts, cores=cores, core=core, me_t=me_t, width=width, cap_dev=cap_dev,
                share=share, size=size, per=per, w_in=w_in, w_ins=w_ins, b_in=b_in, b_ins=b_ins,
                w_out=w_out, w_outs=w_outs, b_out_ref=b_out_ref, rows_s=rows_s, res_s=res_s,
                back_ref=back_ref, own_sem=own_sem, h_copy=h_copy, r_copy=r_copy, c_copy=c_copy,
                g_copy=g_copy, grow_copy=grow_copy, grow_s=grow_s, out_s=out_s,
                gback_ref=gback_ref, gate_in=gate_in, gbout_send=gbout_send, gbout_ref=gbout_ref,
                gbin_own=gbin_own, gbin_send=gbin_send, gbin_rest=gbin_rest, gin_own=gin_own,
                gout_own=gout_own, gin_rest=gin_rest, gout_rest=gout_rest, w_send=w_send,
                w_recv=w_recv, remote=remote,
            ),
        ),
        pltpu.VMEM((experts * cap_dev, share * cores), bf16),
        pltpu.VMEM((experts * cap_dev, share * cores), bf16),
        pltpu.VMEM((2, width, size), bf16),
        pltpu.VMEM((2, size, width), bf16),
    )
    rows_all = experts * cap_dev
    wide = width + LANES

    def token_phase(picks, values, total):
        loads = [
            pltpu.make_async_copy(sent_hbm, grow_s, load_sem.at[0]),
            pltpu.make_async_copy(back_ref, rows_s, load_sem.at[1]),
        ]
        loads[0].start()

        def arrived(k, _):
            r_copy(k).wait()
            return 0

        lax.fori_loop(1, experts, arrived, 0)
        loads[1].start()
        step = 208 if group % 208 == 0 else group
        tiles = group // step
        slot_lanes = lane_iota((step, rows_all))

        def make_picks(i, _):
            tok = pl.ds(pl.multiple_of(i * step, 16), step)
            hit = (fidx_ref[tok, 0:1] == slot_lanes) | (fidx_ref[tok, 1:2] == slot_lanes)
            picks[tok, :] = jnp.where(hit, 1.0, 0.0).astype(bf16)
            return 0

        lax.fori_loop(0, cores * tiles, make_picks, 0)
        for copy in loads:
            copy.wait()

        def gated(k):
            return gslot_ref[pl.ds(pl.multiple_of(cap_dev * k, 8), cap_dev), :]

        def weigh(k, _):
            rows = rows_s[k].astype(f32)
            dots = jnp.sum(rows * grow_s[k].astype(f32), 1, keepdims=True)
            here = pl.ds(pl.multiple_of(cap_dev * k, 16), cap_dev)
            values[here, 0:width] = (rows * gated(k)).astype(bf16)
            mine = lanes == lax.rem(me_e + offset_at(k, experts), experts)
            values[here, width:] = jnp.where(mine, dots, 0.0).astype(bf16)
            return 0

        lax.fori_loop(0, experts, weigh, 0)

        def m_copy(kind, k):
            source = table.at[k] if kind == 0 else table.at[k, :, 0:width]
            return remote(
                source, (moe_rest, gmoe_rest)[kind].at[k - 1],
                m_send.at[kind, k - 1], m_recv.at[kind, k - 1], core(k),
            )

        keep_moe = pltpu.make_async_copy(table.at[0], moe_own, load_sem.at[0])
        keep_gmoe = pltpu.make_async_copy(table.at[0, :, 0:width], gmoe_own, load_sem.at[0])

        for k in list(range(1, cores)) + [0]:

            def sums(i, _, k=k):
                tok = pl.ds(
                    pl.multiple_of(lax.rem(me_t + k, cores) * group + i * step, 16), step
                )
                to = pl.ds(pl.multiple_of(i * step, 16), step)
                table[k, to, :] = dot(picks[tok, :], values[...]).astype(bf16)
                return 0

            lax.fori_loop(0, tiles, sums, 0)
            if k > 0:
                m_copy(0, k).start()
        keep_moe.start()
        keep_moe.wait()
        for k in range(1, cores):
            m_copy(0, k).wait()

        batch = 4
        batches = experts // batch
        for b in range(batches):
            first = b * batch
            for k in range(first, first + batch):
                if k > 0:
                    g_copy(k).wait_recv()
                else:
                    own_grad.wait()
            box = pl.ds(first, batch)
            load = pltpu.make_async_copy(gback_ref.at[box], rows_s.at[box], load_sem.at[0])
            load.start()
            load.wait()
            cols = slice(cap_dev * first, cap_dev * (first + batch))
            for k in range(first, first + batch):
                rows_s[k] = (rows_s[k].astype(f32) * gated(k)).astype(bf16)
            for k in list(range(1, cores)) + [0]:

                def gsums(i, _, k=k, b=b, cols=cols, box=box):
                    tok = pl.ds(
                        pl.multiple_of(lax.rem(me_t + k, cores) * group + i * step, 16), step
                    )
                    to = pl.ds(pl.multiple_of(i * step, 16), step)
                    rows = rows_s[box].reshape(batch * cap_dev, width)
                    value = dot(picks[tok, cols], rows)
                    if b > 0:
                        value = value + total[tok, :]
                    if b < batches - 1:
                        total[tok, :] = value
                    else:
                        table[k, to, 0:width] = value.astype(bf16)
                    return 0

                lax.fori_loop(0, tiles, gsums, 0)
                if b == batches - 1 and k > 0:
                    m_copy(1, k).start()
        keep_gmoe.start()
        keep_gmoe.wait()
        for k in range(1, cores):
            m_copy(1, k).wait()

        def finish(k, _):
            g_copy(k).wait_send()
            return 0

        lax.fori_loop(1, experts, finish, 0)

    own_grad = pltpu.make_async_copy(out_s.at[0], gback_ref.at[0], own_sem.at[1])
    pl.run_scoped(
        token_phase,
        pltpu.VMEM((cores * group, rows_all), bf16),
        pltpu.VMEM((rows_all, wide), bf16),
        pltpu.VMEM((cores * group, width), f32),
    )


class Bag:
    pass


def locals_of(**names):
    bag = Bag()
    bag.__dict__.update(names)
    return bag


def expert_phase(at, hid, slope, stage_in, stage_out):
    experts, cores, core, me_t, width, cap_dev = (
        at.experts, at.cores, at.core, at.me_t, at.width, at.cap_dev
    )
    share, size, per, remote = at.share, at.size, at.per, at.remote
    w_in, w_ins, b_in, b_ins, w_out, w_outs = at.w_in, at.w_ins, at.b_in, at.b_ins, at.w_out, at.w_outs
    b_out_ref, rows_s, res_s, back_ref, own_sem = at.b_out_ref, at.rows_s, at.res_s, at.back_ref, at.own_sem
    h_copy, r_copy, c_copy, g_copy, grow_copy = at.h_copy, at.r_copy, at.c_copy, at.g_copy, at.grow_copy
    grow_s, out_s, gback_ref, gate_in = at.grow_s, at.out_s, at.gback_ref, at.gate_in
    gbout_send, gbout_ref, gbin_own, gbin_send, gbin_rest = (
        at.gbout_send, at.gbout_ref, at.gbin_own, at.gbin_send, at.gbin_rest
    )
    gin_own, gout_own, gin_rest, gout_rest = at.gin_own, at.gout_own, at.gin_rest, at.gout_rest
    w_send, w_recv = at.w_send, at.w_recv

    def forward(i):
        x = rows_s[pl.ds(2 * i, 2)].reshape(2 * cap_dev, width)
        here = pl.ds(pl.multiple_of(2 * cap_dev * i, 16), 2 * cap_dev)
        total = None
        for j in range(cores):
            for n in range(per):
                cols = slice(size * n, size * (n + 1))
                flat = slice(share * j + size * n, share * j + size * (n + 1))
                pre = dot(x, view(w_in, w_ins, j)[:, cols]) + view(b_in, b_ins, j)[:, cols]
                act, steep = gelu_parts(pre)
                act = act.astype(bf16)
                hid[here, flat] = act
                slope[here, flat] = steep.astype(bf16)
                term = dot(act, view(w_out, w_outs, j)[cols, :])
                total = term if total is None else total + term
        res = (total + b_out_ref[...]).astype(bf16)
        res_s[pl.ds(2 * i, 2)] = res.reshape(2, cap_dev, width)

    own_res = pltpu.make_async_copy(res_s.at[0], back_ref.at[0], own_sem.at[0])

    def forward_step(i, _):

        @pl.when(i > 0)
        def _():
            h_copy(2 * i).wait_recv()

        h_copy(2 * i + 1).wait_recv()
        forward(i)

        @pl.when(i > 0)
        def _():
            r_copy(2 * i).start()

        @pl.when(i == 0)
        def _():
            own_res.start()

        r_copy(2 * i + 1).start()
        return 0

    lax.fori_loop(0, experts // 2, forward_step, 0)

    def sent_rows(k, _):
        h_copy(k).wait_send()
        return 0

    lax.fori_loop(1, experts, sent_rows, 0)
    grow_copy.wait()

    def backward(i):
        g = grow_s[pl.ds(2 * i, 2)].reshape(2 * cap_dev, width)
        here = pl.ds(pl.multiple_of(2 * cap_dev * i, 16), 2 * cap_dev)
        total = None
        for j in range(cores):
            for n in range(per):
                cols = slice(size * n, size * (n + 1))
                flat = slice(share * j + size * n, share * j + size * (n + 1))
                grad = dot_nt(g, view(w_out, w_outs, j)[cols, :])
                gpre = (grad * slope[here, flat].astype(f32)).astype(bf16)
                slope[here, flat] = gpre
                term = dot_nt(gpre, view(w_in, w_ins, j)[:, cols])
                total = term if total is None else total + term
        out_s[pl.ds(2 * i, 2)] = total.astype(bf16).reshape(2, cap_dev, width)

    own_grad = pltpu.make_async_copy(out_s.at[0], gback_ref.at[0], own_sem.at[1])

    def backward_step(i, _):
        backward(i)

        @pl.when(i > 0)
        def _():
            g_copy(2 * i).start()

        @pl.when(i == 0)
        def _():
            own_grad.start()

        g_copy(2 * i + 1).start()
        return 0

    lax.fori_loop(0, experts // 2, backward_step, 0)

    def gates_in(k, _):
        c_copy(k).wait()
        return 0

    lax.fori_loop(1, experts, gates_in, 0)

    def scale_rows(k, total):
        square = jnp.broadcast_to(gate_in[k, 0:1, :], (LANES, cap_dev))
        gate = jnp.transpose(square, (1, 0))[:, 0:1]
        rows_s[k] = (rows_s[k].astype(f32) * gate).astype(bf16)
        scaled = (grow_s[k].astype(f32) * gate).astype(bf16)
        grow_s[k] = scaled
        return total + jnp.sum(scaled.astype(f32), 0, keepdims=True)

    bias = lax.fori_loop(0, experts, scale_rows, jnp.zeros((1, width), f32))
    gbout_send[...] = jnp.broadcast_to(bias, gbout_send.shape)
    gbout_ref[me_t] = jnp.broadcast_to(bias, gbout_send.shape)
    rows_all = experts * cap_dev

    def grads(col):
        cols = pl.ds(pl.multiple_of(col, LANES), size)
        left = rows_s[...].reshape(rows_all, width)
        right = grow_s[...].reshape(rows_all, width)
        return dot_tn(left, slope[:, cols]), dot_tn(hid[:, cols], right)

    def column_sums(col):
        cols = pl.ds(pl.multiple_of(col, LANES), size)
        total = jnp.zeros((1, size), f32)
        for k in range(experts):
            square = jnp.broadcast_to(gate_in[k, 0:1, :], (LANES, cap_dev))
            gate = jnp.transpose(square, (1, 0))[:, 0:1]
            here = slice(cap_dev * k, cap_dev * (k + 1))
            total = total + jnp.sum(slope[here, cols].astype(f32) * gate, 0, keepdims=True)
        return total

    pending = []
    for j in list(range(1, cores)) + [0]:
        for n in range(per):
            cols = slice(size * n, size * (n + 1))
            slot = len(pending) % 2
            if len(pending) >= 2:
                for wait in pending[-2]:
                    wait()
            gw_in, gw_out = grads(share * j + size * n)
            stage_in[slot] = gw_in.astype(bf16)
            stage_out[slot] = gw_out.astype(bf16)
            sums = column_sums(share * j + size * n)
            if j == 0:
                gbin_own[:, cols] = sums
                a = pltpu.make_async_copy(stage_in.at[slot], gin_own.at[:, cols], own_sem.at[2 + slot])
                b = pltpu.make_async_copy(stage_out.at[slot], gout_own.at[cols, :], own_sem.at[4 + slot])
                a.start()
                b.start()
                pending.append((a.wait, b.wait))
            else:
                gbin_send[j - 1, :, cols] = sums
                at = (j - 1) * per + n
                a = remote(
                    stage_in.at[slot], gin_rest.at[j - 1, :, cols],
                    w_send.at[0, at], w_recv.at[0, at], core(j),
                )
                b = remote(
                    stage_out.at[slot], gout_rest.at[j - 1, cols, :],
                    w_send.at[1, at], w_recv.at[1, at], core(j),
                )
                a.start()
                b.start()
                pending.append((a.wait_send, b.wait_send))
        if j != 0:
            tail = [
                remote(
                    gbin_send.at[j - 1], gbin_rest.at[j - 1],
                    w_send.at[2, j - 1], w_recv.at[2, j - 1], core(j),
                ),
                remote(
                    gbout_send, gbout_ref.at[me_t],
                    w_send.at[3, j - 1], w_recv.at[3, j - 1], core(j),
                ),
            ]
            for copy in tail:
                copy.start()
    for waits in pending[-2:]:
        for wait in waits:
            wait()
    for j in range(1, cores):
        for n in range(per):
            cols = slice(size * n, size * (n + 1))
            at = (j - 1) * per + n
            remote(
                stage_in.at[0], gin_rest.at[j - 1, :, cols],
                w_send.at[0, at], w_recv.at[0, at], core(j),
            ).wait_recv()
            remote(
                stage_out.at[0], gout_rest.at[j - 1, cols, :],
                w_send.at[1, at], w_recv.at[1, at], core(j),
            ).wait_recv()
        remote(
            gbin_send.at[j - 1], gbin_rest.at[j - 1],
            w_send.at[2, j - 1], w_recv.at[2, j - 1], core(j),
        ).wait()
        remote(
            gbout_send, gbout_ref.at[me_t], w_send.at[3, j - 1], w_recv.at[3, j - 1], core(j)
        ).wait()

    own_res.wait()


def finish_kernel(
    seq, low_ref, small_ref, gbin_own, gbin_rest, gbout_ref, out_own, out_rest, gin_own, gin_rest,
    out_hbm, gin_hbm, gl1, bl1, gq, gk, gv, gbq, gbv, gwp, gbp, gl2, bl2, grout, gbin, gbout, rms,
    out_s, gin_s, in_sem, to_sem
):
    cores, own, seq_pad, width = (out_rest.shape[0] + 1,) + out_rest.shape[1:]
    me_t = lax.axis_index("tensor")
    images = cores * own
    share = gbq.shape[0]
    experts = grout.shape[0]
    jobs = []
    for n, (mine, rest, full, hbm) in enumerate(
        ((out_own, out_rest, out_s, out_hbm), (gin_own, gin_rest, gin_s, gin_hbm))
    ):
        jobs.append((n, mine, rest, full, hbm))
    rows_all = images * seq

    def place(c):
        for n, mine, rest, full, hbm in jobs:
            done = 0
            for im in range(images):
                p = (im // own - c) % cores
                src = mine.at[im % own] if p == 0 else rest.at[p - 1, im % own]
                full[seq * im : seq * (im + 1), :] = src[0:seq, :]
                upto = rows_all if im == images - 1 else seq * (im + 1) // 8 * 8
                pltpu.make_async_copy(
                    full.at[done:upto, :], hbm.at[done:upto, :], to_sem.at[n, im]
                ).start()
                done = upto

    for c in range(cores):

        @pl.when(me_t == c)
        def _(c=c):
            place(c)

    lanes = low_ref.shape[3]
    for c in range(low_ref.shape[1]):
        cols = slice(lanes * c, lanes * (c + 1))
        for grad, phase, n in ((gv, 0, 1), (gq, 1, 0), (gk, 1, 1)):
            grad[:, cols] = low_ref[phase, c, width * n : width * (n + 1), :].astype(f32)
        gwp[cols, :] = jnp.transpose(low_ref[0, c, 0:width, :].astype(f32), (1, 0))
    base = small_base(cores)
    for dst, row in ((gl1, 5), (bl1, 6), (gbp, 4), (gl2, 2), (bl2, 3)):
        dst[...] = small_ref[row]
    which = lax.broadcasted_iota(i32, (base, share), 0)
    for dst, row in ((gbq, 8), (gbv, 8 + cores)):
        dst[...] = jnp.sum(jnp.where(which == row + me_t, small_ref[0:base, 0:share], 0.0), 0)
    grout[...] = small_ref[base + 8 : base + 8 + experts, :]
    value = gbin_own[...]
    for k in range(cores - 1):
        value = value + gbin_rest[k]
    gbin[...] = value
    value = gbout_ref[0, 0:1, :]
    for k in range(1, cores):
        value = value + gbout_ref[k, 0:1, :]
    gbout[...] = value
    count = small_ref[7:8, 0:1] * width
    lanes = lane_iota((1, LANES))
    value = jnp.zeros((1, LANES), f32)
    for n, row in enumerate((base, base + 1, 0, base + 2, 1)):
        square = jnp.sum(small_ref[row : row + 1, :], 1, keepdims=True)
        value = jnp.where(lanes == n, jnp.sqrt(square / count), value)
    rms[...] = value[0, 0:5]
    done = [0] * 2
    for im in range(images):
        upto = rows_all if im == images - 1 else seq * (im + 1) // 8 * 8
        for n, mine, rest, full, hbm in jobs:
            pltpu.make_async_copy(
                full.at[done[n] : upto, :], hbm.at[done[n] : upto, :], to_sem.at[n, im]
            ).wait()
            done[n] = upto


def on_device(
    tokens_in, valid, routes, ln1_gain, ln1_bias, w_query, w_key, w_value, b_query, b_value,
    w_proj, b_proj, ln2_gain, ln2_bias, w_router, w_in, b_in, w_out, b_out, cotangent,
):
    tok_rows, width = tokens_in.shape
    images, seq = valid.shape
    experts = lax.axis_size("expert")
    cores = lax.axis_size("tensor")
    core = lax.axis_index("tensor")
    capacity = (10 * tok_rows // (4 * experts) // 8 + 1) * 8
    cap_dev = up(up(capacity, cores) // cores, 16)
    rows_all = experts * cap_dev
    seq_pad = up(seq, 16)
    key_pad = up(seq_pad, LANES)
    own = images // cores
    tok_own = own * seq
    tok_pad = images * seq_pad
    pad_own = own * seq_pad
    share = w_in.shape[2]
    hidden = share * cores
    wide = width + LANES
    pairs = width // LANES
    S = jax.ShapeDtypeStruct

    dims = (seq, seq_pad, key_pad, own, experts)

    def per_image(*shape):
        return pl.BlockSpec((1,) + shape, lambda i: (i,) + (0,) * len(shape))

    anywhere = pl.BlockSpec(memory_space=pl.ANY)
    inside = pl.BlockSpec(memory_space=pltpu.VMEM)
    block = (experts, cap_dev, width)
    DMA = pltpu.SemaphoreType.DMA
    (
        h1, q, k, v, probs, heads, middle, valid_col, x_pad, h2x, acc_f, send_g, post, fidx,
        wr, wqs, wks, wvs, wps, grow, h2x_rest, w_ins, w_outs, b_ins,
    ) = pl.pallas_call(
        functools.partial(attn_fwd_kernel, (images, seq, seq_pad, key_pad, own, cap_dev)),
        grid=(own,),
        in_specs=[
            *[
                whole(a.shape)
                for a in (
                    tokens_in, cotangent, valid, routes.T, ln1_gain, ln1_bias, w_query, w_key,
                    w_value, w_proj, b_query, b_value, b_proj, ln2_gain, ln2_bias, w_router.T,
                )
            ],
            *[anywhere] * 3,
        ],
        out_specs=[
            per_image(seq_pad, width),
            per_image(seq_pad, width),
            per_image(key_pad, width),
            per_image(key_pad, width),
            per_image(pairs, 2 * seq_pad, key_pad),
            per_image(seq_pad, width),
            per_image(seq_pad, width),
            per_image(seq_pad, 1),
            per_image(seq_pad, width),
            whole((own, seq_pad, wide)),
            whole((8, width)),
            whole(block),
            whole((cores, experts, 1, pad_own)),
            whole((tok_pad, 2)),
            whole((LANES, width)),
            *[anywhere] * 9,
        ],
        out_shape=[
            S((own, seq_pad, width), bf16),
            S((own, seq_pad, width), bf16),
            S((own, key_pad, width), bf16),
            S((own, key_pad, width), bf16),
            S((own, pairs, 2 * seq_pad, key_pad), bf16),
            S((own, seq_pad, width), bf16),
            S((own, seq_pad, width), f32),
            S((own, seq_pad, 1), f32),
            S((own, seq_pad, width), f32),
            S((own, seq_pad, wide), bf16),
            S((8, width), f32),
            S(block, bf16),
            S((cores, experts, 1, pad_own), f32),
            S((tok_pad, 2), i32),
            S((LANES, width), bf16),
            *[S((cores - 1,) + w.shape, bf16) for w in (w_query, w_key, w_value, w_proj)],
            S(block, bf16),
            S((cores - 1, own, seq_pad, wide), bf16),
            S((cores - 1, width, share), bf16),
            S((cores - 1, share, width), bf16),
            S((cores - 1, 1, share), f32),
        ],
        scratch_shapes=[
            *[
                pltpu.VMEM((cores - 1,) + w.shape, bf16)
                for w in (w_query, w_key, w_value, w_proj)
            ],
            pltpu.VMEM((tok_pad, width), bf16),
            pltpu.VMEM((8, up(tok_rows, LANES)), f32),
            pltpu.VMEM((tok_pad, 8), f32),
            pltpu.VMEM((images, key_pad), f32),
            pltpu.VMEM((8, w_query.shape[1]), f32),
            pltpu.VMEM((cores - 1, 8, w_query.shape[1]), f32),
            DMA((7, cores - 1)),
            DMA((7, cores - 1)),
            DMA((cores - 1,)),
            DMA((cores - 1,)),
            DMA((own, cores - 1)),
            DMA((own, cores - 1)),
            DMA((experts,)),
            DMA((experts,)),
            DMA,
            DMA((4,)),
        ],
        compiler_params=params(collective_id=1, has_side_effects=True),
        name="attn_fwd",
    )(
        tokens_in, cotangent, valid, routes.T, ln1_gain, ln1_bias, w_query, w_key, w_value, w_proj,
        b_query, b_value, b_proj, ln2_gain, ln2_bias, w_router.T, w_in[0], w_out[0], b_in,
    )
    attn_w = [w_query, wqs, w_key, wks, w_value, wvs, w_proj, wps]

    size = chunk_of(share)
    per = share // size
    (
        _, _, gin_w, gout_w, gin_rest, gout_rest, gbin_own, gbin_rest, gb_out,
        moe_own, moe_rest, gmoe_own, gmoe_rest,
    ) = pl.pallas_call(
        moe_kernel,
        in_specs=[anywhere, anywhere, inside, anywhere, anywhere] + [inside] * 8,
        out_specs=[anywhere] * 6 + [inside] * 3 + [anywhere] * 4,
        out_shape=[
            S(block, bf16),
            S(block, bf16),
            S((width, share), bf16),
            S((share, width), bf16),
            S((cores - 1, width, share), bf16),
            S((cores - 1, share, width), bf16),
            S((1, share), f32),
            S((cores - 1, 1, share), f32),
            S((cores, 8, width), f32),
            S((pad_own, wide), bf16),
            S((cores - 1, pad_own, wide), bf16),
            S((pad_own, width), bf16),
            S((cores - 1, pad_own, width), bf16),
        ],
        scratch_shapes=[
            pltpu.VMEM((cores, pad_own, wide), bf16),
            pltpu.VMEM(block, bf16),
            pltpu.VMEM(block, bf16),
            pltpu.VMEM(block, bf16),
            pltpu.VMEM(block, bf16),
            pltpu.VMEM((experts, 8, cap_dev), f32),
            pltpu.VMEM((experts, 8, cap_dev), f32),
            pltpu.VMEM((rows_all, 1), f32),
            pltpu.VMEM((cores - 1, 1, share), f32),
            pltpu.VMEM((8, width), f32),
            DMA((2, cores - 1)),
            DMA((2, cores - 1)),
            DMA((2,)),
            DMA((1 + cores,)),
            *[DMA((experts,))] * 8,
            DMA((4, (cores - 1) * per)),
            DMA((4, (cores - 1) * per)),
            DMA((6,)),
        ],
        compiler_params=params(collective_id=2, has_side_effects=True),
        name="moe",
    )(
        h2x.reshape(pad_own, wide), h2x_rest.reshape(cores - 1, pad_own, wide), post, grow, send_g, fidx, w_in[0], w_ins, b_in, b_ins, w_out[0], w_outs, b_out
    )
    def pieces(n):
        return pl.BlockSpec((cores - 1, 1, seq_pad, n), lambda i: (0, i, 0, 0))

    def by_image(x):
        return x.reshape(x.shape[:-2] + (own, seq_pad, x.shape[-1]))

    head_share = w_query.shape[1]
    chunks = 3 if head_share == 3 * LANES else 1
    lanes = head_share // chunks
    buffers = {"pipeline_mode": pl.Buffered(1)} if cores > 2 else {}
    small_b = small_base(cores)
    small_rows = up(small_b + 8 + experts, 8 * cores)
    (
        out_own, gm, gh, dv, first_own, first_rest, small, grad_w_in, grad_w_out,
    ) = pl.pallas_call(
        functools.partial(attn_bwd_a_kernel, dims),
        grid=(own,),
        in_specs=[
            whole(cotangent.shape),
            per_image(seq_pad, 1),
            whole((8, width)),
            per_image(seq_pad, width),
            per_image(seq_pad, wide),
            per_image(seq_pad, width),
            per_image(pairs, 2 * seq_pad, key_pad),
            per_image(seq_pad, width),
            per_image(seq_pad, wide),
            pieces(wide),
            per_image(seq_pad, width),
            pieces(width),
            pl.BlockSpec((width // own, share), lambda i: (i, 0)),
            pl.BlockSpec((cores - 1, width // own, share), lambda i: (0, i, 0), **buffers),
            pl.BlockSpec((share // own, width), lambda i: (i, 0)),
            pl.BlockSpec((cores - 1, share // own, width), lambda i: (0, i, 0), **buffers),
            whole((width,)),
            whole(w_query.shape),
            *[whole(w.shape) for w in attn_w[6:]],
            whole((LANES, width)),
        ],
        out_specs=[
            per_image(seq_pad, width),
            per_image(seq_pad, width),
            per_image(seq_pad, width),
            per_image(seq_pad, width),
            whole((chunks, 2 * width, lanes)),
            whole((cores - 1, chunks, 2 * width, lanes)),
            whole((small_rows, width)),
            pl.BlockSpec((1, width // own, share), lambda i: (0, i, 0)),
            pl.BlockSpec((1, share // own, width), lambda i: (0, i, 0)),
        ],
        out_shape=[
            S((own, seq_pad, width), f32),
            S((own, seq_pad, width), f32),
            S((own, seq_pad, width), bf16),
            S((own, seq_pad, width), bf16),
            S((chunks, 2 * width, lanes), f32),
            S((cores - 1, chunks, 2 * width, lanes), bf16),
            S((small_rows, width), f32),
            S((1, width, share), f32),
            S((1, share, width), f32),
        ],
        scratch_shapes=[pltpu.VMEM((seq_pad, width), f32)]
        + [pltpu.VMEM((pad_own, width), bf16)] * 4,
        compiler_params=params(),
        name="attn_bwd_a",
    )(
        cotangent, valid_col, acc_f, middle, h2x, h1, probs, heads,
        by_image(moe_own), by_image(moe_rest), by_image(gmoe_own), by_image(gmoe_rest),
        gin_w, gin_rest, gout_w, gout_rest, ln2_gain, w_query, *attn_w[6:], wr,
    )
    bits = experts.bit_length() - 1
    piece_rows = small_rows // cores
    low, small, gin_own, out_rest, gin_tok = pl.pallas_call(
        functools.partial(attn_bwd_b_kernel, dims),
        grid=(own,),
        in_specs=[
            per_image(seq_pad, width),
            per_image(key_pad, width),
            per_image(key_pad, width),
            per_image(pairs, 2 * seq_pad, key_pad),
            per_image(seq_pad, width),
            whole((chunks, 2 * width, lanes)),
            anywhere,
            whole((small_rows, width)),
            whole((width,)),
            *[whole(w.shape) for w in attn_w[:6]],
            *[anywhere] * 5,
        ],
        out_specs=[
            anywhere,
            anywhere,
            whole((own, seq_pad, width)),
            anywhere,
            anywhere,
        ],
        out_shape=[
            S((2, chunks, 2 * width, lanes), bf16),
            S((small_rows, width), f32),
            S((own, seq_pad, width), f32),
            S((cores - 1, own, seq_pad, width), f32),
            S((cores - 1, own, seq_pad, width), f32),
        ],
        scratch_shapes=[
            pltpu.VMEM((2, chunks, 2 * width, lanes), bf16),
            pltpu.VMEM((small_rows, width), f32),
            pltpu.VMEM((pad_own, width), bf16),
            pltpu.VMEM((pad_own, width), bf16),
            pltpu.VMEM((own, seq_pad, width), f32),
            pltpu.VMEM((own, seq_pad, width), f32),
            pltpu.VMEM((own, seq_pad, width), bf16),
            pltpu.VMEM((own, seq_pad, width), bf16),
            pltpu.VMEM((cores - 1, chunks, 2 * width, lanes), bf16),
            pltpu.VMEM((2, cores - 1, chunks, 2 * width, lanes), bf16),
            pltpu.VMEM((2, chunks, 2 * width, lanes), f32),
            pltpu.VMEM((2, chunks, 2 * width, lanes), bf16),
            pltpu.VMEM((2, chunks, 2 * width, lanes), bf16),
            pltpu.VMEM((small_rows, width), f32),
            pltpu.VMEM((cores - 1, piece_rows, width), f32),
            pltpu.VMEM((piece_rows, width), f32),
            pltpu.VMEM((bits, piece_rows, width), f32),
            pltpu.VMEM((bits, piece_rows, width), f32),
            DMA((4,)),
            DMA((2, cores - 1, chunks)),
            DMA((2, cores - 1, chunks)),
            DMA((2, chunks, 2 * bits)),
            DMA((2, chunks, 2 * bits)),
            DMA((cores - 1,)),
            DMA((cores - 1,)),
            DMA((bits,)),
            DMA((bits,)),
            DMA((cores - 1,)),
            DMA((cores - 1,)),
            DMA((cores - 1,)),
            DMA((cores - 1,)),
            DMA((own, cores - 1)),
            DMA((own, cores - 1)),
        ],
        compiler_params=params(collective_id=6, has_side_effects=True),
        name="attn_bwd_b",
    )(
        q, k, v, probs, gh, first_own, first_rest, small, ln1_gain, *attn_w[:6],
        x_pad, gm, dv, h1, out_own,
    )
    vector = S((width,), f32)
    part = S((head_share,), f32)
    square = S((width, head_share), f32)
    (
        output, grad_input, gl1, bl1, gq, gk, gv, gbq, gbv, gwp, gbp, gl2, bl2, grout,
        grad_b_in, grad_b_out, rms,
    ) = pl.pallas_call(
        functools.partial(finish_kernel, seq),
        in_specs=[inside] * 9,
        out_specs=[anywhere] * 2 + [inside] * 15,
        out_shape=[
            S(tokens_in.shape, f32), S(tokens_in.shape, f32), vector, vector, square, square, square,
            part, part, S((head_share, width), f32), vector, vector, vector,
            S((experts, width), f32), S((1, share), f32), S((1, width), f32), S((5,), f32),
        ],
        scratch_shapes=[
            pltpu.VMEM(tokens_in.shape, f32),
            pltpu.VMEM(tokens_in.shape, f32),
            DMA((2, images)),
            DMA((2, images)),
        ],
        compiler_params=params(),
        name="finish",
    )(low, small, gbin_own, gbin_rest, gb_out, out_own, out_rest, gin_own, gin_tok)
    return (
        output, grad_input, gl1, bl1, gq, gk, gv, gbq, gbv, gwp, gbp, gl2, bl2, grout.T,
        grad_w_in, grad_b_in, grad_w_out, grad_b_out, rms,
    )


def solution(mesh):
    in_specs = (
        P("expert", None), P("expert", None), P("expert", None), P(), P(),
        P(None, "tensor"), P(None, "tensor"), P(None, "tensor"), P("tensor"), P("tensor"),
        P("tensor", None), P(), P(), P(), P(),
        P("expert", None, "tensor"), P("expert", "tensor"), P("expert", "tensor", None),
        P("expert", None), P("expert", None),
    )
    out_specs = (
        P("expert", None), P("expert", None), P(), P(),
        P(None, "tensor"), P(None, "tensor"), P(None, "tensor"), P("tensor"), P("tensor"),
        P("tensor", None), P(), P(), P(), P(),
        P("expert", None, "tensor"), P("expert", "tensor"), P("expert", "tensor", None),
        P("expert", None), P(),
    )
    return jax.shard_map(
        on_device, mesh=mesh, in_specs=in_specs, out_specs=out_specs, check_vma=False
    )
```

time: 492 us -> 456 us (0.927)
  local copies, waits for them, and re-layouts: 18.4 us -> 0 us
  waiting for transfers between devices: 17.1 us -> 0 us
  Pallas kernels: 438 us -> 448 us
  starting transfers between devices: 8.63 us -> 0 us
    all_to_all x1 -> x0, waiting for transfers between devices: 17.1 us -> none  [a2a(): lax.all_to_all(rows, 'expert', split_axis=0, concat_axis=0, tiled=True)]
    pallas_call x7 -> x4, Pallas kernels: 427 us -> 437 us  [the longest x1 222 us: on_device(): pl.pallas_call(moe_kernel, in_specs=[anywhere, anywhere, inside, anywhere...]
    all_to_all x1 -> x0, starting transfers between devices: 8.63 us -> none  [a2a(): lax.all_to_all(rows, 'expert', split_axis=0, concat_axis=0, tiled=True)]
    gather x2 -> x0, local copies, waits for them, and re-layouts: 6.71 us -> none  [the longest x1 4.3 us: on_device(): grow = a2a(send_g[turned])]
    reshape x9 -> x0, local copies, waits for them, and re-layouts: 5.14 us -> none  [the longest x7 4.03 us: row(): return v.reshape(1, -1)]
  transfers between devices with their start and end apart: 1 -> 0, of which waited for: 1 -> 0; matrix products, arithmetic and copies ran while one was open for 2% -> 0% of each run, Pallas kernels for 7% -> 0%
where the time goes in v3:
time: 456 us; the launch traced here: 449 us
  Pallas kernels  448 us (98%)
    pallas_call x1, Pallas kernels, on_device(): pl.pallas_call(moe_kernel, in_specs=[anywhere, anywhere, inside, anywhere...  222 us
    pallas_call x1, Pallas kernels, on_device(): pl.pallas_call(functools.partial(attn_bwd_b_kernel, dims), grid=(own,), i...  105 us
    pallas_call x1, Pallas kernels, on_device(): pl.pallas_call(functools.partial(attn_fwd_kernel, (images, seq, seq_pad,...  86.5 us
    pallas_call x1, Pallas kernels, on_device(): pl.pallas_call(functools.partial(attn_bwd_a_kernel, dims), grid=(own,), i...  24.1 us
    pallas_call x1, Pallas kernels, on_device(): pl.pallas_call(functools.partial(finish_kernel, seq), in_specs=[inside] *...  11 us

profile of v3, /device:TPU:0, one launch (start us, length us, event | category | flops | bytes accessed | tf_op | source)
XLA Modules:
  0.0 449.5 jit_solution(544236056151164391)
XLA Ops:
  0.7 86.5 %attn_fwd.1 = (bf16[4,208,768]{2,1,0:T(8,128)(2,1)}, bf16[4,208,768]{2,1,0:T(8,128)(2,1)}, bf16[4,256,768]{2,1,0:T(8,128)(2,1)}, bf16[4,256,768]{2,1,0:T(8,128)(...) custom-call(f32[1576,768]{1,0:T(8,128)} %tok_ref.1, ...), custom_call_target="tpu_custom_call" | custom-call | tf_op jit(solution)/shard_map/attn_fwd/pallas_call | solution.py:1288
  87.2 221.9 %moe.1 = (bf16[16,128,768]{2,1,0:T(8,128)(2,1)}, bf16[16,128,768]{2,1,0:T(8,128)(2,1)}, bf16[768,1536]{1,0:T(8,128)(2,1)}, bf16[1536,768]{1,0:T(8,128)(2,1)}, bf...) custom-call(bf16[832,896]{1,0:T(8,128)(2,1)} %bitcast.15, ...), custom_call_target="tpu_custom_call" | custom-call | tf_op jit(solution)/shard_map/moe/pallas_call | solution.py:1377
  309.1 24.1 %attn_bwd_a.1 = (f32[4,208,768]{2,1,0:T(8,128)}, f32[4,208,768]{2,1,0:T(8,128)}, bf16[4,208,768]{2,1,0:T(8,128)(2,1)}, bf16[4,208,768]{2,1,0:T(8,128)(2,1)}, f32...) custom-call(f32[1576,768]{1,0:T(8,128)} %cot_ref.3, ...), custom_call_target="tpu_custom_call" | custom-call | tf_op jit(solution)/shard_map/attn_bwd_a/pallas_call | solution.py:1435
  333.2 104.9 %attn_bwd_b.1 = (bf16[2,3,1536,128]{3,2,1,0:T(8,128)(2,1)}, f32[48,768]{1,0:T(8,128)}, f32[4,208,768]{2,1,0:T(8,128)}, f32[1,4,208,768]{3,2,1,0:T(8,128)}, f32[1,4,208,768]{3,2,1,0:T(8,128)}) custom-call(bf16[4,208,768]{2,1,0:T(8,128)(2,1)} %get-tuple-element.85.q_ref, bf16[4,256,768]{2,1,0:T(8,128)(2,1)} %get-tuple-element.86.k_ref, ...), custom_call_target="tpu_custom_call" | custom-call | tf_op jit(solution)/shard_map/attn_bwd_b/pallas_call | solution.py:1493
  438.0 11.0 %finish.1 = (f32[1576,768]{1,0:T(8,128)}, f32[1576,768]{1,0:T(8,128)}, f32[768]{0:T(1024)}, f32[768]{0:T(1024)}, f32[768,384]{1,0:T(8,128)}, /*index=5*/f32[768,...) custom-call(bf16[2,3,1536,128]{3,2,1,0:T(8,128)(2,1)} %get-tuple-ele, ...), custom_call_target="tpu_custom_call" | custom-call | tf_op jit(solution)/shard_map/finish/pallas_call | solution.py:1570

commit v4 on v3

--- a/solution.py
+++ b/solution.py
@@ -130,7 +130,7 @@
     for k, named_k, r_k in ((0, named0, r0), (1, named1, r1)):
         slot = jnp.sum(jnp.where(named_k, before, 0.0), 1, keepdims=True)
         fits = (slot >= 0) & (slot < cap_dev) & (r_k >= 0)
-        turn = lax.rem(r_k - expert + experts, experts)
+        turn = jnp.bitwise_xor(r_k, expert)
         half = experts // 2
         far = jnp.where(turn >= half, 1, 0)
         flat = ((turn - far * half) * 2 + far).astype(f32) * cap_dev + slot
@@ -186,7 +186,7 @@
         )
 
     def g_copy(k):
-        there = chip(offset_at(k, experts))
+        there = {"expert": chip_at(k, experts)}
         return remote(sent_ref.at[k], grow_ref.at[k], g_send.at[k], g_recv.at[k], there)
 
     own_rows = pltpu.make_async_copy(sent_ref.at[0], grow_ref.at[0], own_sem)
@@ -218,13 +218,13 @@
             k = lax.rem(n + 1, experts)
             total = None
             for j in range(cores):
-                named_e = post_ref[j, lax.rem(me_e + offset_at(k, experts), experts)]
+                named_e = post_ref[j, chip_at(k, experts)]
                 pick = jnp.where(named_e == slots, 1.0, 0.0).astype(bf16)
                 term = dot(pick, g16[group * j : group * (j + 1), :])
                 total = term if total is None else total + term
             sent_ref[k] = total.astype(bf16)
 
-            @pl.when(k > 0)
+            @pl.when((k > 0) & (k < early_places(experts)))
             def _():
                 g_copy(k).start()
 
@@ -305,7 +305,7 @@
             g_copy(k).wait()
             return 0
 
-        lax.fori_loop(1, experts, arrived, 0)
+        lax.fori_loop(1, early_places(experts), arrived, 0)
         own_rows.wait()
         for copy in keeps:
             copy.wait()
@@ -562,7 +562,7 @@
 
     pairs = width // LANES
     points = {}
-    hidden_points = min(7, 2 * bits + 1)
+    hidden_points = 4
     for n in range(hidden_points):
         turn = 4 + (n * (own * pairs - 5)) // max(hidden_points - 1, 1)
         points.setdefault((turn // pairs, turn % pairs), []).append(n)
@@ -713,8 +713,18 @@
     pl.semaphore_wait(pltpu.get_barrier_semaphore(), len(peers))
 
 
-def offset_at(place, experts):
-    return place // 2 + lax.rem(place, 2) * (experts // 2)
+def early_places(experts):
+    return experts
+
+
+def chip_at(place, experts):
+    me = lax.axis_index("expert")
+    flips = place // 2 + lax.rem(place, 2) * (experts // 2)
+    there = me
+    for b in range(experts.bit_length() - 1):
+        bit = 1 << b
+        there = there + lax.rem(flips // bit, 2) * bit * (1 - 2 * lax.rem(me // bit, 2))
+    return there
 
 
 def around(axis):
@@ -731,7 +741,7 @@
     table, out_s, rows_s, grow_s, res_s, gate_out, gate_in, gslot_ref,
     gbin_send, gbout_send,
     m_send, m_recv, load_sem, local_sem, h_send, h_recv, c_send, c_recv, r_send, r_recv, g_send, g_recv,
-    w_send, w_recv, own_sem
+    l_send, l_recv, w_send, w_recv, own_sem
 ):
     experts, chip = around("expert")
     cores, core = around("tensor")
@@ -751,7 +761,8 @@
             device_id=there, device_id_type=MESH,
         )
 
-    grow_copy = pltpu.make_async_copy(grow_hbm, grow_s, local_sem.at[0])
+    early = early_places(experts)
+    grow_copy = pltpu.make_async_copy(grow_hbm, grow_s.at[0:early], local_sem.at[0])
     grow_copy.start()
     fills = [
         pltpu.make_async_copy(
@@ -770,7 +781,7 @@
     lanes = lane_iota((cap_dev, LANES))
 
     def select(k):
-        e = lax.rem(me_e + offset_at(k, experts), experts)
+        e = chip_at(k, experts)
         total = None
         for j in range(cores):
             pick = jnp.where(post_ref[j, e] == slots, 1.0, 0.0).astype(bf16)
@@ -783,19 +794,19 @@
         return total[:, :width].astype(bf16), spread[0:8]
 
     def h_copy(k):
-        there = chip(offset_at(k, experts))
+        there = {"expert": chip_at(k, experts)}
         return remote(out_s.at[k], rows_s.at[k], h_send.at[k], h_recv.at[k], there)
 
     def c_copy(k):
-        there = chip(offset_at(k, experts))
+        there = {"expert": chip_at(k, experts)}
         return remote(gate_out.at[k], gate_in.at[k], c_send.at[k], c_recv.at[k], there)
 
     def r_copy(k):
-        there = chip(-offset_at(k, experts))
+        there = {"expert": chip_at(k, experts)}
         return remote(res_s.at[k], back_ref.at[k], r_send.at[k], r_recv.at[k], there)
 
     def g_copy(k):
-        there = chip(-offset_at(k, experts))
+        there = {"expert": chip_at(k, experts)}
         return remote(out_s.at[k], gback_ref.at[k], g_send.at[k], g_recv.at[k], there)
 
     def send_rows(j, _):
@@ -811,7 +822,16 @@
 
         return 0
 
+    def l_copy(k):
+        there = {"expert": chip_at(k, experts)}
+        return remote(sent_hbm.at[k], grow_s.at[k], l_send.at[k], l_recv.at[k], there)
+
+    def send_late(k, _):
+        l_copy(k).start()
+        return 0
+
     lax.fori_loop(0, experts, send_rows, 0)
+    lax.fori_loop(early, experts, send_late, 0)
     rows_s[0] = out_s[0]
     gate_in[0] = gate_out[0]
     pl.run_scoped(
@@ -825,7 +845,7 @@
                 gback_ref=gback_ref, gate_in=gate_in, gbout_send=gbout_send, gbout_ref=gbout_ref,
                 gbin_own=gbin_own, gbin_send=gbin_send, gbin_rest=gbin_rest, gin_own=gin_own,
                 gout_own=gout_own, gin_rest=gin_rest, gout_rest=gout_rest, w_send=w_send,
-                w_recv=w_recv, remote=remote,
+                w_recv=w_recv, remote=remote, l_copy=l_copy, early=early,
             ),
         ),
         pltpu.VMEM((experts * cap_dev, share * cores), bf16),
@@ -871,7 +891,7 @@
             dots = jnp.sum(rows * grow_s[k].astype(f32), 1, keepdims=True)
             here = pl.ds(pl.multiple_of(cap_dev * k, 16), cap_dev)
             values[here, 0:width] = (rows * gated(k)).astype(bf16)
-            mine = lanes == lax.rem(me_e + offset_at(k, experts), experts)
+            mine = lanes == chip_at(k, experts)
             values[here, width:] = jnp.where(mine, dots, 0.0).astype(bf16)
             return 0
 
@@ -1034,6 +1054,12 @@
 
     lax.fori_loop(1, experts, sent_rows, 0)
     grow_copy.wait()
+
+    def late_rows(k, _):
+        at.l_copy(k).wait()
+        return 0
+
+    lax.fori_loop(at.early, experts, late_rows, 0)
 
     def backward(i):
         g = grow_s[pl.ds(2 * i, 2)].reshape(2 * cap_dev, width)
@@ -1177,8 +1203,9 @@
 
 def finish_kernel(
     seq, low_ref, small_ref, gbin_own, gbin_rest, gbout_ref, out_own, out_rest, gin_own, gin_rest,
-    out_hbm, gin_hbm, gl1, bl1, gq, gk, gv, gbq, gbv, gwp, gbp, gl2, bl2, grout, gbin, gbout, rms,
-    out_s, gin_s, in_sem, to_sem
+    out_hbm, gin_hbm, gq_hbm, gk_hbm, gv_hbm, gwp_hbm, gl1, bl1, gbq, gbv, gbp, gl2, bl2, grout,
+    gbin, gbout, rms,
+    out_s, gin_s, parts_s, gq, gk, gv, gwp, in_sem, to_sem, g_sem
 ):
     cores, own, seq_pad, width = (out_rest.shape[0] + 1,) + out_rest.shape[1:]
     me_t = lax.axis_index("tensor")
@@ -1192,12 +1219,35 @@
         jobs.append((n, mine, rest, full, hbm))
     rows_all = images * seq
 
+    def incoming(n, p, i):
+        _, mine, rest, _, _ = jobs[n]
+        src = mine.at[i] if p == 0 else rest.at[p - 1, i]
+        return pltpu.make_async_copy(src, parts_s.at[n, p, i], in_sem.at[n, p, i])
+
+    for n in range(2):
+        for p in range(cores):
+            for i in range(own):
+                incoming(n, p, i).start()
+    lanes = low_ref.shape[3]
+    for c in range(low_ref.shape[1]):
+        cols = slice(lanes * c, lanes * (c + 1))
+        for grad, phase, n in ((gv, 0, 1), (gq, 1, 0), (gk, 1, 1)):
+            grad[:, cols] = low_ref[phase, c, width * n : width * (n + 1), :].astype(f32)
+        gwp[cols, :] = jnp.transpose(low_ref[0, c, 0:width, :].astype(f32), (1, 0))
+    grads = [
+        pltpu.make_async_copy(src, dst, g_sem.at[n])
+        for n, (src, dst) in enumerate(((gq, gq_hbm), (gk, gk_hbm), (gv, gv_hbm), (gwp, gwp_hbm)))
+    ]
+    for copy in grads:
+        copy.start()
+
     def place(c):
         for n, mine, rest, full, hbm in jobs:
             done = 0
             for im in range(images):
                 p = (im // own - c) % cores
-                src = mine.at[im % own] if p == 0 else rest.at[p - 1, im % own]
+                incoming(n, p, im % own).wait()
+                src = parts_s.at[n, p, im % own]
                 full[seq * im : seq * (im + 1), :] = src[0:seq, :]
                 upto = rows_all if im == images - 1 else seq * (im + 1) // 8 * 8
                 pltpu.make_async_copy(
@@ -1211,12 +1261,6 @@
         def _(c=c):
             place(c)
 
-    lanes = low_ref.shape[3]
-    for c in range(low_ref.shape[1]):
-        cols = slice(lanes * c, lanes * (c + 1))
-        for grad, phase, n in ((gv, 0, 1), (gq, 1, 0), (gk, 1, 1)):
-            grad[:, cols] = low_ref[phase, c, width * n : width * (n + 1), :].astype(f32)
-        gwp[cols, :] = jnp.transpose(low_ref[0, c, 0:width, :].astype(f32), (1, 0))
     base = small_base(cores)
     for dst, row in ((gl1, 5), (bl1, 6), (gbp, 4), (gl2, 2), (bl2, 3)):
         dst[...] = small_ref[row]
@@ -1239,6 +1283,8 @@
         square = jnp.sum(small_ref[row : row + 1, :], 1, keepdims=True)
         value = jnp.where(lanes == n, jnp.sqrt(square / count), value)
     rms[...] = value[0, 0:5]
+    for copy in grads:
+        copy.wait()
     done = [0] * 2
     for im in range(images):
         upto = rows_all if im == images - 1 else seq * (im + 1) // 8 * 8
@@ -1333,7 +1379,7 @@
             S((tok_pad, 2), i32),
             S((LANES, width), bf16),
             *[S((cores - 1,) + w.shape, bf16) for w in (w_query, w_key, w_value, w_proj)],
-            S(block, bf16),
+            S((early_places(experts), cap_dev, width), bf16),
             S((cores - 1, own, seq_pad, wide), bf16),
             S((cores - 1, width, share), bf16),
             S((cores - 1, share, width), bf16),
@@ -1408,7 +1454,7 @@
             DMA((2, cores - 1)),
             DMA((2,)),
             DMA((1 + cores,)),
-            *[DMA((experts,))] * 8,
+            *[DMA((experts,))] * 10,
             DMA((4, (cores - 1) * per)),
             DMA((4, (cores - 1) * per)),
             DMA((6,)),
@@ -1565,22 +1611,26 @@
     part = S((head_share,), f32)
     square = S((width, head_share), f32)
     (
-        output, grad_input, gl1, bl1, gq, gk, gv, gbq, gbv, gwp, gbp, gl2, bl2, grout,
+        output, grad_input, gq, gk, gv, gwp, gl1, bl1, gbq, gbv, gbp, gl2, bl2, grout,
         grad_b_in, grad_b_out, rms,
     ) = pl.pallas_call(
         functools.partial(finish_kernel, seq),
-        in_specs=[inside] * 9,
-        out_specs=[anywhere] * 2 + [inside] * 15,
+        in_specs=[inside] * 5 + [anywhere] * 4,
+        out_specs=[anywhere] * 6 + [inside] * 11,
         out_shape=[
-            S(tokens_in.shape, f32), S(tokens_in.shape, f32), vector, vector, square, square, square,
-            part, part, S((head_share, width), f32), vector, vector, vector,
+            S(tokens_in.shape, f32), S(tokens_in.shape, f32), square, square, square,
+            S((head_share, width), f32), vector, vector, part, part, vector, vector, vector,
             S((experts, width), f32), S((1, share), f32), S((1, width), f32), S((5,), f32),
         ],
         scratch_shapes=[
             pltpu.VMEM(tokens_in.shape, f32),
             pltpu.VMEM(tokens_in.shape, f32),
+            pltpu.VMEM((2, cores, own, seq_pad, width), f32),
+            *[pltpu.VMEM((width, head_share), f32)] * 3,
+            pltpu.VMEM((head_share, width), f32),
+            DMA((2, cores, own)),
             DMA((2, images)),
-            DMA((2, images)),
+            DMA((4,)),
         ],
         compiler_params=params(),
         name="finish",

time: 456 us -> 443 us (0.971)
  Pallas kernels: 448 us -> 436 us
    pallas_call x1, Pallas kernels: 86.5 us -> 72.2 us  [on_device(): pl.pallas_call(functools.partial(attn_fwd_kernel, (images, seq, seq_pad,...]
    pallas_call x1, Pallas kernels: 222 us -> 235 us  [on_device(): pl.pallas_call(moe_kernel, in_specs=[anywhere, anywhere, inside, anywhere...]
    pallas_call x1, Pallas kernels: 105 us -> 92.4 us  [on_device(): pl.pallas_call(functools.partial(attn_bwd_b_kernel, dims), grid=(own,), i...]
where the time goes in v4:
time: 443 us; the launch traced here: 437 us
  Pallas kernels  436 us (98%)
    pallas_call x1, Pallas kernels, on_device(): pl.pallas_call(moe_kernel, in_specs=[anywhere, anywhere, inside, anywhere...  235 us
    pallas_call x1, Pallas kernels, on_device(): pl.pallas_call(functools.partial(attn_bwd_b_kernel, dims), grid=(own,), i...  92.4 us
    pallas_call x1, Pallas kernels, on_device(): pl.pallas_call(functools.partial(attn_fwd_kernel, (images, seq, seq_pad,...  72.2 us
    pallas_call x1, Pallas kernels, on_device(): pl.pallas_call(functools.partial(attn_bwd_a_kernel, dims), grid=(own,), i...  24.1 us
    pallas_call x1, Pallas kernels, on_device(): pl.pallas_call(functools.partial(finish_kernel, seq), in_specs=[inside] *...  11.7 us

profile of v4, /device:TPU:0, one launch (start us, length us, event | category | flops | bytes accessed | tf_op | source)
XLA Modules:
  0.0 437.0 jit_solution(17580366926780415823)
XLA Ops:
  0.7 72.2 %attn_fwd.1 = (bf16[4,208,768]{2,1,0:T(8,128)(2,1)}, bf16[4,208,768]{2,1,0:T(8,128)(2,1)}, bf16[4,256,768]{2,1,0:T(8,128)(2,1)}, bf16[4,256,768]{2,1,0:T(8,128)(...) custom-call(f32[1576,768]{1,0:T(8,128)} %tok_ref.1, ...), custom_call_target="tpu_custom_call" | custom-call | tf_op jit(solution)/shard_map/attn_fwd/pallas_call | solution.py:1334
  72.9 235.4 %moe.1 = (bf16[16,128,768]{2,1,0:T(8,128)(2,1)}, bf16[16,128,768]{2,1,0:T(8,128)(2,1)}, bf16[768,1536]{1,0:T(8,128)(2,1)}, bf16[1536,768]{1,0:T(8,128)(2,1)}, bf...) custom-call(bf16[832,896]{1,0:T(8,128)(2,1)} %bitcast.15, ...), custom_call_target="tpu_custom_call" | custom-call | tf_op jit(solution)/shard_map/moe/pallas_call | solution.py:1423
  308.3 24.1 %attn_bwd_a.1 = (f32[4,208,768]{2,1,0:T(8,128)}, f32[4,208,768]{2,1,0:T(8,128)}, bf16[4,208,768]{2,1,0:T(8,128)(2,1)}, bf16[4,208,768]{2,1,0:T(8,128)(2,1)}, f32...) custom-call(f32[1576,768]{1,0:T(8,128)} %cot_ref.3, ...), custom_call_target="tpu_custom_call" | custom-call | tf_op jit(solution)/shard_map/attn_bwd_a/pallas_call | solution.py:1481
  332.4 92.4 %attn_bwd_b.1 = (bf16[2,3,1536,128]{3,2,1,0:T(8,128)(2,1)}, f32[48,768]{1,0:T(8,128)}, f32[4,208,768]{2,1,0:T(8,128)}, f32[1,4,208,768]{3,2,1,0:T(8,128)}, f32[1,4,208,768]{3,2,1,0:T(8,128)}) custom-call(bf16[4,208,768]{2,1,0:T(8,128)(2,1)} %get-tuple-element.85.q_ref, bf16[4,256,768]{2,1,0:T(8,128)(2,1)} %get-tuple-element.86.k_ref, ...), custom_call_target="tpu_custom_call" | custom-call | tf_op jit(solution)/shard_map/attn_bwd_b/pallas_call | solution.py:1539
  424.8 11.7 %finish.1 = (f32[1576,768]{1,0:T(8,128)}, f32[1576,768]{1,0:T(8,128)}, f32[768,384]{1,0:T(8,128)}, f32[768,384]{1,0:T(8,128)}, f32[768,384]{1,0:T(8,128)}, /*ind...) custom-call(bf16[2,3,1536,128]{3,2,1,0:T(8,128)(2,1)} %get-tuple-ele, ...), custom_call_target="tpu_custom_call" | custom-call | tf_op jit(solution)/shard_map/finish/pallas_call | solution.py:1616

commit v5 on v4

--- a/solution.py
+++ b/solution.py
@@ -562,7 +562,7 @@
 
     pairs = width // LANES
     points = {}
-    hidden_points = 4
+    hidden_points = 2
     for n in range(hidden_points):
         turn = 4 + (n * (own * pairs - 5)) // max(hidden_points - 1, 1)
         points.setdefault((turn // pairs, turn % pairs), []).append(n)

time: 443 us -> 440 us (level)
  no operation moved by 1% of the time
where the time goes in v5:
time: 440 us; the launch traced here: 434 us
  Pallas kernels  433 us (98%)
    pallas_call x1, Pallas kernels, on_device(): pl.pallas_call(moe_kernel, in_specs=[anywhere, anywhere, inside, anywhere...  235 us
    pallas_call x1, Pallas kernels, on_device(): pl.pallas_call(functools.partial(attn_bwd_b_kernel, dims), grid=(own,), i...  89.4 us
    pallas_call x1, Pallas kernels, on_device(): pl.pallas_call(functools.partial(attn_fwd_kernel, (images, seq, seq_pad,...  72.2 us
    pallas_call x1, Pallas kernels, on_device(): pl.pallas_call(functools.partial(attn_bwd_a_kernel, dims), grid=(own,), i...  24.1 us
    pallas_call x1, Pallas kernels, on_device(): pl.pallas_call(functools.partial(finish_kernel, seq), in_specs=[inside] *...  11.7 us

profile of v5, /device:TPU:0, one launch (start us, length us, event | category | flops | bytes accessed | tf_op | source)
XLA Modules:
  0.0 433.9 jit_solution(6465524547325571508)
XLA Ops:
  0.7 72.2 %attn_fwd.1 = (bf16[4,208,768]{2,1,0:T(8,128)(2,1)}, bf16[4,208,768]{2,1,0:T(8,128)(2,1)}, bf16[4,256,768]{2,1,0:T(8,128)(2,1)}, bf16[4,256,768]{2,1,0:T(8,128)(...) custom-call(f32[1576,768]{1,0:T(8,128)} %tok_ref.1, ...), custom_call_target="tpu_custom_call" | custom-call | tf_op jit(solution)/shard_map/attn_fwd/pallas_call | solution.py:1334
  72.9 235.4 %moe.1 = (bf16[16,128,768]{2,1,0:T(8,128)(2,1)}, bf16[16,128,768]{2,1,0:T(8,128)(2,1)}, bf16[768,1536]{1,0:T(8,128)(2,1)}, bf16[1536,768]{1,0:T(8,128)(2,1)}, bf...) custom-call(bf16[832,896]{1,0:T(8,128)(2,1)} %bitcast.15, ...), custom_call_target="tpu_custom_call" | custom-call | tf_op jit(solution)/shard_map/moe/pallas_call | solution.py:1423
  308.3 24.1 %attn_bwd_a.1 = (f32[4,208,768]{2,1,0:T(8,128)}, f32[4,208,768]{2,1,0:T(8,128)}, bf16[4,208,768]{2,1,0:T(8,128)(2,1)}, bf16[4,208,768]{2,1,0:T(8,128)(2,1)}, f32...) custom-call(f32[1576,768]{1,0:T(8,128)} %cot_ref.3, ...), custom_call_target="tpu_custom_call" | custom-call | tf_op jit(solution)/shard_map/attn_bwd_a/pallas_call | solution.py:1481
  332.4 89.4 %attn_bwd_b.1 = (bf16[2,3,1536,128]{3,2,1,0:T(8,128)(2,1)}, f32[48,768]{1,0:T(8,128)}, f32[4,208,768]{2,1,0:T(8,128)}, f32[1,4,208,768]{3,2,1,0:T(8,128)}, f32[1,4,208,768]{3,2,1,0:T(8,128)}) custom-call(bf16[4,208,768]{2,1,0:T(8,128)(2,1)} %get-tuple-element.85.q_ref, bf16[4,256,768]{2,1,0:T(8,128)(2,1)} %get-tuple-element.86.k_ref, ...), custom_call_target="tpu_custom_call" | custom-call | tf_op jit(solution)/shard_map/attn_bwd_b/pallas_call | solution.py:1539
  421.8 11.7 %finish.1 = (f32[1576,768]{1,0:T(8,128)}, f32[1576,768]{1,0:T(8,128)}, f32[768,384]{1,0:T(8,128)}, f32[768,384]{1,0:T(8,128)}, f32[768,384]{1,0:T(8,128)}, /*ind...) custom-call(bf16[2,3,1536,128]{3,2,1,0:T(8,128)(2,1)} %get-tuple-ele, ...), custom_call_target="tpu_custom_call" | custom-call | tf_op jit(solution)/shard_map/finish/pallas_call | solution.py:1616
